TPU v7x, 32 devices: a whole 2x2x4 slice. The times are simulated.
32 devices in a mesh: rep: 4 (over x, core), fsdp: 8 (over z, y).
Axes of the slice: x: 2, y: 2, z: 4, core: 2. Of those that a mesh axis runs over, the one named last changes fastest.
Arguments:
- tokens: bfloat16 [32, 592, 768], P(('rep', 'fsdp')), may hold values from -6 to 6
- slot_kinds: int32 [32], P(('rep', 'fsdp')), may hold values from 0 to 1
- small_index: int32 [197, 197], replicated, may hold values from 0 to 2239, as said below
- large_index: int32 [577, 577], replicated, may hold values from 0 to 2239, as said below
- first_gain: bfloat16 [1, 768], P(None, 'fsdp'), may hold values from 0.5 to 1.5
- first_shift: bfloat16 [1, 768], P(None, 'fsdp'), may hold values from -2 to 2
- triple_weight: bfloat16 [1, 768, 2304], P(None, 'fsdp'), may hold values from -0.21875 to 0.21875
- query_bias: bfloat16 [1, 768], P(None, 'fsdp'), may hold values from -2 to 2
- value_bias: bfloat16 [1, 768], P(None, 'fsdp'), may hold values from -2 to 2
- bias_table: bfloat16 [1, 2240, 12], P(None, 'fsdp'), may hold values from -4 to 4
- output_weight: bfloat16 [1, 768, 768], P(None, 'fsdp'), may hold values from -2 to 2
- output_bias: bfloat16 [1, 768], P(None, 'fsdp'), may hold values from -2 to 2
- attend_scale: bfloat16 [1, 768], P(None, 'fsdp'), may hold values from 0.5 to 1.5
- second_gain: bfloat16 [1, 768], P(None, 'fsdp'), may hold values from 0.5 to 1.5
- second_shift: bfloat16 [1, 768], P(None, 'fsdp'), may hold values from -2 to 2
- expand_weight: bfloat16 [1, 768, 3072], P(None, 'fsdp'), may hold values from -0.21875 to 0.21875
- expand_bias: bfloat16 [1, 3072], P(None, 'fsdp'), may hold values from -2 to 2
- reduce_weight: bfloat16 [1, 3072, 768], P(None, 'fsdp'), may hold values from -0.15625 to 0.15625
- reduce_bias: bfloat16 [1, 768], P(None, 'fsdp'), may hold values from -2 to 2
- feed_scale: bfloat16 [1, 768], P(None, 'fsdp'), may hold values from 0.5 to 1.5
- cotangent: bfloat16 [32, 592, 768], P(('rep', 'fsdp')), may hold values from -6 to 6
Outputs:
- block_output: bfloat16 [32, 592, 768], P(('rep', 'fsdp'))
- token_grad: bfloat16 [32, 592, 768], P(('rep', 'fsdp'))
- first_gain_grad: float32 [1, 768], P(None, 'fsdp')
- first_shift_grad: float32 [1, 768], P(None, 'fsdp')
- triple_weight_grad: float32 [1, 768, 2304], P(None, 'fsdp')
- query_bias_grad: float32 [1, 768], P(None, 'fsdp')
- value_bias_grad: float32 [1, 768], P(None, 'fsdp')
- bias_table_grad: float32 [1, 2240, 12], P(None, 'fsdp')
- output_weight_grad: float32 [1, 768, 768], P(None, 'fsdp')
- output_bias_grad: float32 [1, 768], P(None, 'fsdp')
- attend_scale_grad: float32 [1, 768], P(None, 'fsdp')
- second_gain_grad: float32 [1, 768], P(None, 'fsdp')
- second_shift_grad: float32 [1, 768], P(None, 'fsdp')
- expand_weight_grad: float32 [1, 768, 3072], P(None, 'fsdp')
- expand_bias_grad: float32 [1, 3072], P(None, 'fsdp')
- reduce_weight_grad: float32 [1, 3072, 768], P(None, 'fsdp')
- reduce_bias_grad: float32 [1, 768], P(None, 'fsdp')
- feed_scale_grad: float32 [1, 768], P(None, 'fsdp')
Inputs may be any that keep to these rules, and one draw needn't show every extreme that they name: small_index[r, s] is the bias table row of tokens r and s of a 14 x 14 image, token 0 the class token and token 1 + 14 i + j the patch in row i, column j; large_index likewise for a 24 x 24 image. In both tables two patch pairs share a row exactly when their offsets on the patch grid agree, and the class-to-patch, patch-to-class and class-to-class pairs have three rows of their own; equal offsets and equal pair kinds take the same row in both tables. `large_index`: as for small_index.
All inputs are finite; a program needn't handle non-finite values.
Results may differ from a plain program's by a relative error of at most 0.012.
Values may be sent and summed in bfloat16 or wider, within the bound.
A program may use at most 576 MiB of HBM per device.

v0:
```python
import jax
import jax.numpy as jnp
from jax import lax
from jax.sharding import PartitionSpec as P

norm_eps = 1e-06
neg_fill = -1000000000.0


def layer_norm(values_in, gain_vec, shift_vec):
    row_mean = jnp.mean(values_in, axis=-1, keepdims=True)
    centred = values_in - row_mean
    row_var = jnp.mean(centred * centred, axis=-1, keepdims=True)
    return centred * lax.rsqrt(row_var + norm_eps) * gain_vec + shift_vec


def gelu_exact(values_in):
    return jax.nn.gelu(values_in, approximate=False)


def segment_ids(slot_kinds, slot_rows, small_len, large_len):
    row_ids = jnp.arange(slot_rows, dtype=jnp.int32)
    small_seg = jnp.where(row_ids < 3 * small_len, row_ids // small_len, 3)
    large_seg = jnp.where(row_ids < large_len, 0, 3)
    return jnp.where(slot_kinds[:, None] == 1, large_seg[None, :], small_seg[None, :])


def pair_bias(table_vals, small_index, large_index, slot_kinds, slot_rows):
    head_count = table_vals.shape[1]
    small_len = small_index.shape[0]
    large_len = large_index.shape[0]
    large_part = jnp.transpose(jnp.take(table_vals, large_index, axis=0), (2, 0, 1))
    small_part = jnp.transpose(jnp.take(table_vals, small_index, axis=0), (2, 0, 1))
    full_large = (
        jnp.zeros((head_count, slot_rows, slot_rows), jnp.float32)
        .at[:, :large_len, :large_len]
        .set(large_part)
    )
    full_small = jnp.zeros((head_count, slot_rows, slot_rows), jnp.float32)
    for block_idx in range(3):
        first_row = block_idx * small_len
        full_small = full_small.at[
            :, first_row : first_row + small_len, first_row : first_row + small_len
        ].set(small_part)
    return jnp.where(slot_kinds[:, None, None, None] == 1, full_large[None], full_small[None])


def table_gradient(score_grads, small_index, large_index, slot_kinds, bucket_count):
    head_count = score_grads.shape[1]
    small_len = small_index.shape[0]
    large_len = large_index.shape[0]
    large_flag = (slot_kinds == 1).astype(jnp.float32)[:, None, None, None]
    large_part = jnp.sum(score_grads[:, :, :large_len, :large_len] * large_flag, axis=0)
    small_part = jnp.zeros((head_count, small_len, small_len), jnp.float32)
    for block_idx in range(3):
        first_row = block_idx * small_len
        piece_grads = score_grads[
            :, :, first_row : first_row + small_len, first_row : first_row + small_len
        ]
        small_part = small_part + jnp.sum(piece_grads * (1.0 - large_flag), axis=0)
    table_acc = jnp.zeros((bucket_count, head_count), jnp.float32)
    table_acc = table_acc.at[large_index].add(jnp.transpose(large_part, (1, 2, 0)))
    table_acc = table_acc.at[small_index].add(jnp.transpose(small_part, (1, 2, 0)))
    return table_acc


def attention_scores(query_rows, key_rows, bias_full, allowed):
    score_scale = query_rows.shape[3] ** (-0.5)
    raw_scores = (
        jnp.einsum("bqhd,bkhd->bhqk", query_rows, key_rows, preferred_element_type=jnp.float32)
        * score_scale
        + bias_full
    )
    return jnp.where(allowed, raw_scores, neg_fill)


def forward_layer(weights, hidden_in, bias_full, allowed, head_count):
    (
        first_gain,
        first_shift,
        triple_weight,
        query_bias,
        value_bias,
        bias_table,
        output_weight,
        output_bias,
        attend_scale,
        second_gain,
        second_shift,
        expand_weight,
        expand_bias,
        reduce_weight,
        reduce_bias,
        feed_scale,
    ) = weights
    slot_count, slot_rows, model_width = hidden_in.shape
    head_dim = model_width // head_count
    heads_shape = (slot_count, slot_rows, head_count, head_dim)
    flat_in = hidden_in.reshape(slot_count * slot_rows, model_width)
    normed = layer_norm(
        flat_in, first_gain.astype(jnp.float32), first_shift.astype(jnp.float32)
    ).astype(jnp.bfloat16)
    triple = jnp.dot(normed, triple_weight, preferred_element_type=jnp.float32)
    query_rows = (
        (triple[:, :model_width] + query_bias.astype(jnp.float32))
        .astype(jnp.bfloat16)
        .reshape(heads_shape)
    )
    key_rows = triple[:, model_width : 2 * model_width].astype(jnp.bfloat16).reshape(heads_shape)
    value_rows = (
        (triple[:, 2 * model_width :] + value_bias.astype(jnp.float32))
        .astype(jnp.bfloat16)
        .reshape(heads_shape)
    )
    scores = attention_scores(query_rows, key_rows, bias_full, allowed)
    row_max = jnp.max(scores, axis=-1, keepdims=True)
    exp_scores = jnp.exp(scores - row_max)
    exp_total = jnp.sum(exp_scores, axis=-1, keepdims=True)
    soft_probs = (exp_scores / exp_total).astype(jnp.bfloat16)
    log_total = row_max + jnp.log(exp_total)
    mixed_heads = jnp.einsum(
        "bhqk,bkhd->bqhd", soft_probs, value_rows, preferred_element_type=jnp.float32
    )
    mixed_heads = mixed_heads.reshape(slot_count * slot_rows, model_width).astype(jnp.bfloat16)
    branch = jnp.dot(
        mixed_heads, output_weight, preferred_element_type=jnp.float32
    ) + output_bias.astype(jnp.float32)
    middle = flat_in + attend_scale.astype(jnp.float32) * branch
    second = layer_norm(
        middle, second_gain.astype(jnp.float32), second_shift.astype(jnp.float32)
    ).astype(jnp.bfloat16)
    pre_act = jnp.dot(
        second, expand_weight, preferred_element_type=jnp.float32
    ) + expand_bias.astype(jnp.float32)
    activated = gelu_exact(pre_act).astype(jnp.bfloat16)
    feed_out = jnp.dot(
        activated, reduce_weight, preferred_element_type=jnp.float32
    ) + reduce_bias.astype(jnp.float32)
    hidden_out = middle + feed_scale.astype(jnp.float32) * feed_out
    saved_acts = (
        flat_in,
        normed,
        query_rows,
        key_rows,
        value_rows,
        log_total,
        mixed_heads,
        branch,
        middle,
        second,
        pre_act,
        activated,
        feed_out,
    )
    return (hidden_out.reshape(slot_count, slot_rows, model_width), saved_acts)


def backward_layer(
    weights, saved_acts, grad_out, bias_full, allowed, slot_kinds, small_index, large_index
):
    (
        first_gain,
        first_shift,
        triple_weight,
        query_bias,
        value_bias,
        bias_table,
        output_weight,
        output_bias,
        attend_scale,
        second_gain,
        second_shift,
        expand_weight,
        expand_bias,
        reduce_weight,
        reduce_bias,
        feed_scale,
    ) = weights
    (
        flat_in,
        normed,
        query_rows,
        key_rows,
        value_rows,
        log_total,
        mixed_heads,
        branch,
        middle,
        second,
        pre_act,
        activated,
        feed_out,
    ) = saved_acts
    slot_count, slot_rows, head_count, head_dim = query_rows.shape
    model_width = head_count * head_dim
    flat_rows = slot_count * slot_rows
    score_scale = head_dim ** (-0.5)
    d_feed = (feed_scale.astype(jnp.float32) * grad_out).astype(jnp.bfloat16)
    feed_scale_grad = jnp.sum(grad_out * feed_out, axis=0)
    reduce_weight_grad = jnp.einsum(
        "rf,rd->fd", activated, d_feed, preferred_element_type=jnp.float32
    )
    reduce_bias_grad = jnp.sum(d_feed.astype(jnp.float32), axis=0)
    d_act = jnp.einsum("rd,fd->rf", d_feed, reduce_weight, preferred_element_type=jnp.float32)
    gelu_value, gelu_pull = jax.vjp(gelu_exact, pre_act)
    d_pre = gelu_pull(d_act)[0].astype(jnp.bfloat16)
    expand_weight_grad = jnp.einsum("rd,rf->df", second, d_pre, preferred_element_type=jnp.float32)
    expand_bias_grad = jnp.sum(d_pre.astype(jnp.float32), axis=0)
    d_second = jnp.einsum("rf,df->rd", d_pre, expand_weight, preferred_element_type=jnp.float32)
    norm_value, norm_pull = jax.vjp(
        layer_norm, middle, second_gain.astype(jnp.float32), second_shift.astype(jnp.float32)
    )
    middle_part, second_gain_grad, second_shift_grad = norm_pull(d_second)
    d_middle = grad_out + middle_part
    d_branch = (attend_scale.astype(jnp.float32) * d_middle).astype(jnp.bfloat16)
    attend_scale_grad = jnp.sum(d_middle * branch, axis=0)
    output_weight_grad = jnp.einsum(
        "rd,re->de", mixed_heads, d_branch, preferred_element_type=jnp.float32
    )
    output_bias_grad = jnp.sum(d_branch.astype(jnp.float32), axis=0)
    d_mixed = jnp.einsum("re,de->rd", d_branch, output_weight, preferred_element_type=jnp.float32)
    d_mixed = d_mixed.astype(jnp.bfloat16).reshape(slot_count, slot_rows, head_count, head_dim)
    scores = attention_scores(query_rows, key_rows, bias_full, allowed)
    probs_full = jnp.exp(scores - log_total)
    soft_probs = probs_full.astype(jnp.bfloat16)
    d_value = jnp.einsum(
        "bhqk,bqhd->bkhd", soft_probs, d_mixed, preferred_element_type=jnp.float32
    ).astype(jnp.bfloat16)
    d_probs = jnp.einsum("bqhd,bkhd->bhqk", d_mixed, value_rows, preferred_element_type=jnp.float32)
    row_delta = jnp.sum(probs_full * d_probs, axis=-1, keepdims=True)
    d_scores = (probs_full * (d_probs - row_delta)).astype(jnp.bfloat16)
    bias_table_grad = table_gradient(
        d_scores.astype(jnp.float32), small_index, large_index, slot_kinds, bias_table.shape[0]
    )
    d_query = (
        jnp.einsum("bhqk,bkhd->bqhd", d_scores, key_rows, preferred_element_type=jnp.float32)
        * score_scale
    ).astype(jnp.bfloat16)
    d_key = (
        jnp.einsum("bhqk,bqhd->bkhd", d_scores, query_rows, preferred_element_type=jnp.float32)
        * score_scale
    ).astype(jnp.bfloat16)
    d_triple = jnp.concatenate(
        [
            d_query.reshape(flat_rows, model_width),
            d_key.reshape(flat_rows, model_width),
            d_value.reshape(flat_rows, model_width),
        ],
        axis=1,
    )
    query_bias_grad = jnp.sum(d_query.reshape(flat_rows, model_width).astype(jnp.float32), axis=0)
    value_bias_grad = jnp.sum(d_value.reshape(flat_rows, model_width).astype(jnp.float32), axis=0)
    triple_weight_grad = jnp.einsum(
        "rd,re->de", normed, d_triple, preferred_element_type=jnp.float32
    )
    d_normed = jnp.einsum("re,de->rd", d_triple, triple_weight, preferred_element_type=jnp.float32)
    first_value, first_pull = jax.vjp(
        layer_norm, flat_in, first_gain.astype(jnp.float32), first_shift.astype(jnp.float32)
    )
    input_part, first_gain_grad, first_shift_grad = first_pull(d_normed)
    grad_in = d_middle + input_part
    layer_grads = (
        first_gain_grad,
        first_shift_grad,
        triple_weight_grad,
        query_bias_grad,
        value_bias_grad,
        bias_table_grad,
        output_weight_grad,
        output_bias_grad,
        attend_scale_grad,
        second_gain_grad,
        second_shift_grad,
        expand_weight_grad,
        expand_bias_grad,
        reduce_weight_grad,
        reduce_bias_grad,
        feed_scale_grad,
    )
    return (grad_in, layer_grads)


def sum_gradients(layer_grads):
    shard_grads = (
        lax.psum_scatter(layer_grads[0], "fsdp", scatter_dimension=0, tiled=True),
        lax.psum_scatter(layer_grads[1], "fsdp", scatter_dimension=0, tiled=True),
        lax.psum_scatter(layer_grads[2], "fsdp", scatter_dimension=0, tiled=True),
        lax.psum_scatter(layer_grads[3], "fsdp", scatter_dimension=0, tiled=True),
        lax.psum_scatter(layer_grads[4], "fsdp", scatter_dimension=0, tiled=True),
        lax.psum_scatter(layer_grads[5], "fsdp", scatter_dimension=0, tiled=True),
        lax.psum_scatter(layer_grads[6], "fsdp", scatter_dimension=0, tiled=True),
        lax.psum_scatter(layer_grads[7], "fsdp", scatter_dimension=0, tiled=True),
        lax.psum_scatter(layer_grads[8], "fsdp", scatter_dimension=0, tiled=True),
        lax.psum_scatter(layer_grads[9], "fsdp", scatter_dimension=0, tiled=True),
        lax.psum_scatter(layer_grads[10], "fsdp", scatter_dimension=0, tiled=True),
        lax.psum_scatter(layer_grads[11], "fsdp", scatter_dimension=0, tiled=True),
        lax.psum_scatter(layer_grads[12], "fsdp", scatter_dimension=0, tiled=True),
        lax.psum_scatter(layer_grads[13], "fsdp", scatter_dimension=0, tiled=True),
        lax.psum_scatter(layer_grads[14], "fsdp", scatter_dimension=0, tiled=True),
        lax.psum_scatter(layer_grads[15], "fsdp", scatter_dimension=0, tiled=True),
    )
    return lax.psum(
        (
            shard_grads[0],
            shard_grads[1],
            shard_grads[2],
            shard_grads[3],
            shard_grads[4],
            shard_grads[5],
            shard_grads[6],
            shard_grads[7],
            shard_grads[8],
            shard_grads[9],
            shard_grads[10],
            shard_grads[11],
            shard_grads[12],
            shard_grads[13],
            shard_grads[14],
            shard_grads[15],
        ),
        "rep",
    )


def per_device(
    tokens,
    slot_kinds,
    small_index,
    large_index,
    first_gain,
    first_shift,
    triple_weight,
    query_bias,
    value_bias,
    bias_table,
    output_weight,
    output_bias,
    attend_scale,
    second_gain,
    second_shift,
    expand_weight,
    expand_bias,
    reduce_weight,
    reduce_bias,
    feed_scale,
    cotangent,
):
    shards = (
        first_gain,
        first_shift,
        triple_weight,
        query_bias,
        value_bias,
        bias_table,
        output_weight,
        output_bias,
        attend_scale,
        second_gain,
        second_shift,
        expand_weight,
        expand_bias,
        reduce_weight,
        reduce_bias,
        feed_scale,
    )
    head_count = bias_table.shape[2]
    layer_count = first_gain.shape[0]
    slot_count, slot_rows, model_width = tokens.shape
    segment = segment_ids(slot_kinds, slot_rows, small_index.shape[0], large_index.shape[0])
    allowed = (segment[:, :, None] == segment[:, None, :])[:, None]
    live_rows = (segment < 3).astype(jnp.float32).reshape(slot_count * slot_rows, 1)
    hidden_now = tokens.astype(jnp.float32)
    kept_weights = []
    layer_idx = 0
    picked = [shard_arr[layer_idx] for shard_arr in shards]
    weights = (
        lax.all_gather(picked[0], "fsdp", axis=0, tiled=True),
        lax.all_gather(picked[1], "fsdp", axis=0, tiled=True),
        lax.all_gather(picked[2], "fsdp", axis=0, tiled=True),
        lax.all_gather(picked[3], "fsdp", axis=0, tiled=True),
        lax.all_gather(picked[4], "fsdp", axis=0, tiled=True),
        lax.all_gather(picked[5], "fsdp", axis=0, tiled=True),
        lax.all_gather(picked[6], "fsdp", axis=0, tiled=True),
        lax.all_gather(picked[7], "fsdp", axis=0, tiled=True),
        lax.all_gather(picked[8], "fsdp", axis=0, tiled=True),
        lax.all_gather(picked[9], "fsdp", axis=0, tiled=True),
        lax.all_gather(picked[10], "fsdp", axis=0, tiled=True),
        lax.all_gather(picked[11], "fsdp", axis=0, tiled=True),
        lax.all_gather(picked[12], "fsdp", axis=0, tiled=True),
        lax.all_gather(picked[13], "fsdp", axis=0, tiled=True),
        lax.all_gather(picked[14], "fsdp", axis=0, tiled=True),
        lax.all_gather(picked[15], "fsdp", axis=0, tiled=True),
    )
    bias_full = pair_bias(
        weights[5].astype(jnp.float32), small_index, large_index, slot_kinds, slot_rows
    )
    hidden_now, saved_acts = forward_layer(weights, hidden_now, bias_full, allowed, head_count)
    kept_weights.append(weights)
    saved_layers = [saved_acts]
    block_output = hidden_now.astype(jnp.bfloat16)
    grad_now = (
        cotangent.astype(jnp.float32).reshape(slot_count * slot_rows, model_width) * live_rows
    )
    summed_layers = [None] * layer_count
    for layer_idx in reversed(range(layer_count)):
        picked = [shard_arr[layer_idx] for shard_arr in shards]
        weights = (
            lax.all_gather(picked[0], "fsdp", axis=0, tiled=True),
            lax.all_gather(picked[1], "fsdp", axis=0, tiled=True),
            lax.all_gather(picked[2], "fsdp", axis=0, tiled=True),
            lax.all_gather(picked[3], "fsdp", axis=0, tiled=True),
            lax.all_gather(picked[4], "fsdp", axis=0, tiled=True),
            lax.all_gather(picked[5], "fsdp", axis=0, tiled=True),
            lax.all_gather(picked[6], "fsdp", axis=0, tiled=True),
            lax.all_gather(picked[7], "fsdp", axis=0, tiled=True),
            lax.all_gather(picked[8], "fsdp", axis=0, tiled=True),
            lax.all_gather(picked[9], "fsdp", axis=0, tiled=True),
            lax.all_gather(picked[10], "fsdp", axis=0, tiled=True),
            lax.all_gather(picked[11], "fsdp", axis=0, tiled=True),
            lax.all_gather(picked[12], "fsdp", axis=0, tiled=True),
            lax.all_gather(picked[13], "fsdp", axis=0, tiled=True),
            lax.all_gather(picked[14], "fsdp", axis=0, tiled=True),
            lax.all_gather(picked[15], "fsdp", axis=0, tiled=True),
        )
        bias_full = pair_bias(
            weights[5].astype(jnp.float32), small_index, large_index, slot_kinds, slot_rows
        )
        grad_now, layer_grads = backward_layer(
            weights,
            saved_layers[layer_idx],
            grad_now,
            bias_full,
            allowed,
            slot_kinds,
            small_index,
            large_index,
        )
        summed_layers[layer_idx] = sum_gradients(layer_grads)
    token_grad = grad_now.reshape(slot_count, slot_rows, model_width).astype(jnp.bfloat16)
    stacked = tuple((jnp.stack([summed_layers[0][param_idx]]) for param_idx in range(16)))
    return (block_output, token_grad) + stacked


def solution(mesh):
    placed = (
        P(("rep", "fsdp"), None, None),
        P(("rep", "fsdp")),
        P(),
        P(),
        P(None, "fsdp"),
        P(None, "fsdp"),
        P(None, "fsdp", None),
        P(None, "fsdp"),
        P(None, "fsdp"),
        P(None, "fsdp", None),
        P(None, "fsdp", None),
        P(None, "fsdp"),
        P(None, "fsdp"),
        P(None, "fsdp"),
        P(None, "fsdp"),
        P(None, "fsdp", None),
        P(None, "fsdp"),
        P(None, "fsdp", None),
        P(None, "fsdp"),
        P(None, "fsdp"),
        P(("rep", "fsdp"), None, None),
    )
    return jax.shard_map(
        per_device,
        mesh=mesh,
        in_specs=placed,
        out_specs=(
            P(("rep", "fsdp"), None, None),
            P(("rep", "fsdp"), None, None),
            P(None, "fsdp"),
            P(None, "fsdp"),
            P(None, "fsdp", None),
            P(None, "fsdp"),
            P(None, "fsdp"),
            P(None, "fsdp", None),
            P(None, "fsdp", None),
            P(None, "fsdp"),
            P(None, "fsdp"),
            P(None, "fsdp"),
            P(None, "fsdp"),
            P(None, "fsdp", None),
            P(None, "fsdp"),
            P(None, "fsdp", None),
            P(None, "fsdp"),
            P(None, "fsdp"),
        ),
        check_vma=False,
    )
```

profile of v0, /device:TPU:0, one launch (start us, length us, event | category | flops | bytes accessed | tf_op | source)
XLA Modules:
  0.0 3560.4 jit_solution(8374065612776506903)
XLA Ops:
  12.2 2.7 compare_select_fusion
  14.8 1.2 compare_and_fusion
  20.9 40.4 %all-reduce.27 = (bf16[768]{0:T(1024)(128)(2,1)S(1)}, bf16[768]{0:T(1024)(128)(2,1)S(1)}, bf16[768]{0:T(1024)(128)(2,1)S(1)}, bf16[768]{0:T(1024)(128)(2,1)S(1)}...) all-reduce(bf16[768]{0:T(1024)(128)(2,1)S(1)} %dynamic-update-slice, ...), channel_id=4, replica_groups=mesh['rep'=4,'fsdp'=8] {'fsdp'}, use_global_device_ids=true, to_apply=%add.4 | all-reduce | flops 7680 | bytes 30720
  65.1 32.6 all-gather.6
  98.2 128.8 %gather_fusion.1 = f32[38809,12]{1,0:T(8,128)} fusion(f32[2240,12]{1,0:T(8,128)S(1)} %bitcast_convert_fusion, s32[38912]{0:T(1024)S(1)} %pad_clamp_fusion.1), kind=kCustom, calls=%fused_computation.1.clone | custom fusion | bytes 3880900 | tf_op jit(solution)/shard_map/jit(_take)/gather | solution.py:33
  227.0 12.2 copy.82
  239.1 4.1 reshape.725
  243.2 3.4 copy.83
  246.8 3.6 select_bitcast_fusion.1
  250.3 7.4 pad_bitcast_fusion
  258.7 2.3 reshape.718
  261.0 1.5 pad_clamp_fusion
  262.5 608.4 %gather_fusion = f32[332929,12]{1,0:T(8,128)} fusion(f32[2240,12]{1,0:T(8,128)S(1)} %bitcast_convert_fusion, s32[333824]{0:T(1024)S(1)} %pad_clamp_fusion), kind=kCustom, calls=%fused_computation.clone | custom fusion | bytes 33292900 | tf_op jit(solution)/shard_map/jit(_take)/gather | solution.py:32
  870.9 90.3 %copy.79 = f32[332929,12]{0,1:T(8,128)} copy(f32[332929,12]{1,0:T(8,128)} %gather_fusion) | data formatting | bytes 31961184 | tf_op jit(solution)/shard_map/jit(_take)/gather | solution.py:32
  961.2 26.8 reshape.721
  988.0 18.5 copy.80
  1007.3 25.9 all-gather.13
  1033.2 21.1 scatter.16
  1054.4 17.1 scatter.19
  1071.5 12.4 select_bitcast_fusion
  1083.9 4.5 fusion.32
  1089.4 1.2 fusion.51
  1091.3 1.9 copy.76
  1093.2 2.6 copy.74
  1095.7 12.9 fusion.100
  1108.7 8.8 fusion.4
  1117.5 10.5 fusion.62
  1128.1 3.8 fusion.97
  1132.3 22.3 multiply_convert_fusion
  1154.7 12.0 convert_reduce_fusion
  1166.7 3.9 multiply_reduce_fusion
  1171.3 1.2 copy-done.11
  1174.5 2.5 fusion.103
  1177.1 3.4 convolution_convert_fusion
  1180.4 2.2 copy.85
  1182.7 16.6 fusion.1
  1199.3 20.2 fusion.93
  1219.5 1.8 convert_reduce_fusion.3
  1221.4 2.8 multiply_convert_fusion.1
  1224.2 9.5 convert_reduce_fusion.2
  1234.7 6.3 fusion.68
  1241.0 8.6 fusion.91
  1249.7 1.1 copy-done.27
  1250.8 9.0 fusion.87
  1261.9 12.1 fusion.3
  1274.0 18.4 copy.89
  1292.4 21.5 reshape.600
  1313.9 76.0 %copy.90 = f32[332929,12]{1,0:T(8,128)} copy(f32[332929,12]{0,1:T(8,128)} %reshape.600) | data formatting | bytes 31961184 | tf_op jit(solution)/shard_map/transpose | solution.py:62
  1389.9 6.9 fusion.37
  1396.8 3.3 copy.91
  1400.0 3.9 reshape.608
  1403.9 10.9 copy.92
  1414.8 1771.2 %scatter_custom_fusion = f32[2240,12]{1,0:T(8,128)S(1)} fusion(s32[332929]{0:T(1024)} %reshape.718, f32[332929,12]{1,0:T(8,128)} %copy.90, f32[]{:T(128)} %constant.261.clone.1), kind=kCustom, calls=%fused_computation.122 | custom fusion | flops 3995148 | bytes 108032 | tf_op jit(solution)/shard_map/scatter-add | solution.py:62
  3186.0 208.4 %scatter_fusion = f32[2240,12]{1,0:T(8,128)S(1)} fusion(f32[2240,12]{1,0:T(8,128)S(1)} %scatter_custom_fusion, s32[38809]{0:T(1024)S(1)} %copy-done.19, f32[38809,12]{1,0:T(8,128)} %copy.92), kind=kCustom, calls=%fused_computation.3 | custom fusion | flops 465708 | bytes 5743732 | tf_op jit(solution)/shard_map/scatter-add | solution.py:63
  3394.4 6.2 fusion.92
  3400.7 1.2 copy-done.17
  3403.5 9.8 fusion.57
  3413.3 42.0 %all-reduce.24 = (f32[768]{0:T(1024)S(1)}, f32[768]{0:T(1024)S(1)}, f32[768]{0:T(1024)S(1)}, f32[768]{0:T(1024)S(1)}, f32[768]{0:T(1024)S(1)}, /*index=5*/f32[76...) all-reduce(f32[768]{0:T(1024)S(1)} %get-tuple-element.138, ...), channel_id=18, replica_groups=mesh['rep'=4,'fsdp'=8] {'fsdp'}, use_global_device_ids=true, to_apply=%region_12.15.clone | all-reduce | flops 10752 | bytes 86016
  3455.8 12.3 reduce-scatter.16.cloned.1.call-done
  3468.1 14.4 all-reduce.25
  3483.2 62.6 %all-reduce.30.cloned.1.call-done = (f32[1,96,2304]{2,1,0:T(8,128)}, f32[1,96,768]{2,1,0:T(8,128)}, f32[1,96,3072]{2,1,0:T(8,128)}, f32[1,384,768]{2,1,0:T(8,128)}) async-done(((f32[1,96,2304]{2,1,0:T(8,128)}, f32[1,96,768]{2,1,0:T(8,128)}, f32[1,96,3072]{2,1,0:T(8,128)}, f32[1,384,768]{2,1,0:T(8,128)}), (f32[1,96,2304]{2,1,0:T(8,128)}, f32[1,96,768]{2,1,0:T(8,128)}, f32[1,96,3072]{2,1,0:T(8,128)}, ...) | async-done | bytes 3538960 | tf_op jit(solution)/shard_map/psum | solution.py:302
  3545.8 2.2 copy.116
  3548.0 1.7 copy.117
  3549.7 2.4 copy.118
  (238 shorter events, 24.8 us)
Async XLA Ops:
  7.2 7.6 copy-start.12
  7.2 1076.7 %all-gather.21.cloned.1.call-start = ((), (), s32[]{:S(2)}) async-start(), calls=%async_computation.9 | async-start | bytes 3981312 | tf_op jit(solution)/shard_map/all_gather | solution.py:379
  7.9 9.4 copy-start.58
  8.0 10.6 copy-start.61
  8.0 10.8 copy-start.62
  8.0 11.1 copy-start.63
  8.0 11.3 copy-start.64
  8.0 11.5 copy-start.65
  8.0 11.7 copy-start.66
  8.0 12.0 copy-start.67
  8.0 12.2 copy-start.68
  8.0 12.4 copy-start.69
  8.0 12.6 copy-start.70
  8.1 54.5 %copy-start.2 = (bf16[1,592,768]{2,1,0:T(8,128)(2,1)S(1)}, bf16[1,592,768]{2,1,0:T(8,128)(2,1)}, u32[]{:S(2)}) copy-start(bf16[1,592,768]{2,1,0:T(8,128)(2,1)} %param.41) | copy-start | bytes 2727940
  8.1 1120.0 %all-gather.23.cloned.1.call-start = ((), (), s32[]{:S(2)}) async-start(), calls=%async_computation.10 | async-start | bytes 1327104 | tf_op jit(solution)/shard_map/all_gather | solution.py:383
  8.8 1123.5 %all-gather.25.cloned.1.call-start = ((), (), s32[]{:S(2)}) async-start(), calls=%async_computation.11 | async-start | bytes 5308416 | tf_op jit(solution)/shard_map/all_gather | solution.py:388
  9.5 1145.1 %all-gather.27.cloned.1.call-start = ((), (), s32[]{:S(2)}) async-start(), calls=%async_computation.12 | async-start | bytes 5308416 | tf_op jit(solution)/shard_map/all_gather | solution.py:390
  10.1 3392.8 %reduce-scatter.10.cloned.1.call-start = ((), (), s32[]{:S(2)}) async-start(), calls=%async_computation.6 | async-start | bytes 2654208 | tf_op jit(solution)/shard_map/reduce_scatter | solution.py:291
  11.1 53.8 %copy-start.46 = (bf16[1,280,12]{1,2,0:T(8,128)(2,1)S(1)}, bf16[1,280,12]{1,2,0:T(8,128)(2,1)}, u32[]{:S(2)}) copy-start(bf16[1,280,12]{1,2,0:T(8,128)(2,1)} %param.50) | copy-start | bytes 20164
  98.1 128.8 %copy-start.18 = (s32[38809]{0:T(1024)}, s32[38809]{0:T(1024)S(1)}, u32[]{:S(2)}) copy-start(s32[38809]{0:T(1024)S(1)} %reshape.722) | copy-start | bytes 465712
  250.3 8.4 copy-start.13
  988.0 18.6 copy-start.21
  988.0 19.2 copy-start.57
  988.0 19.2 copy-start.56
  988.0 19.2 copy-start.55
  988.0 19.2 copy-start.54
  988.0 19.3 copy-start.59
  988.0 45.2 %copy-start.53 = (bf16[768]{0:T(1024)(128)(2,1)S(1)}, bf16[768]{0:T(1024)(128)(2,1)}, u32[]{:S(2)}) copy-start(bf16[768]{0:T(1024)(128)(2,1)} %get-tuple-element.182) | copy-start | bytes 4612
  988.0 45.2 %copy-start.1 = (f32[1,12,197,197]{2,3,1,0:T(8,128)S(1)}, f32[1,12,197,197]{2,3,1,0:T(8,128)}, u32[]{:S(2)}) copy-start(f32[1,12,197,197]{2,3,1,0:T(8,128)} %get-tuple-element.196) | copy-start | bytes 5588500
  1007.2 120.8 %copy-start.42 = (f32[768]{0:T(1024)}, f32[768]{0:T(1024)S(1)}, u32[]{:S(2)}) copy-start(f32[768]{0:T(1024)S(1)} %convert_element_type.232) | copy-start | bytes 9220
  1071.5 12.4 copy-start.3
  1071.5 12.4 copy-start.30
  1071.5 12.4 copy-start.35
  1071.5 12.4 copy-start.37
  1071.5 12.4 copy-start.48
  1083.9 5.5 copy-start.44
  1083.9 5.5 copy-start.45
  1091.3 17.4 copy-start.9
  1093.2 15.5 copy-start.6
  1108.7 8.8 copy-start.14
  1132.3 22.4 copy-start.34
  1154.6 12.0 copy-start.60
  1171.3 5.7 copy-start.39
  1177.0 2225.9 %reduce-scatter.8.cloned.1.call-start = ((), (), s32[]{:S(2)}) async-start(), calls=%async_computation.5 | async-start | bytes 7962624 | tf_op jit(solution)/shard_map/reduce_scatter | solution.py:287
  1199.3 20.2 copy-start.7
  1221.3 12.4 copy-start.16
  1224.2 9.6 copy-start.25
  1224.2 10.5 copy-start.31
  1224.2 10.5 copy-start.36
  1224.2 10.5 copy-start.38
  1224.2 10.5 copy-start.49
  1241.0 2162.0 %reduce-scatter.12.cloned.1.call-start = ((), (), s32[]{:S(2)}) async-start(), calls=%async_computation.7 | async-start | bytes 10616832 | tf_op jit(solution)/shard_map/reduce_scatter | solution.py:296
  1249.7 2153.3 %reduce-scatter.14.cloned.1.call-start = ((), (), s32[]{:S(2)}) async-start(), calls=%async_computation.8 | async-start | bytes 10616832 | tf_op jit(solution)/shard_map/reduce_scatter | solution.py:298
  1259.8 2208.3 %reduce-scatter.16.cloned.1.call-start = ((), (), s32[]{:S(2)}) async-start(), calls=%async_computation.13 | async-start | bytes 1290240
  1403.9 1782.1 %copy-start.19 = (s32[38809]{0:T(1024)S(1)}, s32[38809]{0:T(1024)}, u32[]{:S(2)}) copy-start(s32[38809]{0:T(1024)} %copy-done.18) | copy-start | bytes 465712
  3394.4 6.2 copy-start
  3394.4 6.2 copy-start.33
  3394.4 7.5 copy-start.4
  3402.8 143.0 %all-reduce.30.cloned.1.call-start = ((), (), s32[]{:S(2)}) async-start(), calls=%async_computation.14 | async-start | bytes 7077888 | tf_op jit(solution)/shard_map/psum | solution.py:302
  3403.5 9.9 copy-start.41
  3403.5 9.9 copy-start.47
  3403.5 9.9 copy-start.50
  3403.5 9.9 copy-start.51
  3545.8 6.3 copy-start.22
  (17 other events, 34.7 us)
Sparse Core Ops, SparseCore 0:
  10.2 74.8 all-gather.20
  87.2 38.6 all-gather.22
  128.2 78.6 all-gather.24
  208.9 78.0 all-gather.26
  1177.1 74.4 reduce-scatter.9
  1255.2 128.0 reduce-scatter.7
  1387.2 162.3 reduce-scatter.11
  1553.7 162.3 reduce-scatter.13
  3403.0 65.1 reduce-scatter.15
  3470.7 75.0 all-reduce.29
where the time goes:
time: 3570 us; the launch traced here: 3560 us
  other arithmetic  2060 us (58%)
  local copies, waits for them, and re-layouts  1100 us (31%)
  blocking collectives  155 us (4%)
  matrix products  146 us (4%)
  waiting for transfers between devices  78 us (2%)
    scatter-add x1, other arithmetic, table_gradient(): table_acc.at[large_index].add(jnp.transpose(large_part, (1, 2, 0)))  1770 us
    gather x4, local copies, waits for them, and re-layouts, pair_bias(): jnp.take(table_vals, large_index, axis=0)  744 us
    scatter-add x1, other arithmetic, table_gradient(): table_acc.at[small_index].add(jnp.transpose(small_part, (1, 2, 0)))  208 us
    gather x4, local copies, waits for them, and re-layouts, pair_bias(): jnp.take(table_vals, small_index, axis=0)  148 us
    transpose x3, local copies, waits for them, and re-layouts, table_gradient(): jnp.transpose(large_part, (1, 2, 0))  116 us
    unnamed x2, blocking collectives  82.5 us
  transfers between devices with their start and end apart: 10, of which 2 were waited for; matrix products, arithmetic and copies ran while one was open for 92% of the time, Pallas kernels for 0%

commit v1 on v0

v1 whole, which is shorter than its diff:
```python
import functools

import jax
import jax.numpy as jnp
import numpy as np
from jax import lax
from jax.experimental import pallas as pl
from jax.experimental.pallas import tpu as pltpu
from jax.sharding import PartitionSpec as P

f32 = jnp.float32
bf16 = jnp.bfloat16
norm_eps = 1e-06
neg_fill = -1000000000.0
vmem_bytes = 60 << 20

NN = (((1,), (0,)), ((), ()))
NT = (((1,), (1,)), ((), ()))
TN = (((0,), (0,)), ((), ()))


def mm(left, right, dims=NN):
    return lax.dot_general(left, right, dims, preferred_element_type=f32)


def round_up(value, unit):
    return -(-value // unit) * unit


class Plan:
    def __init__(self, small_len, large_len, rows):
        self.rows = rows
        self.small_len, self.large_len = small_len, large_len
        self.gs = int(round((small_len - 1) ** 0.5))
        self.gl = int(round((large_len - 1) ** 0.5))
        gl, gs = self.gl, self.gs
        self.strip_l = round_up(2 * gl * gl, 128)
        self.strip_s = round_up(2 * gs * (2 * gs - 1) + gs, 128)
        self.line = 2 * self.strip_l
        self.lanes = self.line + 128
        self.pad_cols = round_up(2 * gs * gs + 1, 128)
        self.pad_rows = 16 * gs
        self.cls_col = 2 * gs * gs
        self.cls_row = gs

    def place(self, di, dj, limit):
        gl = self.gl
        good = (np.abs(di) < limit) & (np.abs(dj) < limit)
        row = 1 + gl * np.maximum(di, 0) + np.maximum(dj, 0)
        col = 1 + gl * np.maximum(-di, 0) + np.maximum(-dj, 0)
        return np.where(good, row, 0), np.where(good, col, 0), good

    def positions(self):
        gl, gs = self.gl, self.gs
        x = np.arange(self.strip_l)
        rows, cols, goods = [], [], []
        for parity in range(2):
            m = 2 * ((x + gl) // (2 * gl)) if parity == 0 else 2 * (x // (2 * gl)) + 1
            t = x - gl * m
            r, c, g = self.place(gl - m, -t, gl)
            rows.append(r), cols.append(c), goods.append(g)
        large = [np.concatenate(v) for v in (rows, cols, goods)]
        x = np.arange(self.strip_s)
        m = x // (2 * gs)
        t = x - 2 * gs * m - gs
        small = [np.resize(np.zeros(1, v.dtype), self.line) for v in large]
        for dst, src in zip(small, self.place(gs - 1 - m, -t, gs)):
            dst[: self.strip_s] = src
        tail_r, tail_c, tail_g = np.zeros(128, int), np.zeros(128, int), np.zeros(128, bool)
        tail_r[:3], tail_c[:3], tail_g[:3] = (0, 1, 0), (1, 0, 0), True
        out = []
        for base in (large, small):
            out.append([np.concatenate(v) for v in zip(base, (tail_r, tail_c, tail_g))])
        return out

    def selectors(self):
        gs = self.gs
        rows = np.zeros((self.rows, self.pad_rows), np.float32)
        cols = np.zeros((self.pad_cols, self.rows), np.float32)
        for image in range(3):
            for tok in range(self.small_len):
                r = image * self.small_len + tok
                i, j = divmod(tok - 1, gs)
                rows[r, self.cls_row if tok == 0 else 16 * i + j] = 1
                cols[self.cls_col if tok == 0 else 2 * gs * i + j, r] = 1
        return jnp.asarray(rows, bf16), jnp.asarray(cols, bf16)


def table_labels(plan, large_index, kind):
    (lr, lc, lg), (sr, sc, sg) = plan.positions()
    is_large = kind == 1
    row = jnp.where(is_large, jnp.asarray(lr, jnp.int32), jnp.asarray(sr, jnp.int32))
    col = jnp.where(is_large, jnp.asarray(lc, jnp.int32), jnp.asarray(sc, jnp.int32))
    good = jnp.where(is_large, jnp.asarray(lg), jnp.asarray(sg))
    return jnp.where(good, large_index[row, col], -1).reshape(1, plan.lanes)


def iota(shape, dim):
    return lax.broadcasted_iota(jnp.int32, shape, dim)


def one_hot(lab_ref, chunk, buckets):
    lab = lab_ref[:, chunk * 128 : (chunk + 1) * 128]
    return jnp.where(iota((buckets, 128), 0) == lab, 1.0, 0.0).astype(bf16)


def row_roll(value, first, step, span):
    shape = value.shape
    out = pltpu.roll(value, first % span, axis=1) if first % span else value
    bit = 1
    while bit < shape[0]:
        moved = pltpu.roll(out, (step * bit) % span, axis=1)
        out = jnp.where((iota(shape, 0) & bit) != 0, moved, out)
        bit *= 2
    return out


def bias_large(plan, line_ref, h, out_ref):
    gl, rows, span = plan.gl, plan.rows, plan.strip_l
    f0 = jnp.broadcast_to(line_ref[h, :, 0:span], (gl, span))
    f1 = jnp.broadcast_to(line_ref[h, :, span : 2 * span], (gl, span))
    tail = line_ref[h, :, 2 * span : 2 * span + 128]
    r0 = row_roll(f0, -1, 1, span)
    r1 = row_roll(f1, -1, 1, span)
    odd = (iota((gl, span), 1) // gl) % 2
    odd = jnp.where(iota((gl, span), 0) == 0, 1 - odd, odd)
    strip = jnp.where(odd == 1, r1, r0)
    strip = jnp.concatenate([jnp.zeros((gl, 128), f32), strip, jnp.zeros((gl, 128), f32)], axis=1)
    wide = round_up(rows, 128)
    col = iota((2 * gl, wide), 1)
    bands = -(-rows // gl)
    for pair in range(-(-bands // 2)):
        parts = []
        for a in range(2 * pair, 2 * pair + 2):
            if a >= bands:
                parts.append(jnp.zeros((gl, wide), f32))
                continue
            move = 127 + gl * (gl - a)
            low = move // 128 * 128
            piece = strip[:, low : low + wide + 128]
            parts.append(pltpu.roll(piece, (wide + 128 - (move - low)) % (wide + 128), axis=1)[:, :wide])
        block = jnp.concatenate(parts, axis=0)
        row = iota((2 * gl, wide), 0) + 2 * gl * pair
        block = jnp.where(col == 0, tail[:, 1:2], block)
        if pair == 0:
            block = jnp.where(row == 0, jnp.where(col == 0, tail[:, 2:3], tail[:, 0:1]), block)
        block = jnp.where((row < plan.large_len) == (col < plan.large_len), block, neg_fill)
        block = jnp.where((row < plan.large_len) | (col < plan.large_len), block, 0.0)
        first = 2 * gl * pair
        count = min(2 * gl, rows - first)
        out_ref[0, first : first + count, :] = block[:count, :rows].astype(bf16)


def segment(plan, ids):
    n = plan.small_len
    return (
        jnp.where(ids >= n, 1, 0) + jnp.where(ids >= 2 * n, 1, 0) + jnp.where(ids >= 3 * n, 1, 0)
    )


def bias_small(plan, line_ref, rowsel_ref, colsel_ref, h, out_ref):
    gs, span, rows = plan.gs, plan.strip_s, plan.rows
    line = jnp.broadcast_to(line_ref[h, :, 0:span], (16, span))
    tail = line_ref[h, :, plan.line : plan.line + 128]
    strip = row_roll(line, -gs, 1, span)
    col = iota((16, plan.pad_cols), 1)
    row = iota((16, plan.pad_cols), 0)
    bands = []
    for i in range(gs):
        band = pltpu.roll(strip, (span - 2 * gs * (gs - 1 - i)) % span, axis=1)[:, : plan.pad_cols]
        band = jnp.where(col == plan.cls_col, tail[:, 1:2], band)
        if i == 0:
            edge = jnp.where(col == plan.cls_col, tail[:, 2:3], tail[:, 0:1])
            band = jnp.where(row == plan.cls_row, edge, band)
        bands.append(band)
    padded = jnp.concatenate(bands, axis=0).astype(bf16)
    cols = mm(padded, colsel_ref[...]).astype(bf16)
    full = mm(rowsel_ref[...], cols)
    same = segment(plan, iota((rows, rows), 0)) == segment(plan, iota((rows, rows), 1))
    out_ref[0] = jnp.where(same, full, neg_fill).astype(bf16)


def bias_kernel(plan, kind_ref, lab_ref, tab_ref, rowsel_ref, colsel_ref, out_ref, line_ref):
    h = pl.program_id(0)

    @pl.when(h == 0)
    def _():
        for chunk in range(plan.lanes // 128):
            part = mm(tab_ref[...], one_hot(lab_ref, chunk, tab_ref.shape[1]))
            for i in range(line_ref.shape[0]):
                line_ref[i, :, chunk * 128 : (chunk + 1) * 128] = part[i : i + 1]

    @pl.when(kind_ref[0] == 1)
    def _():
        bias_large(plan, line_ref, h, out_ref)

    @pl.when(kind_ref[0] != 1)
    def _():
        bias_small(plan, line_ref, rowsel_ref, colsel_ref, h, out_ref)


def whole(shape):
    zeros = (0,) * len(shape)
    return pl.BlockSpec(shape, lambda i: zeros)


smem_spec = pl.BlockSpec(memory_space=pltpu.SMEM)
params = pltpu.CompilerParams(vmem_limit_bytes=vmem_bytes)


def pair_bias(plan, kind, labels, table, rowsel, colsel):
    heads, buckets = table.shape
    table = jnp.pad(table, ((0, 16 - heads), (0, 0)))
    rows = plan.rows
    return pl.pallas_call(
        functools.partial(bias_kernel, plan),
        grid=(heads,),
        in_specs=[
            smem_spec,
            whole(labels.shape),
            whole(table.shape),
            whole(rowsel.shape),
            whole(colsel.shape),
        ],
        out_specs=pl.BlockSpec((1, rows, rows), lambda i: (i, 0, 0)),
        out_shape=jax.ShapeDtypeStruct((heads, rows, rows), bf16),
        scratch_shapes=[pltpu.VMEM((16, 1, plan.lanes), f32)],
        compiler_params=params,
        name="pair_bias",
    )(kind, labels, table, rowsel, colsel)


def fold_large(plan, ds_ref, h, line_ref):
    gl, rows, span = plan.gl, plan.rows, plan.strip_l
    wide = round_up(rows, 128)
    total = jnp.zeros((gl, span + 256), f32)
    pieces = {}
    bands = -(-rows // gl)
    side = jnp.zeros((1, 1), f32)
    for pair in range(-(-bands // 2)):
        first = 2 * gl * pair
        count = min(2 * gl, rows - first)
        block = ds_ref[0, first : first + count, :].astype(f32)
        block = jnp.concatenate([block, jnp.zeros((count, wide - rows), f32)], axis=1)
        if count < 2 * gl:
            block = jnp.concatenate([block, jnp.zeros((2 * gl - count, wide), f32)], axis=0)
        shape = (2 * gl, wide)
        col = iota(shape, 1)
        if pair == 0:
            row = iota(shape, 0)
            corner = jnp.sum(jnp.where((row == 0) & (col == 0), block, 0.0), keepdims=True)
            top = jnp.sum(jnp.where((row == 0) & (col > 0), block, 0.0), keepdims=True)
            block = jnp.where(row == 0, 0.0, block)
        side = side + jnp.sum(block[:, 0:1], keepdims=True)
        block = jnp.where(col == 0, 0.0, block)
        for half in range(2):
            a = 2 * pair + half
            if a >= bands:
                continue
            move = 127 + gl * (gl - a)
            low = move // 128 * 128
            piece = block[half * gl : (half + 1) * gl]
            piece = jnp.concatenate([piece, jnp.zeros((gl, 128), f32)], axis=1)
            piece = pltpu.roll(piece, move - low, axis=1) if move > low else piece
            pieces[low] = piece if low not in pieces else pieces[low] + piece
    for low, piece in pieces.items():
        parts = [piece]
        if low:
            parts.insert(0, jnp.zeros((gl, low), f32))
        rest = span + 256 - low - wide - 128
        if rest > 0:
            parts.append(jnp.zeros((gl, rest), f32))
        total = total + jnp.concatenate(parts, axis=1)[:, : span + 256]
    strip = total[:, 128 : 128 + span]
    odd = (iota((gl, span), 1) // gl) % 2
    odd = jnp.where(iota((gl, span), 0) == 0, 1 - odd, odd)
    for parity in range(2):
        part = jnp.where(odd == parity, strip, 0.0)
        part = row_roll(part, 1, -1, span)
        line_ref[h, :, parity * span : (parity + 1) * span] = jnp.sum(
            part, axis=0, keepdims=True
        )
    store_tail(plan, line_ref, h, top, side, corner)


def store_tail(plan, line_ref, h, top, side, corner):
    lane = iota((1, 128), 1)
    tail = jnp.where(lane == 0, top, jnp.where(lane == 1, side, jnp.where(lane == 2, corner, 0.0)))
    line_ref[h, :, plan.line : plan.line + 128] = tail


def fold_small(plan, ds_ref, rowsel_ref, colsel_ref, h, line_ref):
    gs, span = plan.gs, plan.strip_s
    cols = mm(ds_ref[0], colsel_ref[...], NT).astype(bf16)
    padded = mm(rowsel_ref[...], cols, TN)
    row = iota((16, plan.pad_cols), 0)
    col = iota((16, plan.pad_cols), 1)
    total = jnp.zeros((16, span), f32)
    side = jnp.zeros((1, 1), f32)
    for i in range(gs):
        band = padded[16 * i : 16 * (i + 1)]
        if i == 0:
            is_top = row == plan.cls_row
            corner = jnp.sum(jnp.where(is_top & (col == plan.cls_col), band, 0.0), keepdims=True)
            top = jnp.sum(jnp.where(is_top & (col < plan.cls_col), band, 0.0), keepdims=True)
            band = jnp.where(is_top, 0.0, band)
        side = side + jnp.sum(jnp.where(col == plan.cls_col, band, 0.0), keepdims=True)
        band = jnp.where(col < plan.cls_col, band, 0.0)
        band = jnp.concatenate([band, jnp.zeros((16, span - plan.pad_cols), f32)], axis=1)
        move = 2 * gs * (gs - 1 - i)
        total = total + (pltpu.roll(band, move, axis=1) if move else band)
    total = row_roll(total, gs, -1, span)
    line_ref[h, :, 0 : plan.line] = jnp.zeros((1, plan.line), f32)
    line_ref[h, :, 0:span] = jnp.sum(total, axis=0, keepdims=True)
    store_tail(plan, line_ref, h, top, side, corner)


def fold_kernel(plan, kind_ref, ds_ref, lab_ref, rowsel_ref, colsel_ref, out_ref, line_ref):
    h = pl.program_id(0)

    @pl.when(h == 0)
    def _():
        line_ref[...] = jnp.zeros_like(line_ref)

    @pl.when(kind_ref[0] == 1)
    def _():
        fold_large(plan, ds_ref, h, line_ref)

    @pl.when(kind_ref[0] != 1)
    def _():
        fold_small(plan, ds_ref, rowsel_ref, colsel_ref, h, line_ref)

    @pl.when(h == pl.num_programs(0) - 1)
    def _():
        buckets = out_ref.shape[1]
        total = jnp.zeros(out_ref.shape, f32)
        for chunk in range(plan.lanes // 128):
            hot = one_hot(lab_ref, chunk, buckets)
            part = jnp.concatenate(
                [line_ref[i, :, chunk * 128 : (chunk + 1) * 128] for i in range(16)], axis=0
            )
            high = part.astype(bf16)
            low = (part - high.astype(f32)).astype(bf16)
            total = total + mm(high, hot, NT) + mm(low, hot, NT)
        out_ref[...] = total


def table_gradient(plan, kind, d_scores, labels, rowsel, colsel, buckets):
    heads, rows, _ = d_scores.shape
    return pl.pallas_call(
        functools.partial(fold_kernel, plan),
        grid=(heads,),
        in_specs=[
            smem_spec,
            pl.BlockSpec((1, rows, rows), lambda i: (i, 0, 0)),
            whole(labels.shape),
            whole(rowsel.shape),
            whole(colsel.shape),
        ],
        out_specs=whole((16, buckets)),
        out_shape=jax.ShapeDtypeStruct((16, buckets), f32),
        scratch_shapes=[pltpu.VMEM((16, 1, plan.lanes), f32)],
        compiler_params=params,
        name="table_gradient",
    )(kind, d_scores, labels, rowsel, colsel)


def norm_stats(values):
    mean = jnp.mean(values, axis=1, keepdims=True)
    centred = values - mean
    var = jnp.mean(centred * centred, axis=1, keepdims=True)
    inv = lax.rsqrt(var + norm_eps)
    return centred * inv, inv


def norm_back(d_out, gain, normal, inv):
    d_normal = d_out * gain
    mean_d = jnp.mean(d_normal, axis=1, keepdims=True)
    mean_dn = jnp.mean(d_normal * normal, axis=1, keepdims=True)
    return inv * (d_normal - mean_d - normal * mean_dn)


def rows_sum(values):
    return jnp.sum(values, axis=0, keepdims=True)


def gelu_parts(v):
    size = jnp.abs(v)
    bell = jnp.exp(-0.5 * v * v)
    t = 1.0 / (1.0 + (0.3275911 * 0.7071067811865476) * size)
    poly = t * (
        0.127414796
        + t * (-0.142248368 + t * (0.7107068705 + t * (-0.7265760135 + t * 0.5307027145)))
    )
    tail = poly * bell
    phi = jnp.where(v < 0, tail, 1.0 - tail)
    return v * phi, phi + v * bell * 0.3989422804014327


(
    FIRST_GAIN,
    FIRST_SHIFT,
    QUERY_BIAS,
    VALUE_BIAS,
    OUTPUT_BIAS,
    ATTEND_SCALE,
    SECOND_GAIN,
    SECOND_SHIFT,
    REDUCE_BIAS,
    FEED_SCALE,
) = range(10)


def vec(ref, idx):
    return ref[idx : idx + 1, :]


def project_kernel(tok_ref, vec_ref, w_ref, normed_ref, out_ref):
    part = pl.program_id(0)

    @pl.when(part == 0)
    def _():
        normal, _ = norm_stats(tok_ref[...].astype(f32))
        normed_ref[...] = (normal * vec(vec_ref, FIRST_GAIN) + vec(vec_ref, FIRST_SHIFT)).astype(
            bf16
        )

    bias = jnp.where(
        part == 0,
        vec(vec_ref, QUERY_BIAS),
        jnp.where(part == 2, vec(vec_ref, VALUE_BIAS), 0.0),
    )
    scale = jnp.where(part == 0, 0.125, 1.0)
    triple = mm(normed_ref[...], w_ref[...]) + bias
    out_ref[...] = (triple.astype(bf16).astype(f32) * scale).astype(bf16)


def project(tokens, vecs, weight):
    rows, width = tokens.shape
    return pl.pallas_call(
        project_kernel,
        grid=(3,),
        in_specs=[
            whole(tokens.shape),
            whole(vecs.shape),
            pl.BlockSpec((width, width), lambda i: (0, i)),
        ],
        out_specs=[whole(tokens.shape), pl.BlockSpec((rows, width), lambda i: (0, i))],
        out_shape=[
            jax.ShapeDtypeStruct((rows, width), bf16),
            jax.ShapeDtypeStruct((rows, 3 * width), bf16),
        ],
        compiler_params=params,
        name="project",
    )(tokens, vecs, weight)


def half_mask(rows):
    return iota((rows, 128), 1) < 64


def attend_kernel(q_ref, k_ref, v_ref, b_ref, mixed_ref, p_ref):
    q, k, v = q_ref[...], k_ref[...], v_ref[...]
    lower = half_mask(q.shape[0])
    mixed = []
    for t in range(2):
        keep = lower if t == 0 else ~lower
        scores = mm(jnp.where(keep, q, jnp.zeros_like(q)), k, NT) + b_ref[t].astype(f32)
        top = jnp.max(scores, axis=1, keepdims=True)
        exps = jnp.exp(scores - top)
        total = jnp.sum(exps, axis=1, keepdims=True)
        probs = (exps * (1.0 / total)).astype(bf16)
        p_ref[t] = probs
        mixed.append(mm(probs, v))
    mixed_ref[...] = jnp.where(lower, mixed[0], mixed[1]).astype(bf16)


def attend(triple, bias):
    rows = triple.shape[0]
    heads = bias.shape[0]
    pairs = heads // 2
    cols = lambda part: pl.BlockSpec((rows, 128), lambda i: (0, i + part * pairs))
    square = pl.BlockSpec((2, rows, rows), lambda i: (i, 0, 0))
    return pl.pallas_call(
        attend_kernel,
        grid=(pairs,),
        in_specs=[cols(0), cols(1), cols(2), square],
        out_specs=[cols(0), square],
        out_shape=[
            jax.ShapeDtypeStruct((rows, 64 * heads), bf16),
            jax.ShapeDtypeStruct((heads, rows, rows), bf16),
        ],
        compiler_params=params,
        name="attend",
    )(triple, triple, triple, bias)


def attend_back_kernel(q_ref, k_ref, v_ref, do_ref, m_ref, p_ref, dq_ref, dk_ref, dv_ref, ds_ref):
    q, k, v, do = q_ref[...], k_ref[...], v_ref[...], do_ref[...]
    lower = half_mask(q.shape[0])
    prod = do.astype(f32) * m_ref[...].astype(f32)
    dq, dk, dv = [], [], []
    for t in range(2):
        keep = lower if t == 0 else ~lower
        d_mixed = jnp.where(keep, do, jnp.zeros_like(do))
        delta = jnp.sum(jnp.where(keep, prod, 0.0), axis=1, keepdims=True)
        d_probs = mm(d_mixed, v, NT)
        probs = p_ref[t]
        d_scores = (probs.astype(f32) * (d_probs - delta)).astype(bf16)
        ds_ref[t] = d_scores
        dq.append(mm(d_scores, k))
        dk.append(mm(d_scores, q, TN))
        dv.append(mm(probs, do, TN))
    dq_ref[...] = (jnp.where(lower, dq[0], dq[1]) * 0.125).astype(bf16)
    dk_ref[...] = jnp.where(lower, dk[0], dk[1]).astype(bf16)
    dv_ref[...] = jnp.where(lower, dv[0], dv[1]).astype(bf16)


def attend_back(triple, d_mixed, mixed, probs):
    heads, rows, _ = probs.shape
    pairs = heads // 2
    cols = lambda part: pl.BlockSpec((rows, 128), lambda i: (0, i + part * pairs))
    square = pl.BlockSpec((2, rows, rows), lambda i: (i, 0, 0))
    wide = jax.ShapeDtypeStruct((rows, 64 * heads), bf16)
    return pl.pallas_call(
        attend_back_kernel,
        grid=(pairs,),
        in_specs=[cols(0), cols(1), cols(2), cols(0), cols(0), square],
        out_specs=[cols(0), cols(0), cols(0), square],
        out_shape=[wide, wide, wide, jax.ShapeDtypeStruct(probs.shape, bf16)],
        compiler_params=params,
        name="attend_back",
    )(triple, triple, triple, d_mixed, mixed, probs)


def feed_kernel(
    plan,
    kind_ref,
    tok_ref,
    cot_ref,
    mixed_ref,
    wo_ref,
    vec_ref,
    be_ref,
    we_ref,
    wr_ref,
    out_ref,
    dmid_ref,
    dmix_ref,
    dwo_ref,
    dwe_ref,
    dwr_ref,
    small_ref,
    dbe_ref,
    middle_ref,
    branch_ref,
    second_ref,
    dfeed_ref,
    feed_ref,
    dsec_ref,
):
    step = pl.program_id(0)
    rows = plan.rows

    def masked_cot():
        limit = jnp.where(kind_ref[0] == 1, plan.large_len, 3 * plan.small_len)
        live = iota((rows, 1), 0) < limit
        return jnp.where(live, cot_ref[...].astype(f32), 0.0)

    @pl.when(step == 0)
    def _():
        branch = mm(mixed_ref[...], wo_ref[...]) + vec(vec_ref, OUTPUT_BIAS)
        branch_ref[...] = branch
        middle = tok_ref[...].astype(f32) + vec(vec_ref, ATTEND_SCALE) * branch
        middle_ref[...] = middle
        normal, _ = norm_stats(middle)
        second_ref[...] = (
            normal * vec(vec_ref, SECOND_GAIN) + vec(vec_ref, SECOND_SHIFT)
        ).astype(bf16)
        dfeed_ref[...] = (vec(vec_ref, FEED_SCALE) * masked_cot()).astype(bf16)
        feed_ref[...] = jnp.zeros_like(feed_ref)
        dsec_ref[...] = jnp.zeros_like(dsec_ref)

    second, d_feed = second_ref[...], dfeed_ref[...]
    we, wr = we_ref[...], wr_ref[...]
    pre = mm(second, we) + be_ref[...]
    value, slope = gelu_parts(pre)
    activated = value.astype(bf16)
    feed_ref[...] += mm(activated, wr)
    d_pre = (mm(d_feed, wr, NT) * slope).astype(bf16)
    dsec_ref[...] += mm(d_pre, we, NT)
    dwr_ref[...] = mm(activated, d_feed, TN).astype(bf16)
    dwe_ref[...] = mm(second, d_pre, TN).astype(bf16)
    dbe_ref[...] = rows_sum(d_pre.astype(f32))

    @pl.when(step == pl.num_programs(0) - 1)
    def _():
        feed_out = feed_ref[...] + vec(vec_ref, REDUCE_BIAS)
        middle = middle_ref[...]
        out_ref[...] = (middle + vec(vec_ref, FEED_SCALE) * feed_out).astype(bf16)
        grad = masked_cot()
        d_second = dsec_ref[...]
        normal, inv = norm_stats(middle)
        d_middle = grad + norm_back(d_second, vec(vec_ref, SECOND_GAIN), normal, inv)
        dmid_ref[...] = d_middle
        d_branch = (vec(vec_ref, ATTEND_SCALE) * d_middle).astype(bf16)
        dwo_ref[...] = mm(mixed_ref[...], d_branch, TN).astype(bf16)
        dmix_ref[...] = mm(d_branch, wo_ref[...], NT).astype(bf16)
        small_ref[...] = jnp.zeros_like(small_ref)
        small_ref[FEED_SCALE : FEED_SCALE + 1, :] = rows_sum(grad * feed_out)
        small_ref[REDUCE_BIAS : REDUCE_BIAS + 1, :] = rows_sum(dfeed_ref[...].astype(f32))
        small_ref[SECOND_GAIN : SECOND_GAIN + 1, :] = rows_sum(d_second * normal)
        small_ref[SECOND_SHIFT : SECOND_SHIFT + 1, :] = rows_sum(d_second)
        small_ref[ATTEND_SCALE : ATTEND_SCALE + 1, :] = rows_sum(d_middle * branch_ref[...])
        small_ref[OUTPUT_BIAS : OUTPUT_BIAS + 1, :] = rows_sum(d_branch.astype(f32))


def feed(plan, kind, tokens, cot, mixed, wo, vecs, be, we, wr):
    rows, width = tokens.shape
    hidden = we.shape[1]
    tile = 512
    sds = jax.ShapeDtypeStruct
    return pl.pallas_call(
        functools.partial(feed_kernel, plan),
        grid=(hidden // tile,),
        in_specs=[
            smem_spec,
            whole(tokens.shape),
            whole(cot.shape),
            whole(mixed.shape),
            whole(wo.shape),
            whole(vecs.shape),
            pl.BlockSpec((1, tile), lambda i: (0, i)),
            pl.BlockSpec((width, tile), lambda i: (0, i)),
            pl.BlockSpec((tile, width), lambda i: (i, 0)),
        ],
        out_specs=[
            whole((rows, width)),
            whole((rows, width)),
            whole((rows, width)),
            whole((width, width)),
            pl.BlockSpec((width, tile), lambda i: (0, i)),
            pl.BlockSpec((tile, width), lambda i: (i, 0)),
            whole(vecs.shape),
            pl.BlockSpec((1, tile), lambda i: (0, i)),
        ],
        out_shape=[
            sds((rows, width), bf16),
            sds((rows, width), f32),
            sds((rows, width), bf16),
            sds((width, width), bf16),
            sds((width, hidden), bf16),
            sds((hidden, width), bf16),
            sds(vecs.shape, f32),
            sds((1, hidden), f32),
        ],
        scratch_shapes=[
            pltpu.VMEM((rows, width), f32),
            pltpu.VMEM((rows, width), f32),
            pltpu.VMEM((rows, width), bf16),
            pltpu.VMEM((rows, width), bf16),
            pltpu.VMEM((rows, width), f32),
            pltpu.VMEM((rows, width), f32),
        ],
        compiler_params=params,
        name="feed",
    )(kind, tokens, cot, mixed, wo, vecs, be, we, wr)


def finish_kernel(
    tok_ref, dmid_ref, normed_ref, vec_ref, dt_ref, w_ref, dw_ref, out_ref, small_ref, acc_ref
):
    part = pl.program_id(0)

    @pl.when(part == 0)
    def _():
        acc_ref[...] = jnp.zeros_like(acc_ref)
        small_ref[...] = jnp.zeros_like(small_ref)

    d_part = dt_ref[0]
    dw_ref[...] = mm(normed_ref[...], d_part, TN).astype(bf16)
    acc_ref[...] += mm(d_part, w_ref[...], NT)
    sums = rows_sum(d_part.astype(f32))

    @pl.when(part == 0)
    def _():
        small_ref[QUERY_BIAS : QUERY_BIAS + 1, :] = sums

    @pl.when(part == 2)
    def _():
        small_ref[VALUE_BIAS : VALUE_BIAS + 1, :] = sums
        d_normed = acc_ref[...]
        normal, inv = norm_stats(tok_ref[...].astype(f32))
        back = norm_back(d_normed, vec(vec_ref, FIRST_GAIN), normal, inv)
        out_ref[...] = (dmid_ref[...] + back).astype(bf16)
        small_ref[FIRST_GAIN : FIRST_GAIN + 1, :] = rows_sum(d_normed * normal)
        small_ref[FIRST_SHIFT : FIRST_SHIFT + 1, :] = rows_sum(d_normed)


def finish(tokens, d_middle, normed, vecs, d_triple, weight):
    rows, width = tokens.shape
    sds = jax.ShapeDtypeStruct
    return pl.pallas_call(
        finish_kernel,
        grid=(3,),
        in_specs=[
            whole(tokens.shape),
            whole(d_middle.shape),
            whole(normed.shape),
            whole(vecs.shape),
            pl.BlockSpec((1, rows, width), lambda i: (i, 0, 0)),
            pl.BlockSpec((width, width), lambda i: (0, i)),
        ],
        out_specs=[
            pl.BlockSpec((width, width), lambda i: (0, i)),
            whole(tokens.shape),
            whole(vecs.shape),
        ],
        out_shape=[
            sds(weight.shape, bf16),
            sds(tokens.shape, bf16),
            sds(vecs.shape, f32),
        ],
        scratch_shapes=[pltpu.VMEM((rows, width), f32)],
        compiler_params=params,
        name="finish",
    )(tokens, d_middle, normed, vecs, d_triple, weight)


def per_device(
    tokens,
    slot_kinds,
    small_index,
    large_index,
    first_gain,
    first_shift,
    triple_weight,
    query_bias,
    value_bias,
    bias_table,
    output_weight,
    output_bias,
    attend_scale,
    second_gain,
    second_shift,
    expand_weight,
    expand_bias,
    reduce_weight,
    reduce_bias,
    feed_scale,
    cotangent,
):
    _, rows, width = tokens.shape
    heads = bias_table.shape[2]
    plan = Plan(small_index.shape[0], large_index.shape[0], rows)
    tokens, cotangent = tokens[0], cotangent[0]
    gather = lambda value: lax.all_gather(value, "fsdp", axis=0, tiled=True)

    short = [
        first_gain,
        first_shift,
        query_bias,
        value_bias,
        output_bias,
        attend_scale,
        second_gain,
        second_shift,
        reduce_bias,
        feed_scale,
    ]
    share = first_gain.shape[1]
    wide_share = expand_bias.shape[1]
    bucket_share = bias_table.shape[1]
    packed = jnp.concatenate(
        [v[0] for v in short] + [expand_bias[0], bias_table[0].T.reshape(-1)], axis=0
    )
    packed = lax.all_gather(packed, "fsdp", axis=0, tiled=False)
    n = packed.shape[0]
    cut = len(short) * share
    vecs = packed[:, :cut].reshape(n, len(short), share).transpose(1, 0, 2)
    vecs = jnp.pad(vecs.reshape(len(short), width).astype(f32), ((0, 16 - len(short)), (0, 0)))
    be = packed[:, cut : cut + wide_share].reshape(1, n * wide_share).astype(f32)
    table = packed[:, cut + wide_share :].reshape(n, heads, bucket_share).transpose(1, 0, 2)
    table = table.reshape(heads, n * bucket_share)

    wt = gather(triple_weight[0])
    wo = gather(output_weight[0])
    we = gather(expand_weight[0])
    wr = gather(reduce_weight[0])

    rowsel, colsel = plan.selectors()
    labels = table_labels(plan, large_index, slot_kinds[0])
    bias = pair_bias(plan, slot_kinds, labels, table, rowsel, colsel)

    normed, triple = project(tokens, vecs, wt)
    mixed, probs = attend(triple, bias)
    block_output, d_middle, d_mixed, dwo, dwe, dwr, small_a, dbe = feed(
        plan, slot_kinds, tokens, cotangent, mixed, wo, vecs, be, we, wr
    )
    dq, dk, dv, d_scores = attend_back(triple, d_mixed, mixed, probs)
    d_table = table_gradient(plan, slot_kinds, d_scores, labels, rowsel, colsel, table.shape[1])
    dwt, token_grad, small_b = finish(
        tokens, d_middle, normed, vecs, jnp.stack([dq, dk, dv]), wt
    )

    def reduce_weight_part(value):
        value = lax.psum_scatter(value, "fsdp", scatter_dimension=0, tiled=True)
        return lax.psum(value, "rep").astype(f32)[None]

    smalls = (small_a + small_b)[: len(short)]
    smalls = lax.psum((smalls, dbe, d_table[:heads]), ("rep", "fsdp"))
    me = lax.axis_index("fsdp")
    cut_of = lambda value, size: lax.dynamic_slice_in_dim(value, me * size, size, axis=1)
    small = cut_of(smalls[0], share)
    d_be = cut_of(smalls[1], wide_share)
    d_tab = cut_of(smalls[2], bucket_share).T[None]
    row = lambda idx: small[idx : idx + 1]
    return (
        block_output[None],
        token_grad[None],
        row(FIRST_GAIN),
        row(FIRST_SHIFT),
        reduce_weight_part(dwt),
        row(QUERY_BIAS),
        row(VALUE_BIAS),
        d_tab,
        reduce_weight_part(dwo),
        row(OUTPUT_BIAS),
        row(ATTEND_SCALE),
        row(SECOND_GAIN),
        row(SECOND_SHIFT),
        reduce_weight_part(dwe),
        d_be,
        reduce_weight_part(dwr),
        row(REDUCE_BIAS),
        row(FEED_SCALE),
    )


def solution(mesh):
    rows = P(("rep", "fsdp"), None, None)
    vector = P(None, "fsdp")
    matrix = P(None, "fsdp", None)
    weights = (
        vector,
        vector,
        matrix,
        vector,
        vector,
        matrix,
        matrix,
        vector,
        vector,
        vector,
        vector,
        matrix,
        vector,
        matrix,
        vector,
        vector,
    )
    return jax.shard_map(
        per_device,
        mesh=mesh,
        in_specs=(rows, P(("rep", "fsdp")), P(), P()) + weights + (rows,),
        out_specs=(rows, rows) + weights,
        check_vma=False,
    )
```

time: 3570 us -> 929 us (0.26)
  other arithmetic: 2060 us -> 11.1 us
  local copies, waits for them, and re-layouts: 1100 us -> 35 us
  waiting for transfers between devices: 78 us -> 704 us
  matrix products: 146 us -> 0 us
  Pallas kernels: 0 us -> 121 us
  blocking collectives: 155 us -> 41.1 us
    scatter-add x2 -> x0, other arithmetic: 1980 us -> none  [the longest x1 1770 us: table_gradient(): table_acc.at[large_index].add(jnp.transpose(large_part, (1, 2, 0)))]
    gather x8 -> x1, local copies, waits for them, and re-layouts: 892 us -> 18.8 us  [table_labels(): return jnp.where(good, large_index[row, col], -1).reshape(1, plan.lanes)]
    reduce_scatter x4, waiting for transfers between devices: 0.08 us -> 287 us  [reduce_weight_part(): value = lax.psum_scatter(value, 'fsdp', scatter_dimension=0, tiled=True)]
    all_gather x4, waiting for transfers between devices: 0.03 us -> 232 us  [per_device(): gather = lambda value: lax.all_gather(value, 'fsdp', axis=0, tiled=True)]
    dot_general x18 -> x0, matrix products: 146 us -> none  [the longest x1 22.3 us: forward_layer(): jnp.dot(second, expand_weight, preferred_element_type=jnp.float32)]
    transpose x6 -> x1, local copies, waits for them, and re-layouts: 134 us -> 0.02 us  [per_device(): packed[:, cut + wide_share:].reshape(n, heads, bucket_share)]
    pallas_call x0 -> x7, Pallas kernels: none -> 121 us  [the longest x1 36.1 us: feed(): pl.pallas_call(functools.partial(feed_kernel, plan), grid=(hidden // tile...]
    unnamed x2 -> x0, blocking collectives: 82.5 us -> none
  transfers between devices with their start and end apart: 10 -> 11, of which waited for: 2 -> 11; matrix products, arithmetic and copies ran while one was open for 92% -> 3% of each run, Pallas kernels for 0% -> 9%
where the time goes in v1:
time: 929 us; the launch traced here: 928 us
  waiting for transfers between devices  704 us (76%)
  Pallas kernels  121 us (13%)
  blocking collectives  41.1 us (4%)
  local copies, waits for them, and re-layouts  35 us (4%)
  between operations  15.5 us (2%)
  other arithmetic  11.1 us (1%)
    reduce_scatter x4, waiting for transfers between devices, reduce_weight_part(): value = lax.psum_scatter(value, 'fsdp', scatter_dimension=0, tiled=True)  287 us
    all_gather x4, waiting for transfers between devices, per_device(): gather = lambda value: lax.all_gather(value, 'fsdp', axis=0, tiled=True)  232 us
    psum x1, waiting for transfers between devices, per_device(): smalls = lax.psum((smalls, dbe, d_table[:heads]), ('rep', 'fsdp'))  84.1 us
    unnamed x12, waiting for transfers between devices  52.4 us
    psum x1, waiting for transfers between devices, reduce_weight_part(): return lax.psum(value, 'rep').astype(f32)[None]  49.8 us
    psum x1, blocking collectives, per_device(): smalls = lax.psum((smalls, dbe, d_table[:heads]), ('rep', 'fsdp'))  41.1 us
    pallas_call x1, Pallas kernels, feed(): pl.pallas_call(functools.partial(feed_kernel, plan), grid=(hidden // tile...  36.1 us
    pallas_call x1, Pallas kernels, table_gradient(): pl.pallas_call(functools.partial(fold_kernel, plan), grid=(heads,), in_sp...  22.2 us
  transfers between devices with their start and end apart: 11, of which 11 were waited for; matrix products, arithmetic and copies ran while one was open for 3% of the time, Pallas kernels for 9%

profile of v1, /device:TPU:0, one launch (start us, length us, event | category | flops | bytes accessed | tf_op | source)
XLA Modules:
  0.0 928.0 jit_solution(2849761457514122248)
XLA Ops:
  7.3 0.0 all-reduce.11.cloned.1.call-start
  7.3 0.9 reshape.71
  8.2 0.7 reduce
  8.9 1.2 dynamic-slice
  10.8 6.8 concatenate.6
  17.6 0.4 dynamic-update-slice
  18.0 0.6 copy-done.4
  18.6 0.0 all-gather.10.cloned.1.call-start
  18.7 0.7 all-gather.10.cloned.1.call-update
  19.4 0.0 all-gather.12.cloned.1.call-start
  19.4 0.7 all-gather.12.cloned.1.call-update
  20.1 0.0 all-gather.14.cloned.1.call-start
  20.2 0.5 all-gather.14.cloned.1.call-update
  20.7 0.0 all-gather.16.cloned.1.call-start
  20.7 0.5 all-gather.16.cloned.1.call-update
  21.3 0.0 reduce-scatter.7.cloned.1.call-start
  22.1 18.8 %gather_fusion = s32[2432]{0:T(1024)S(1)} fusion(s32[577,577]{1,0:T(8,128)S(1)} %copy-done, s32[2432]{0:T(1024)S(1)} %fusion.2), kind=kCustom, calls=%fused_computation | custom fusion | bytes 38912 | tf_op jit(solution)/shard_map/gather | solution.py:95
  41.0 0.6 reshape.72.lab_ref
  41.6 48.5 %all-reduce.11.cloned.1.call-done = bf16[37632]{0:T(1024)(128)(2,1)} async-done(((bf16[37632]{0:T(1024)(128)(2,1)}), bf16[37632]{0:T(1024)(128)(2,1)}) %all-reduce.11.cloned.1.call-update) | async-done | bytes 75280
  90.1 1.0 reshape.82
  91.1 0.1 slice.63
  91.2 0.1 convert_element_type.23
  91.3 0.1 convert_element_type.25
  91.4 0.2 reshape.73
  91.6 0.1 reshape.74
  91.7 0.6 pad.12.tab_ref
  92.4 0.1 convert_bitcast_fusion
  92.5 0.6 copy.51
  93.1 13.3 %pair_bias.1.b_ref = bf16[12,592,592]{2,1,0:T(8,128)(2,1)} custom-call(s32[1]{0:T(128)S(6)} %copy.59.kind_ref, s32[1,2432]{1,0:T(1,128)} %reshape.72.lab_ref, bf16[16,2240]{1,0:T(8,128)(2,1)} %pad.12.tab_ref, bf16[592,224]{1,0:T(8,128)(2,1)} %constant.46.clone.rowsel_ref, bf16[512,592]{1,0:T(8,128)(2,1)} %constant.47.clone.colsel_ref), custom_call_target="tpu_custom_call" | custom-call | tf_op jit(solution)/shard_map/pair_bias/pallas_call | solution.py:215
  106.4 0.6 pad_convert_fusion.vec_ref
  107.0 50.3 %all-gather.10.cloned.1.call-done = bf16[1,768,2304]{2,1,0:T(8,128)(2,1)} async-done(((bf16[1,96,2304]{2,1,0:T(8,128)(2,1)}), bf16[1,768,2304]{2,1,0:T(8,128)(2,1)}) %all-gather.10.cloned.1.call-update) | async-done | bytes 3538960 | tf_op jit(solution)/shard_map/all_gather | solution.py:757
  157.3 6.6 project.1
  163.9 14.8 %attend.1 = (bf16[592,768]{1,0:T(8,128)(2,1)}, bf16[12,592,592]{2,1,0:T(8,128)(2,1)}) custom-call(bf16[592,2304]{1,0:T(8,128)(2,1)} %get-tuple-element.37.q_ref.k_ref.v_ref, bf16[592,2304]{1,0:T(8,128)(2,1)} %get-tuple-element.37.q_ref.k_ref.v_ref, bf16[592,2304]{1,0:T(8,128)(2,1)} %get-tuple-element.37.q_ref.k_ref.v_ref, bf16[12,592,592]{2,1,0:T(8,128)(2,1)} %pair_bias.1.b_ref), custom_call_target="tpu_custom_call" | custom-call | tf_op jit(solution)/shard_map/attend/pallas_call | solution.py:484
  178.7 20.4 %all-gather.12.cloned.1.call-done = bf16[1,768,768]{2,1,0:T(8,128)(2,1)} async-done(((bf16[1,96,768]{2,1,0:T(8,128)(2,1)}), bf16[1,768,768]{2,1,0:T(8,128)(2,1)}) %all-gather.12.cloned.1.call-update) | async-done | bytes 1179664 | tf_op jit(solution)/shard_map/all_gather | solution.py:757
  199.1 80.7 %all-gather.14.cloned.1.call-done = bf16[1,768,3072]{2,1,0:T(8,128)(2,1)} async-done(((bf16[1,96,3072]{2,1,0:T(8,128)(2,1)}), bf16[1,768,3072]{2,1,0:T(8,128)(2,1)}) %all-gather.14.cloned.1.call-update) | async-done | bytes 4718608 | tf_op jit(solution)/shard_map/all_gather | solution.py:757
  279.8 80.1 %all-gather.16.cloned.1.call-done = bf16[1,3072,768]{2,1,0:T(8,128)(2,1)} async-done(((bf16[1,384,768]{2,1,0:T(8,128)(2,1)}), bf16[1,3072,768]{2,1,0:T(8,128)(2,1)}) %all-gather.16.cloned.1.call-update) | async-done | bytes 4718608 | tf_op jit(solution)/shard_map/all_gather | solution.py:757
  359.9 36.1 %feed.1 = (bf16[592,768]{1,0:T(8,128)(2,1)}, f32[592,768]{1,0:T(8,128)}, bf16[592,768]{1,0:T(8,128)(2,1)}, bf16[768,768]{1,0:T(8,128)(2,1)}, bf16[768,3072]{1,0:...) custom-call(s32[1]{0:T(128)S(6)} %copy.59.kind_ref, bf16[592,768]{1,0:T(8,128)(2,1)} %bitcast.44, ...), custom_call_target="tpu_custom_call" | custom-call | tf_op jit(solution)/shard_map/feed/pallas_call | solution.py:623
  396.0 0.0 reduce-scatter.7.cloned.1.call-update
  396.0 0.0 reduce-scatter.5.cloned.1.call-start
  396.1 16.5 %attend_back.1 = (bf16[592,768]{1,0:T(8,128)(2,1)}, bf16[592,768]{1,0:T(8,128)(2,1)}, bf16[592,768]{1,0:T(8,128)(2,1)}, bf16[12,592,592]{2,1,0:T(8,128)(2,1)}) custom-call(bf16[592,2304]{1,0:T(8,128)(2,1)} %get-tuple-element.37.q_ref.k_ref.v_ref, bf16[592,2304]{1,0:T(8,128)(2,1)} %get-tuple-element.37.q_ref.k_ref.v_ref, ...), custom_call_target="tpu_custom_call" | custom-call | tf_op jit(solution)/shard_map/attend_back/pallas_call | solution.py:525
  412.6 3.7 pad_maximum_fusion.dt_ref
  416.3 11.1 %finish.1 = (bf16[768,2304]{1,0:T(8,128)(2,1)}, bf16[592,768]{1,0:T(8,128)(2,1)}, f32[16,768]{1,0:T(8,128)}) custom-call(bf16[592,768]{1,0:T(8,128)(2,1)} %bitcast.45, f32[592,768]{1,0:T(8,128)} %get-tuple-element.40.dmid_ref, bf16[592,768]{1,0:T(8,128)(2,1)} %get-tuple-element.41.normed_ref, f32[16,768]{1,0:T(8,128)} %pad_convert_fusion.vec_ref, ...), custom_call_target="tpu_custom_call" | custom-call | tf_op jit(solution)/shard_map/finish/pallas_call | solution.py:703
  427.5 0.0 reduce-scatter.9.cloned.1.call-start
  427.5 0.7 reduce-scatter.9.cloned.1.call-update
  428.2 0.0 reduce-scatter.11.cloned.1.call-start
  428.3 0.7 reduce-scatter.11.cloned.1.call-update
  428.9 0.0 all-reduce.9.cloned.1.call-start
  429.0 22.2 %table_gradient.1 = f32[16,2240]{1,0:T(8,128)} custom-call(s32[1]{0:T(128)S(6)} %copy.59.kind_ref, bf16[12,592,592]{2,1,0:T(8,128)(2,1)} %get-tuple-element.51.ds_ref, s32[1,2432]{1,0:T(1,128)} %reshape.72.lab_ref, bf16[592,224]{1,0:T(8,128)(2,1)} %constant.46.clone.rowsel_ref, bf16[512,592]{1,0:T(8,128)(2,1)} %constant.47.clone.colsel_ref), custom_call_target="tpu_custom_call" | custom-call | tf_op jit(solution)/shard_map/table_gradient/pallas_call | solution.py:350
  451.2 0.0 all-reduce.13.cloned.1.call-start
  451.3 7.2 reduce-scatter.7.cloned.1.call-done
  458.5 81.8 %reduce-scatter.5.cloned.1.call-done = bf16[96,2304]{1,0:T(8,128)(2,1)} async-done(((bf16[768,2304]{1,0:T(8,128)(2,1)}), bf16[96,2304]{1,0:T(8,128)(2,1)}) %reduce-scatter.5.cloned.1.call-update) | async-done | bytes 442384 | tf_op jit(solution)/shard_map/reduce_scatter | solution.py:807
  540.2 98.7 %reduce-scatter.9.cloned.1.call-done = bf16[96,3072]{1,0:T(8,128)(2,1)} async-done(((bf16[768,3072]{1,0:T(8,128)(2,1)}), bf16[96,3072]{1,0:T(8,128)(2,1)}) %reduce-scatter.9.cloned.1.call-update) | async-done | bytes 589840 | tf_op jit(solution)/shard_map/reduce_scatter | solution.py:807
  638.9 98.9 %reduce-scatter.11.cloned.1.call-done = bf16[384,768]{1,0:T(8,128)(2,1)} async-done(((bf16[3072,768]{1,0:T(8,128)(2,1)}), bf16[384,768]{1,0:T(8,128)(2,1)}) %reduce-scatter.11.cloned.1.call-update) | async-done | bytes 589840 | tf_op jit(solution)/shard_map/reduce_scatter | solution.py:807
  737.9 41.1 %all-reduce.3 = (f32[10,768]{1,0:T(8,128)S(1)}, f32[1,3072]{1,0:T(1,128)S(1)}) all-reduce(f32[10,768]{1,0:T(8,128)S(1)} %slice_add_fusion, f32[1,3072]{1,0:T(1,128)S(1)} %copy-done.7), channel_id=1, replica_groups=mesh['rep'=4,'fsdp'=8] {'rep','fsdp'}, use_global_device_ids=true, to_apply=%region_0.1 | all-reduce | flops 10752 | bytes 86016 | tf_op jit(solution)/shard_map/psum | solution.py:811
  779.0 0.6 constant_dynamic-slice_fusion.1
  779.6 0.6 fusion.5
  780.2 84.1 %all-reduce.9.cloned.1.call-done = f32[12,2240]{1,0:T(8,128)} async-done(((f32[12,2240]{1,0:T(8,128)}), f32[12,2240]{1,0:T(8,128)}) %all-reduce.9.cloned.1.call-update) | async-done | bytes 107536 | tf_op jit(solution)/shard_map/psum | solution.py:811
  864.3 0.8 dynamic-slice_bitcast_fusion
  865.1 0.6 copy.50
  865.8 49.8 %all-reduce.13.cloned.1.call-done = (bf16[1,96,2304]{2,1,0:T(8,128)(2,1)}, bf16[1,96,768]{2,1,0:T(8,128)(2,1)}, bf16[1,96,3072]{2,1,0:T(8,128)(2,1)}, bf16[1,384,768]{2,1,0:T(8,128)(2,1)}) async-done(((bf16[1,96,2304]{2,1,0:T(8,128)(2,1)}, bf16[1,96,768]{2,1,0:T(8,128)(2,1)}, bf16[1,96,3072]{2,1,0:T(8,128)(2,1)}, bf16[1,384,768]{2,1,0:T(8,128)(2,1)}), (bf16[1,96,2304]{2,1,0:T(8,128)(2,1)}, ...) | async-done | bytes 1769488 | tf_op jit(solution)/shard_map/psum | solution.py:808
  915.5 2.1 broadcast_in_dim.49
  917.6 1.6 broadcast_in_dim.52
  919.2 1.1 broadcast_in_dim.54
  920.4 1.1 broadcast_in_dim.56
  (38 shorter events, 0.2 us)
Async XLA Ops:
  7.2 14.9 %copy-start = (s32[577,577]{1,0:T(8,128)S(1)}, s32[577,577]{1,0:T(8,128)}, u32[]{:S(2)}) copy-start(s32[577,577]{1,0:T(8,128)} %param.31) | copy-start | bytes 3995152
  7.2 14.8 %copy-start.8 = (s32[2432]{0:T(1024)S(1)}, s32[2432]{0:T(1024)}, u32[]{:S(2)}) copy-start(s32[2432]{0:T(1024)} %constant.50.clone) | copy-start | bytes 29188
  7.2 14.8 %copy-start.9 = (s32[2432]{0:T(1024)S(1)}, s32[2432]{0:T(1024)}, u32[]{:S(2)}) copy-start(s32[2432]{0:T(1024)} %constant.51.clone) | copy-start | bytes 29188
  7.2 14.8 %copy-start.10 = (s32[2432]{0:T(1024)S(1)}, s32[2432]{0:T(1024)}, u32[]{:S(2)}) copy-start(s32[2432]{0:T(1024)} %constant.48.clone) | copy-start | bytes 29188
  7.2 14.8 %copy-start.11 = (s32[2432]{0:T(1024)S(1)}, s32[2432]{0:T(1024)}, u32[]{:S(2)}) copy-start(s32[2432]{0:T(1024)} %constant.49.clone) | copy-start | bytes 29188
  7.3 82.8 %all-reduce.11.cloned.1.call-start = ((), (), s32[]{:S(2)}) async-start(), calls=%async_computation.13 | async-start | bytes 151552
  18.0 0.6 copy-start.4
  18.6 138.7 %all-gather.10.cloned.1.call-start = ((), (), s32[]{:S(2)}) async-start(), calls=%async_computation.9 | async-start | bytes 3981312 | tf_op jit(solution)/shard_map/all_gather | solution.py:757
  19.4 179.7 %all-gather.12.cloned.1.call-start = ((), (), s32[]{:S(2)}) async-start(), calls=%async_computation.10 | async-start | bytes 1327104 | tf_op jit(solution)/shard_map/all_gather | solution.py:757
  20.1 259.7 %all-gather.14.cloned.1.call-start = ((), (), s32[]{:S(2)}) async-start(), calls=%async_computation.11 | async-start | bytes 5308416 | tf_op jit(solution)/shard_map/all_gather | solution.py:757
  20.7 339.2 %all-gather.16.cloned.1.call-start = ((), (), s32[]{:S(2)}) async-start(), calls=%async_computation.12 | async-start | bytes 5308416 | tf_op jit(solution)/shard_map/all_gather | solution.py:757
  21.3 437.2 %reduce-scatter.7.cloned.1.call-start = ((), (), s32[]{:S(2)}) async-start(), calls=%async_computation.6 | async-start | bytes 1327104 | tf_op jit(solution)/shard_map/reduce_scatter | solution.py:807
  22.1 18.9 %copy-start.12 = (pred[2432]{0:T(1024)(128)(4,1)S(1)}, pred[2432]{0:T(1024)(128)(4,1)}, u32[]{:S(2)}) copy-start(pred[2432]{0:T(1024)(128)(4,1)} %constant.52.clone) | copy-start | bytes 7300
  22.1 18.9 %copy-start.13 = (pred[2432]{0:T(1024)(128)(4,1)S(1)}, pred[2432]{0:T(1024)(128)(4,1)}, u32[]{:S(2)}) copy-start(pred[2432]{0:T(1024)(128)(4,1)} %constant.53.clone) | copy-start | bytes 7300
  396.0 144.2 %reduce-scatter.5.cloned.1.call-start = ((), (), s32[]{:S(2)}) async-start(), calls=%async_computation.4 | async-start | bytes 3981312 | tf_op jit(solution)/shard_map/reduce_scatter | solution.py:807
  427.5 211.5 %reduce-scatter.9.cloned.1.call-start = ((), (), s32[]{:S(2)}) async-start(), calls=%async_computation.7 | async-start | bytes 5308416 | tf_op jit(solution)/shard_map/reduce_scatter | solution.py:807
  428.2 309.6 %reduce-scatter.11.cloned.1.call-start = ((), (), s32[]{:S(2)}) async-start(), calls=%async_computation.8 | async-start | bytes 5308416 | tf_op jit(solution)/shard_map/reduce_scatter | solution.py:807
  428.9 435.4 %all-reduce.9.cloned.1.call-start = ((), (), s32[]{:S(2)}) async-start(), calls=%async_computation.5 | async-start | bytes 294912 | tf_op jit(solution)/shard_map/psum | solution.py:811
  451.2 286.6 %copy-start.5 = (f32[16,768]{1,0:T(8,128)S(1)}, f32[16,768]{1,0:T(8,128)}, u32[]{:S(2)}) copy-start(f32[16,768]{1,0:T(8,128)} %get-tuple-element.48) | copy-start | bytes 147460
  451.2 286.6 %copy-start.6 = (f32[16,768]{1,0:T(8,128)S(1)}, f32[16,768]{1,0:T(8,128)}, u32[]{:S(2)}) copy-start(f32[16,768]{1,0:T(8,128)} %get-tuple-element.49) | copy-start | bytes 147460
  451.2 286.7 %copy-start.7 = (f32[1,3072]{1,0:T(1,128)S(1)}, f32[1,3072]{1,0:T(1,128)}, u32[]{:S(2)}) copy-start(f32[1,3072]{1,0:T(1,128)} %get-tuple-element.54) | copy-start | bytes 36868
  451.2 464.3 %all-reduce.13.cloned.1.call-start = ((), (), s32[]{:S(2)}) async-start(), calls=%async_computation.14 | async-start | bytes 3538944 | tf_op jit(solution)/shard_map/psum | solution.py:808
  915.5 3.7 copy-start.3
  915.5 4.8 copy-start.2
  919.2 2.2 copy-start.1
Sparse Core Ops, SparseCore 0:
  18.8 71.2 all-reduce.10
  92.2 65.0 all-gather.9
  159.5 39.5 all-gather.11
  201.1 78.6 all-gather.13
  281.8 78.0 all-gather.15
  396.1 62.2 reduce-scatter.6
  462.1 78.0 reduce-scatter.4
  543.9 94.9 reduce-scatter.8
  642.6 95.1 reduce-scatter.10
  743.8 120.4 all-reduce.8
  866.9 48.5 all-reduce.12

commit v2 on v1

--- a/solution.py
+++ b/solution.py
@@ -28,7 +28,8 @@
 
 
 class Plan:
-    def __init__(self, small_len, large_len, rows):
+    def __init__(self, small_len, large_len, rows, heads):
+        self.heads = heads
         self.rows = rows
         self.small_len, self.large_len = small_len, large_len
         self.gs = int(round((small_len - 1) ** 0.5))
@@ -86,13 +87,44 @@
         return jnp.asarray(rows, bf16), jnp.asarray(cols, bf16)
 
 
-def table_labels(plan, large_index, kind):
-    (lr, lc, lg), (sr, sc, sg) = plan.positions()
-    is_large = kind == 1
-    row = jnp.where(is_large, jnp.asarray(lr, jnp.int32), jnp.asarray(sr, jnp.int32))
-    col = jnp.where(is_large, jnp.asarray(lc, jnp.int32), jnp.asarray(sc, jnp.int32))
-    good = jnp.where(is_large, jnp.asarray(lg), jnp.asarray(sg))
-    return jnp.where(good, large_index[row, col], -1).reshape(1, plan.lanes)
+def pick_plan(plan):
+    out = []
+    for r, c, good in plan.positions():
+        down = r > c
+        down = np.where(good, (r - 1) // plan.gl >= (c - 1) // plan.gl, False)
+        key = np.where(down, r, c)
+        sub = np.where(down, c, r) - 1
+        valid = good.copy()
+        valid[plan.line :] = False
+        out.append(np.stack([key, sub, down.astype(int), valid.astype(int)]))
+    return jnp.asarray(np.concatenate(out), jnp.int32)
+
+
+def read_labels(plan, is_large, idx_ref, pick_ref, lab_ref):
+    size, gl = idx_ref.shape[0], plan.gl
+    across = idx_ref[1 : 1 + gl, :]
+    down = idx_ref[:, 1 : 1 + gl]
+    digits = lambda v: [(v >> 6).astype(f32).astype(bf16), (v & 63).astype(f32).astype(bf16)]
+    across, down = digits(across), digits(down)
+    for chunk in range(plan.line // 128):
+        lanes = slice(chunk * 128, (chunk + 1) * 128)
+        key, sub, use_down, valid = [
+            jnp.where(is_large, pick_ref[i : i + 1, lanes], pick_ref[4 + i : 5 + i, lanes])
+            for i in range(4)
+        ]
+        hot = jnp.where(iota((size, 128), 0) == key, 1.0, 0.0).astype(bf16)
+        here = iota((gl, 128), 0) == sub
+        found = []
+        for digit in range(2):
+            rows = jnp.where(use_down == 1, mm(down[digit], hot, TN), mm(across[digit], hot))
+            found.append(jnp.sum(jnp.where(here, rows, 0.0), axis=0, keepdims=True))
+        label = (found[0] * 64.0 + found[1]).astype(jnp.int32)
+        lab_ref[:, lanes] = jnp.where(valid == 1, label, -1)
+    lane = iota((1, 128), 1)
+    tail = jnp.where(lane == 0, idx_ref[0:1, 1:2], -1)
+    tail = jnp.where(lane == 1, idx_ref[1:2, 0:1], tail)
+    tail = jnp.where(lane == 2, idx_ref[0:1, 0:1], tail)
+    lab_ref[:, plan.line : plan.line + 128] = tail
 
 
 def iota(shape, dim):
@@ -180,11 +212,14 @@
     out_ref[0] = jnp.where(same, full, neg_fill).astype(bf16)
 
 
-def bias_kernel(plan, kind_ref, lab_ref, tab_ref, rowsel_ref, colsel_ref, out_ref, line_ref):
+def bias_kernel(
+    plan, kind_ref, idx_ref, pick_ref, tab_ref, rowsel_ref, colsel_ref, out_ref, lab_ref, line_ref
+):
     h = pl.program_id(0)
 
     @pl.when(h == 0)
     def _():
+        read_labels(plan, kind_ref[0] == 1, idx_ref, pick_ref, lab_ref)
         for chunk in range(plan.lanes // 128):
             part = mm(tab_ref[...], one_hot(lab_ref, chunk, tab_ref.shape[1]))
             for i in range(line_ref.shape[0]):
@@ -208,26 +243,31 @@
 params = pltpu.CompilerParams(vmem_limit_bytes=vmem_bytes)
 
 
-def pair_bias(plan, kind, labels, table, rowsel, colsel):
+def pair_bias(plan, kind, large_index, table, rowsel, colsel):
     heads, buckets = table.shape
-    table = jnp.pad(table, ((0, 16 - heads), (0, 0)))
+    heads = plan.heads
     rows = plan.rows
+    picks = pick_plan(plan)
     return pl.pallas_call(
         functools.partial(bias_kernel, plan),
         grid=(heads,),
         in_specs=[
             smem_spec,
-            whole(labels.shape),
+            whole(large_index.shape),
+            whole(picks.shape),
             whole(table.shape),
             whole(rowsel.shape),
             whole(colsel.shape),
         ],
-        out_specs=pl.BlockSpec((1, rows, rows), lambda i: (i, 0, 0)),
-        out_shape=jax.ShapeDtypeStruct((heads, rows, rows), bf16),
+        out_specs=[pl.BlockSpec((1, rows, rows), lambda i: (i, 0, 0)), whole((1, plan.lanes))],
+        out_shape=[
+            jax.ShapeDtypeStruct((heads, rows, rows), bf16),
+            jax.ShapeDtypeStruct((1, plan.lanes), jnp.int32),
+        ],
         scratch_shapes=[pltpu.VMEM((16, 1, plan.lanes), f32)],
         compiler_params=params,
         name="pair_bias",
-    )(kind, labels, table, rowsel, colsel)
+    )(kind, large_index, picks, table, rowsel, colsel)
 
 
 def fold_large(plan, ds_ref, h, line_ref):
@@ -668,7 +708,18 @@
 
 
 def finish_kernel(
-    tok_ref, dmid_ref, normed_ref, vec_ref, dt_ref, w_ref, dw_ref, out_ref, small_ref, acc_ref
+    tok_ref,
+    dmid_ref,
+    normed_ref,
+    vec_ref,
+    dq_ref,
+    dk_ref,
+    dv_ref,
+    w_ref,
+    dw_ref,
+    out_ref,
+    small_ref,
+    acc_ref,
 ):
     part = pl.program_id(0)
 
@@ -677,7 +728,7 @@
         acc_ref[...] = jnp.zeros_like(acc_ref)
         small_ref[...] = jnp.zeros_like(small_ref)
 
-    d_part = dt_ref[0]
+    d_part = jnp.where(part == 0, dq_ref[...], jnp.where(part == 1, dk_ref[...], dv_ref[...]))
     dw_ref[...] = mm(normed_ref[...], d_part, TN).astype(bf16)
     acc_ref[...] += mm(d_part, w_ref[...], NT)
     sums = rows_sum(d_part.astype(f32))
@@ -708,7 +759,9 @@
             whole(d_middle.shape),
             whole(normed.shape),
             whole(vecs.shape),
-            pl.BlockSpec((1, rows, width), lambda i: (i, 0, 0)),
+            whole(tokens.shape),
+            whole(tokens.shape),
+            whole(tokens.shape),
             pl.BlockSpec((width, width), lambda i: (0, i)),
         ],
         out_specs=[
@@ -724,7 +777,448 @@
         scratch_shapes=[pltpu.VMEM((rows, width), f32)],
         compiler_params=params,
         name="finish",
-    )(tokens, d_middle, normed, vecs, d_triple, weight)
+    )(tokens, d_middle, normed, vecs, *d_triple, weight)
+
+
+class Spot:
+    def __init__(self, n):
+        self.n, self.levels = n, n // 2
+        self.rep, self.f = lax.axis_index("rep"), lax.axis_index("fsdp")
+        self.half, self.core = self.rep // 2, self.rep % 2
+        self.level, self.side = self.f // 2, self.f % 2
+
+    def at(self, rep=None, f=None):
+        return {"rep": self.rep if rep is None else rep, "fsdp": self.f if f is None else f}
+
+    def sibling(self):
+        return self.at(rep=2 * self.half + 1 - self.core)
+
+    def across(self):
+        return self.at(rep=2 * (1 - self.half) + self.core)
+
+    def beside(self):
+        return self.at(f=2 * self.level + 1 - self.side)
+
+    def along(self, step):
+        return self.at(f=2 * ((self.level + step) % self.levels) + self.side)
+
+    def from_along(self, step, side=None):
+        side = self.side if side is None else side
+        return 2 * ((self.level + self.levels - step) % self.levels) + side
+
+
+MESH = pl.DeviceIdType.MESH
+
+
+def greet(devices, count):
+    barrier = pltpu.get_barrier_semaphore()
+    for device in devices:
+        pl.semaphore_signal(barrier, inc=1, device_id=device, device_id_type=MESH)
+    pl.semaphore_wait(barrier, count)
+
+
+def send(src, dst, send_sem, recv_sem, device):
+    return pltpu.make_async_remote_copy(
+        src_ref=src,
+        dst_ref=dst,
+        send_sem=send_sem,
+        recv_sem=recv_sem,
+        device_id=device,
+        device_id_type=MESH,
+    )
+
+
+def fast_shape(reps, n, shard_rows):
+    return reps == 4 and n % 2 == 0 and n > 2 and all(rows % 96 == 0 for rows in shard_rows)
+
+
+class Gather:
+    def __init__(self, spot, shard, whole_ref, send_sems, recv_sems, local_sem):
+        self.spot, self.shard, self.whole = spot, shard, whole_ref
+        self.ss, self.rs = send_sems, recv_sems
+        self.part = shard.shape[0] // 2
+        self.third = self.part // 3
+        base = spot.core * self.part
+        self.plane = pl.ds(base + spot.half * self.third, 2 * self.third)
+        self.mine = pl.ds(base + spot.half * 2 * self.third, self.third)
+        self.core_rows = pl.ds(base, self.part)
+        self.local = pltpu.make_async_copy(shard, whole_ref.at[spot.f], local_sem)
+        levels = spot.levels
+        self.zs, self.ys, self.xs, self.cs = [], [], [], []
+        idx = 0
+        for step in range(1, levels):
+            self.zs.append(self.copy(shard.at[self.plane], self.plane, spot.f, idx, spot.along(step)))
+            idx += 1
+        for step in range(levels):
+            f = spot.from_along(step)
+            src = shard.at[self.plane] if step == 0 else whole_ref.at[f, self.plane]
+            self.ys.append(self.copy(src, self.plane, f, idx, spot.beside()))
+            idx += 1
+        arrivals = [spot.from_along(step) for step in range(1, levels)]
+        arrivals += [spot.from_along(step, 1 - spot.side) for step in range(levels)]
+        for f in arrivals:
+            self.xs.append(self.copy(whole_ref.at[f, self.mine], self.mine, f, idx, spot.across()))
+            idx += 1
+        for f in arrivals:
+            rows = self.core_rows
+            self.cs.append(self.copy(whole_ref.at[f, rows], rows, f, idx, spot.sibling()))
+            idx += 1
+
+    @staticmethod
+    def count(n):
+        return n // 2 - 1 + n // 2 + 2 * (n - 1)
+
+    def copy(self, src, rows, f, idx, device):
+        return send(src, self.whole.at[f, rows], self.ss.at[idx], self.rs.at[idx], device)
+
+    def start(self):
+        self.local.start()
+        for copy in self.zs:
+            copy.start()
+        self.ys[0].start()
+
+    def step_z(self, k):
+        self.zs[k].wait_recv()
+        self.ys[k + 1].start()
+        self.xs[k].start()
+
+    def step_y(self, k):
+        self.ys[k].wait_recv()
+        self.xs[len(self.zs) + k].start()
+
+    def step_x(self, k):
+        self.xs[k].wait_recv()
+        self.cs[k].start()
+
+    def step_c(self, k):
+        self.cs[k].wait_recv()
+
+    def finish(self):
+        self.local.wait()
+        for copy in self.zs + self.ys + self.xs + self.cs:
+            copy.wait_send()
+
+
+def spread_block(refs, block_ref):
+    *vectors, be_ref, table_ref = refs
+    share, heads = table_ref.shape
+    eye = jnp.where(iota((16, heads), 0) == iota((16, heads), 1), 1.0, 0.0).astype(bf16)
+    lanes = block_ref.shape[1]
+    table = mm(eye, table_ref[...], NT)
+    width = vectors[0].shape[1]
+    rows = [v[...].astype(f32) for v in vectors]
+    rows.append(jnp.zeros((16 - len(rows), width), f32))
+    block = jnp.concatenate(
+        [table, jnp.zeros((16, lanes - share - width), f32), jnp.concatenate(rows, axis=0)], axis=1
+    )
+    wide = jnp.broadcast_to(be_ref[...].astype(f32), (16, lanes))
+    block_ref[...] = jnp.where(iota((16, lanes), 0) == heads, wide, block).astype(bf16)
+
+
+def gather_kernel(n, heads, *refs):
+    shorts, (wt, wo, we, wr), outs = refs[:12], refs[12:16], refs[16:23]
+    wholes, (vec_ref, be_ref, tab_ref) = outs[:4], outs[4:]
+    block, blocks, ss, rs, local, bss, brs = refs[23:]
+    spot = Spot(n)
+    peers = [spot.at(f=(spot.f + k) % n) for k in range(1, n)]
+    greet(peers + [spot.sibling(), spot.across()], n + 1)
+    spread_block(shorts, block)
+    small = []
+    for k, peer in enumerate(peers):
+        small.append(send(block, blocks.at[spot.f], bss.at[k], brs.at[k], peer))
+        small[k].start()
+    blocks[spot.f] = block[...]
+    jobs = []
+    for i, (shard, out) in enumerate(zip((wt, wo, we, wr), wholes)):
+        jobs.append(Gather(spot, shard, out, ss.at[i], rs.at[i], local.at[i]))
+    for job in jobs:
+        job.start()
+    for job in jobs:
+        for k in range(len(job.zs)):
+            job.step_z(k)
+        for k in range(len(job.ys)):
+            job.step_y(k)
+    for job in jobs:
+        for k in range(len(job.xs)):
+            job.step_x(k)
+    for copy in small:
+        copy.wait()
+    share = shorts[0].shape[1]
+    bshare = shorts[11].shape[0]
+    for f in range(n):
+        part = blocks[f].astype(f32)
+        wide = part.shape[1]
+        vec_ref[:, f * share : (f + 1) * share] = part[:, wide - share :]
+        tab_ref[:, f * bshare : (f + 1) * bshare] = part[:, :bshare]
+        be_ref[:, f * wide : (f + 1) * wide] = part[heads : heads + 1, :]
+    for job in jobs:
+        for k in range(len(job.cs)):
+            job.step_c(k)
+    for job in jobs:
+        job.finish()
+
+
+any_spec = pl.BlockSpec(memory_space=pl.ANY)
+vmem_spec = pl.BlockSpec(memory_space=pltpu.VMEM)
+
+
+def gather_all(shorts, shards, n):
+    sds = jax.ShapeDtypeStruct
+    share, wide = shorts[0].shape[1], shorts[10].shape[1]
+    bshare, heads = shorts[11].shape
+    count = Gather.count(n)
+    outs = pl.pallas_call(
+        functools.partial(gather_kernel, n, heads),
+        in_specs=[vmem_spec] * 12 + [any_spec] * 4,
+        out_specs=[any_spec] * 4 + [vmem_spec] * 3,
+        out_shape=[sds((n,) + w.shape, bf16) for w in shards]
+        + [sds((16, n * share), f32), sds((1, n * wide), f32), sds((16, n * bshare), f32)],
+        scratch_shapes=[
+            pltpu.VMEM((16, wide), bf16),
+            pltpu.VMEM((n, 16, wide), bf16),
+            pltpu.SemaphoreType.DMA((4, count)),
+            pltpu.SemaphoreType.DMA((4, count)),
+            pltpu.SemaphoreType.DMA((4,)),
+            pltpu.SemaphoreType.DMA((n - 1,)),
+            pltpu.SemaphoreType.DMA((n - 1,)),
+        ],
+        compiler_params=pltpu.CompilerParams(
+            collective_id=1, has_side_effects=True, vmem_limit_bytes=vmem_bytes
+        ),
+        name="gather_all",
+    )(*shorts, *shards)
+    wholes = [w.reshape(-1, w.shape[2]) for w in outs[:4]]
+    return wholes, outs[4], outs[5], outs[6].astype(bf16)
+
+
+class Reduce:
+    def __init__(self, spot, grad, out, bufs, send_sems, recv_sems, local_sem):
+        self.spot, self.out, self.bufs = spot, out, bufs
+        own, got_c, got_x, got_y, got_z, total, got_f = bufs
+        self.part = part = own.shape[2]
+        self.third = q = part // 3
+        half, core, side, level, levels = spot.half, spot.core, spot.side, spot.level, spot.levels
+        rows = lambda start, size: pl.ds(pl.multiple_of(start, 16), size)
+        self.plane = rows(half * q, 2 * q)
+        self.mine = rows(half * 2 * q, q)
+        self.core_rows = rows(core * part, part)
+
+        def copy(idx, src, dst, device):
+            return send(src, dst, send_sems.at[idx], recv_sems.at[idx], device)
+
+        self.load = pltpu.make_async_copy(grad.at[:, :, self.core_rows], own, local_sem)
+        other = rows((1 - core) * part, part)
+        self.c = copy(0, grad.at[:, :, other], got_c, spot.sibling())
+        self.x = copy(1, own.at[:, :, rows((1 - half) * 2 * q, q)], got_x, spot.across())
+        self.y = copy(2, own.at[:, 1 - side, self.plane], got_y, spot.beside())
+        self.z = []
+        for step in range(1, levels):
+            src = own.at[(level + step) % levels, side, self.plane]
+            self.z.append(copy(4 + step, src, got_z.at[step - 1], spot.along(step)))
+        self.f = copy(3, total, got_f, spot.across())
+        self.last = copy(4, out.at[self.core_rows], out.at[self.core_rows], spot.sibling())
+
+    @staticmethod
+    def count(n):
+        return 4 + n // 2
+
+    @staticmethod
+    def buffers(n, shard_rows, cols):
+        part, levels = shard_rows // 2, n // 2
+        q = part // 3
+        shapes = [
+            (levels, 2, part, cols),
+            (levels, 2, part, cols),
+            (levels, 2, q, cols),
+            (levels, 2 * q, cols),
+            (levels - 1, 2 * q, cols),
+            (2 * q, cols),
+            (2 * q, cols),
+        ]
+        return [pltpu.VMEM(shape, bf16) for shape in shapes]
+
+    def start(self):
+        self.load.start()
+        self.c.start()
+
+    def step_c(self):
+        own, got = self.bufs[0], self.bufs[1]
+        self.load.wait()
+        self.c.wait_recv()
+
+        @pl.loop(0, own.shape[0])
+        def _(level):
+            for side in range(2):
+                own[level, side] = add16(own[level, side], got[level, side])
+
+        self.x.start()
+
+    def step_x(self):
+        own, got = self.bufs[0], self.bufs[2]
+        self.x.wait_recv()
+
+        @pl.loop(0, own.shape[0])
+        def _(level):
+            for side in range(2):
+                own[level, side, self.mine] = add16(own[level, side, self.mine], got[level, side])
+
+        self.y.start()
+
+    def step_y(self):
+        own, got = self.bufs[0], self.bufs[3]
+        side = self.spot.side
+        self.y.wait_recv()
+
+        @pl.loop(0, own.shape[0])
+        def _(level):
+            own[level, side, self.plane] = add16(own[level, side, self.plane], got[level])
+
+        for copy in self.z:
+            copy.start()
+
+    def step_z(self):
+        own, got, total = self.bufs[0], self.bufs[4], self.bufs[5]
+        for copy in self.z:
+            copy.wait_recv()
+        value = own[self.spot.level, self.spot.side, self.plane].astype(f32)
+        for k in range(len(self.z)):
+            value = value + got[k].astype(f32)
+        total[...] = value.astype(bf16)
+        self.f.start()
+
+    def step_f(self):
+        total, got, out = self.bufs[5], self.bufs[6], self.out
+        q, half = self.third, self.spot.half
+        base = self.spot.core * self.part
+        rows = lambda start: pl.ds(pl.multiple_of(start, 16), q)
+        self.f.wait_recv()
+        out[rows(base + half * 2 * q)] = total[rows(half * q)]
+        out[rows(base + q)] = add16(total[rows((1 - half) * q)], got[rows(half * q)])
+        out[rows(base + (1 - half) * 2 * q)] = got[rows((1 - half) * q)]
+        self.last.start()
+
+    def finish(self):
+        self.last.wait_recv()
+        for copy in [self.c, self.x, self.y, self.f, self.last] + self.z:
+            copy.wait_send()
+
+
+def add16(left, right):
+    return (left.astype(f32) + right.astype(f32)).astype(bf16)
+
+
+def reduce_kernel(n, *refs):
+    grads, (vec_ref, be_ref, tab_ref) = refs[:4], refs[4:7]
+    outs, small_out = refs[7:11], refs[11]
+    bufs = [refs[12 + 7 * i : 19 + 7 * i] for i in range(4)]
+    block, got, reps, ss, rs, local, bss, brs = refs[40:]
+    spot = Spot(n)
+    peers = [spot.at(f=(spot.f + k) % n) for k in range(1, n)]
+    others = [spot.at(rep=(spot.rep + k) % 4) for k in range(1, 4)]
+    greet(peers + others, n + 2)
+    jobs = []
+    for i in range(4):
+        jobs.append(Reduce(spot, grads[i], outs[i], bufs[i], ss.at[i], rs.at[i], local.at[i]))
+    for job in jobs:
+        job.start()
+    share, bshare = vec_ref.shape[1] // n, tab_ref.shape[1] // n
+    wide = be_ref.shape[1] // n
+    heads = 12
+    for f in range(n):
+        value = jnp.concatenate(
+            [
+                tab_ref[:, f * bshare : (f + 1) * bshare],
+                jnp.zeros((16, wide - bshare - share), f32),
+                vec_ref[:, f * share : (f + 1) * share],
+            ],
+            axis=1,
+        )
+        bias = jnp.broadcast_to(be_ref[:, f * wide : (f + 1) * wide], (16, wide))
+        block[f] = jnp.where(iota((16, wide), 0) == heads, bias, value)
+    small = []
+    for k, peer in enumerate(peers):
+        dst = (spot.f + k + 1) % n
+        small.append(send(block.at[dst], got.at[k], bss.at[k], brs.at[k], peer))
+        small[k].start()
+    steps = ["step_c", "step_x", "step_y", "step_z", "step_f", "finish"]
+    second = []
+    for slot in range(len(jobs) + len(steps) - 1):
+        for i, job in enumerate(jobs):
+            if 0 <= slot - i < len(steps):
+                getattr(job, steps[slot - i])()
+        if slot == 1:
+            value = block[spot.f]
+            for k, copy in enumerate(small):
+                copy.wait_recv()
+                value = value + got[k]
+            reps[spot.rep] = value
+            for k, other in enumerate(others):
+                mine = reps.at[spot.rep]
+                second.append(send(mine, mine, bss.at[n - 1 + k], brs.at[n - 1 + k], other))
+                second[k].start()
+        if slot == 3:
+            for copy in second:
+                copy.wait_recv()
+            small_out[...] = (reps[0] + reps[1]) + (reps[2] + reps[3])
+    for copy in small + second:
+        copy.wait_send()
+
+
+def reduce_all(grads, vec_sums, be_sums, table_sums, n):
+    sds = jax.ShapeDtypeStruct
+    grads = [g.reshape(n // 2, 2, g.shape[0] // n, g.shape[1]) for g in grads]
+    wide = be_sums.shape[1] // n
+    scratch = []
+    for g in grads:
+        scratch += Reduce.buffers(n, g.shape[2], g.shape[3])
+    count = Reduce.count(n)
+    outs = pl.pallas_call(
+        functools.partial(reduce_kernel, n),
+        in_specs=[any_spec] * 4 + [vmem_spec] * 3,
+        out_specs=[vmem_spec] * 5,
+        out_shape=[sds(g.shape[2:], bf16) for g in grads] + [sds((16, wide), f32)],
+        scratch_shapes=scratch
+        + [
+            pltpu.VMEM((n, 16, wide), f32),
+            pltpu.VMEM((n - 1, 16, wide), f32),
+            pltpu.VMEM((4, 16, wide), f32),
+            pltpu.SemaphoreType.DMA((4, count)),
+            pltpu.SemaphoreType.DMA((4, count)),
+            pltpu.SemaphoreType.DMA((4,)),
+            pltpu.SemaphoreType.DMA((n + 2,)),
+            pltpu.SemaphoreType.DMA((n + 2,)),
+        ],
+        compiler_params=pltpu.CompilerParams(
+            collective_id=2, has_side_effects=True, vmem_limit_bytes=vmem_bytes
+        ),
+        name="reduce_all",
+    )(*grads, vec_sums, be_sums, table_sums)
+    return outs[:4], outs[4]
+
+
+def gather_plain(shorts, shards, n):
+    gather = lambda value, axis: lax.all_gather(value, "fsdp", axis=axis, tiled=True)
+    vecs = gather(jnp.concatenate(shorts[:10], axis=0), 1).astype(f32)
+    vecs = jnp.pad(vecs, ((0, 6), (0, 0)))
+    table = gather(shorts[11], 0).T
+    table = jnp.pad(table, ((0, 16 - table.shape[0]), (0, 0)))
+    return [gather(w, 0) for w in shards], vecs, gather(shorts[10], 1).astype(f32), table
+
+
+def reduce_plain(grads, vec_sums, be_sums, table_sums, n):
+    def whole_sum(value):
+        value = lax.psum_scatter(value, "fsdp", scatter_dimension=0, tiled=True)
+        return lax.psum(value, "rep")
+
+    sums = lax.psum((vec_sums, be_sums, table_sums), ("rep", "fsdp"))
+    me = lax.axis_index("fsdp")
+    cut = lambda v: lax.dynamic_slice_in_dim(v, me * (v.shape[1] // n), v.shape[1] // n, axis=1)
+    vec_part, be_part, table_part = [cut(v) for v in sums]
+    wide = be_part.shape[1]
+    space = max(wide - vec_part.shape[1] - table_part.shape[1], 0)
+    body = jnp.concatenate([table_part, jnp.zeros((16, space), f32), vec_part], axis=1)
+    block = jnp.where(jnp.arange(16)[:, None] == 12, jnp.pad(be_part, ((0, 0), (0, body.shape[1] - wide))), body)
+    return [whole_sum(g) for g in grads], block
 
 
 def per_device(
@@ -752,10 +1246,8 @@
 ):
     _, rows, width = tokens.shape
     heads = bias_table.shape[2]
-    plan = Plan(small_index.shape[0], large_index.shape[0], rows)
+    plan = Plan(small_index.shape[0], large_index.shape[0], rows, heads)
     tokens, cotangent = tokens[0], cotangent[0]
-    gather = lambda value: lax.all_gather(value, "fsdp", axis=0, tiled=True)
-
     short = [
         first_gain,
         first_shift,
@@ -768,29 +1260,16 @@
         reduce_bias,
         feed_scale,
     ]
-    share = first_gain.shape[1]
-    wide_share = expand_bias.shape[1]
-    bucket_share = bias_table.shape[1]
-    packed = jnp.concatenate(
-        [v[0] for v in short] + [expand_bias[0], bias_table[0].T.reshape(-1)], axis=0
+    n = width // first_gain.shape[1]
+    fast = fast_shape(
+        lax.axis_size("rep"), n, [w.shape[1] for w in (triple_weight, output_weight, reduce_weight)]
     )
-    packed = lax.all_gather(packed, "fsdp", axis=0, tiled=False)
-    n = packed.shape[0]
-    cut = len(short) * share
-    vecs = packed[:, :cut].reshape(n, len(short), share).transpose(1, 0, 2)
-    vecs = jnp.pad(vecs.reshape(len(short), width).astype(f32), ((0, 16 - len(short)), (0, 0)))
-    be = packed[:, cut : cut + wide_share].reshape(1, n * wide_share).astype(f32)
-    table = packed[:, cut + wide_share :].reshape(n, heads, bucket_share).transpose(1, 0, 2)
-    table = table.reshape(heads, n * bucket_share)
-
-    wt = gather(triple_weight[0])
-    wo = gather(output_weight[0])
-    we = gather(expand_weight[0])
-    wr = gather(reduce_weight[0])
+    gathered = gather_all if fast else gather_plain
+    shards = [w[0] for w in (triple_weight, output_weight, expand_weight, reduce_weight)]
+    (wt, wo, we, wr), vecs, be, table = gathered(short + [expand_bias, bias_table[0]], shards, n)
 
     rowsel, colsel = plan.selectors()
-    labels = table_labels(plan, large_index, slot_kinds[0])
-    bias = pair_bias(plan, slot_kinds, labels, table, rowsel, colsel)
+    bias, labels = pair_bias(plan, slot_kinds, large_index, table, rowsel, colsel)
 
     normed, triple = project(tokens, vecs, wt)
     mixed, probs = attend(triple, bias)
@@ -800,38 +1279,31 @@
     dq, dk, dv, d_scores = attend_back(triple, d_mixed, mixed, probs)
     d_table = table_gradient(plan, slot_kinds, d_scores, labels, rowsel, colsel, table.shape[1])
     dwt, token_grad, small_b = finish(
-        tokens, d_middle, normed, vecs, jnp.stack([dq, dk, dv]), wt
+        tokens, d_middle, normed, vecs, (dq, dk, dv), wt
     )
 
-    def reduce_weight_part(value):
-        value = lax.psum_scatter(value, "fsdp", scatter_dimension=0, tiled=True)
-        return lax.psum(value, "rep").astype(f32)[None]
-
-    smalls = (small_a + small_b)[: len(short)]
-    smalls = lax.psum((smalls, dbe, d_table[:heads]), ("rep", "fsdp"))
-    me = lax.axis_index("fsdp")
-    cut_of = lambda value, size: lax.dynamic_slice_in_dim(value, me * size, size, axis=1)
-    small = cut_of(smalls[0], share)
-    d_be = cut_of(smalls[1], wide_share)
-    d_tab = cut_of(smalls[2], bucket_share).T[None]
-    row = lambda idx: small[idx : idx + 1]
+    reduced = reduce_all if fast else reduce_plain
+    (dwr, dwe, dwo, dwt), block = reduced((dwr, dwe, dwo, dwt), small_a + small_b, dbe, d_table, n)
+    share, bshare = first_gain.shape[1], bias_table.shape[1]
+    row = lambda idx: block[idx : idx + 1, block.shape[1] - share :]
+    full = lambda value: value.astype(f32)[None]
     return (
         block_output[None],
         token_grad[None],
         row(FIRST_GAIN),
         row(FIRST_SHIFT),
-        reduce_weight_part(dwt),
+        full(dwt),
         row(QUERY_BIAS),
         row(VALUE_BIAS),
-        d_tab,
-        reduce_weight_part(dwo),
+        block[:heads, :bshare].T[None],
+        full(dwo),
         row(OUTPUT_BIAS),
         row(ATTEND_SCALE),
         row(SECOND_GAIN),
         row(SECOND_SHIFT),
-        reduce_weight_part(dwe),
-        d_be,
-        reduce_weight_part(dwr),
+        full(dwe),
+        block[heads : heads + 1],
+        full(dwr),
         row(REDUCE_BIAS),
         row(FEED_SCALE),
     )

time: 929 us -> 353 us (0.38)
  waiting for transfers between devices: 704 us -> 0 us
  Pallas kernels: 121 us -> 331 us
  blocking collectives: 41.1 us -> 0 us
  local copies, waits for them, and re-layouts: 35 us -> 5.75 us
  between operations: 15.5 us -> 1.35 us
    reduce_scatter x4 -> x0, waiting for transfers between devices: 287 us -> none  [reduce_weight_part(): value = lax.psum_scatter(value, 'fsdp', scatter_dimension=0, tiled=True)]
    all_gather x4 -> x0, waiting for transfers between devices: 232 us -> none  [per_device(): gather = lambda value: lax.all_gather(value, 'fsdp', axis=0, tiled=True)]
    pallas_call x0 -> x2, Pallas kernels: none -> 208 us  [the longest x1 123 us: reduce_all(): pl.pallas_call(functools.partial(reduce_kernel, n), in_specs=[any_spec] *...]
    psum x2 -> x0, waiting for transfers between devices: 134 us -> none  [the longest x1 84.1 us: per_device(): smalls = lax.psum((smalls, dbe, d_table[:heads]), ('rep', 'fsdp'))]
    unnamed x12 -> x0, waiting for transfers between devices: 52.4 us -> none
    psum x1 -> x0, blocking collectives: 41.1 us -> none  [per_device(): smalls = lax.psum((smalls, dbe, d_table[:heads]), ('rep', 'fsdp'))]
    gather x1 -> x0, local copies, waits for them, and re-layouts: 18.8 us -> none  [table_labels(): return jnp.where(good, large_index[row, col], -1).reshape(1, plan.lanes)]
  transfers between devices with their start and end apart: 11 -> 0, of which waited for: 11 -> 0; matrix products, arithmetic and copies ran while one was open for 3% -> 0% of each run, Pallas kernels for 9% -> 0%
where the time goes in v2:
time: 353 us; the launch traced here: 348 us
  Pallas kernels  331 us (94%)
  other arithmetic  9.87 us (3%)
  local copies, waits for them, and re-layouts  5.75 us (2%)
    pallas_call x1, Pallas kernels, reduce_all(): pl.pallas_call(functools.partial(reduce_kernel, n), in_specs=[any_spec] *...  123 us
    pallas_call x1, Pallas kernels, gather_all(): pl.pallas_call(functools.partial(gather_kernel, n, heads), in_specs=[vmem...  84.8 us
    pallas_call x1, Pallas kernels, feed(): pl.pallas_call(functools.partial(feed_kernel, plan), grid=(hidden // tile...  36.3 us
    pallas_call x1, Pallas kernels, table_gradient(): pl.pallas_call(functools.partial(fold_kernel, plan), grid=(heads,), in_sp...  21.9 us
    pallas_call x1, Pallas kernels, attend_back(): pl.pallas_call(attend_back_kernel, grid=(pairs,), in_specs=[cols(0), cols...  16.3 us
    pallas_call x1, Pallas kernels, pair_bias(): pl.pallas_call(functools.partial(bias_kernel, plan), grid=(heads,), in_sp...  15.4 us
    pallas_call x1, Pallas kernels, attend(): pl.pallas_call(attend_kernel, grid=(pairs,), in_specs=[cols(0), cols(1),...  14.8 us
    pallas_call x1, Pallas kernels, finish(): pl.pallas_call(finish_kernel, grid=(3,), in_specs=[whole(tokens.shape), w...  11.8 us

profile of v2, /device:TPU:0, one launch (start us, length us, event | category | flops | bytes accessed | tf_op | source)
XLA Modules:
  0.0 348.0 jit_solution(7514767734809755022)
XLA Ops:
  1.3 1.5 copy.41
  2.8 84.8 %gather_all.1 = (bf16[8,96,2304]{2,1,0:T(8,128)(2,1)}, bf16[8,96,768]{2,1,0:T(8,128)(2,1)}, bf16[8,96,3072]{2,1,0:T(8,128)(2,1)}, bf16[8,384,768]{2,1,0:T(8,128)...) custom-call(bf16[1,96]{1,0:T(2,128)(2,1)} %refs_0_.1, bf16[1,96]{1,0:T(2,128)(2,1)} %refs_1_.1, ...), custom_call_target="tpu_custom_call" | custom-call | tf_op jit(solution)/shard_map/gather_all/pallas_call | solution.py:970
  87.6 1.6 convert_element_type.2.tab_ref
  89.2 6.6 %project.1 = (bf16[592,768]{1,0:T(8,128)(2,1)}, bf16[592,2304]{1,0:T(8,128)(2,1)}) custom-call(bf16[592,768]{1,0:T(8,128)(2,1)} %bitcast.35, f32[16,768]{1,0:T(8,128)} %get-tuple-element.51.vec_ref, bf16[768,2304]{1,0:T(8,128)(2,1)} %bitcast.33), custom_call_target="tpu_custom_call" | custom-call | tf_op jit(solution)/shard_map/project/pallas_call | solution.py:480
  95.7 15.4 %pair_bias.1 = (bf16[12,592,592]{2,1,0:T(8,128)(2,1)}, s32[1,2432]{1,0:T(1,128)}) custom-call(s32[1]{0:T(128)S(6)} %copy.43.kind_ref, s32[577,577]{1,0:T(8,128)} %idx_ref.1, s32[8,2432]{1,0:T(8,128)} %constant.8.clone.pick_ref, bf16[16,2240]{1,0:T(8,128)(2,1)} %convert_element_type.2.tab_ref, bf16[592,224]{1,0:T(8,128)(2,1)} %constant.6.clone.rowsel_ref, ...), custom_call_target="tpu_custom_call" | custom-call | tf_op jit(solution)/shard_map/pair_bias/pallas_call | solution.py:251
  111.1 14.8 %attend.1 = (bf16[592,768]{1,0:T(8,128)(2,1)}, bf16[12,592,592]{2,1,0:T(8,128)(2,1)}) custom-call(bf16[592,2304]{1,0:T(8,128)(2,1)} %get-tuple-element.53.q_ref.k_ref.v_ref, bf16[592,2304]{1,0:T(8,128)(2,1)} %get-tuple-element.53.q_ref.k_ref.v_ref, bf16[592,2304]{1,0:T(8,128)(2,1)} %get-tuple-element.53.q_ref.k_ref.v_ref, ...), custom_call_target="tpu_custom_call" | custom-call | tf_op jit(solution)/shard_map/attend/pallas_call | solution.py:524
  126.0 36.3 %feed.1 = (bf16[592,768]{1,0:T(8,128)(2,1)}, f32[592,768]{1,0:T(8,128)}, bf16[592,768]{1,0:T(8,128)(2,1)}, bf16[768,768]{1,0:T(8,128)(2,1)}, bf16[768,3072]{1,0:...) custom-call(s32[1]{0:T(128)S(6)} %copy.43.kind_ref, bf16[592,768]{1,0:T(8,128)(2,1)} %bitcast.36, ...), custom_call_target="tpu_custom_call" | custom-call | tf_op jit(solution)/shard_map/feed/pallas_call | solution.py:663
  162.3 16.3 %attend_back.1 = (bf16[592,768]{1,0:T(8,128)(2,1)}, bf16[592,768]{1,0:T(8,128)(2,1)}, bf16[592,768]{1,0:T(8,128)(2,1)}, bf16[12,592,592]{2,1,0:T(8,128)(2,1)}) custom-call(bf16[592,2304]{1,0:T(8,128)(2,1)} %get-tuple-element.53.q_ref.k_ref.v_ref, bf16[592,2304]{1,0:T(8,128)(2,1)} %get-tuple-element.53.q_ref.k_ref.v_ref, ...), custom_call_target="tpu_custom_call" | custom-call | tf_op jit(solution)/shard_map/attend_back/pallas_call | solution.py:565
  178.6 0.0 copy-start.1
  178.6 11.8 %finish.1 = (bf16[768,2304]{1,0:T(8,128)(2,1)}, bf16[592,768]{1,0:T(8,128)(2,1)}, f32[16,768]{1,0:T(8,128)}) custom-call(bf16[592,768]{1,0:T(8,128)(2,1)} %bitcast.37, f32[592,768]{1,0:T(8,128)} %get-tuple-element.62.dmid_ref, bf16[592,768]{1,0:T(8,128)(2,1)} %get-tuple-element.63.normed_ref, f32[16,768]{1,0:T(8,128)} %get-tuple-element.51.vec_ref, ...), custom_call_target="tpu_custom_call" | custom-call | tf_op jit(solution)/shard_map/finish/pallas_call | solution.py:754
  190.4 0.0 copy-done.1
  190.5 1.4 add.3.refs_4_
  191.9 21.9 %table_gradient.1.refs_6_ = f32[16,2240]{1,0:T(8,128)} custom-call(s32[1]{0:T(128)S(6)} %copy.43.kind_ref, bf16[12,592,592]{2,1,0:T(8,128)(2,1)} %get-tuple-element.77.ds_ref, s32[1,2432]{1,0:T(1,128)} %get-tuple-element.78.lab_ref, bf16[592,224]{1,0:T(8,128)(2,1)} %constant.6.clone.rowsel_ref, bf16[512,592]{1,0:T(8,128)(2,1)} %constant.7.clone.colsel_ref), custom_call_target="tpu_custom_call" | custom-call | tf_op jit(solution)/shard_map/table_gradient/pallas_call | solution.py:390
  213.8 123.0 %reduce_all.1 = (bf16[384,768]{1,0:T(8,128)(2,1)}, bf16[96,3072]{1,0:T(8,128)(2,1)}, bf16[96,768]{1,0:T(8,128)(2,1)}, bf16[96,2304]{1,0:T(8,128)(2,1)}, f32[16,384]{1,0:T(8,128)}) custom-call(bf16[4,2,384,768]{3,2,1,0:T(8,128)(2,1)} %bitcast.39, bf16[4,2,96,3072]{3,2,1,0:T(8,128)(2,1)} %bitcast.38, bf16[4,2,96,768]{3,2,1,0:T(8,128)(2,1)} %bitcast.43, ...), custom_call_target="tpu_custom_call" | custom-call | tf_op jit(solution)/shard_map/reduce_all/pallas_call | solution.py:1175
  336.8 0.0 copy-start
  336.8 1.3 slice.45
  338.1 1.6 fusion
  339.7 0.7 slice_bitcast_fusion
  340.4 0.6 copy.42
  341.1 1.6 bitcast_convert_fusion.3
  342.7 2.0 bitcast_convert_fusion.2
  344.7 2.2 bitcast_convert_fusion.1
  346.9 0.0 copy-done
  346.9 1.1 bitcast_convert_fusion
Async XLA Ops:
  178.6 11.8 %copy-start.1 = (f32[16,768]{1,0:T(8,128)S(1)}, f32[16,768]{1,0:T(8,128)}, u32[]{:S(2)}) copy-start(f32[16,768]{1,0:T(8,128)} %get-tuple-element.74) | copy-start | bytes 147460
  336.8 10.1 %copy-start = (bf16[384,768]{1,0:T(8,128)(2,1)S(1)}, bf16[384,768]{1,0:T(8,128)(2,1)}, u32[]{:S(2)}) copy-start(bf16[384,768]{1,0:T(8,128)(2,1)} %get-tuple-element.83) | copy-start | bytes 1769476

commit v3 on v1

v3 whole, which is shorter than its diff:
```python
import functools

import jax
import jax.numpy as jnp
import numpy as np
from jax import lax
from jax.experimental import pallas as pl
from jax.experimental.pallas import tpu as pltpu
from jax.sharding import PartitionSpec as P

f32 = jnp.float32
bf16 = jnp.bfloat16
norm_eps = 1e-06
neg_fill = -1000000000.0
vmem_bytes = 60 << 20

NN = (((1,), (0,)), ((), ()))
NT = (((1,), (1,)), ((), ()))
TN = (((0,), (0,)), ((), ()))


def mm(left, right, dims=NN):
    return lax.dot_general(left, right, dims, preferred_element_type=f32)


def round_up(value, unit):
    return -(-value // unit) * unit


class Plan:
    def __init__(self, small_len, large_len, rows, heads, buckets):
        self.heads, self.buckets = heads, buckets
        self.rows = rows
        self.small_len, self.large_len = small_len, large_len
        self.gs = int(round((small_len - 1) ** 0.5))
        self.gl = int(round((large_len - 1) ** 0.5))
        gl, gs = self.gl, self.gs
        self.strip_l = round_up(2 * gl * gl, 128)
        self.strip_s = round_up(2 * gs * (2 * gs - 1) + gs, 128)
        self.line = 2 * self.strip_l
        self.lanes = self.line + 128
        self.pad_cols = round_up(2 * gs * gs + 1, 128)
        self.pad_rows = 16 * gs
        self.cls_col = 2 * gs * gs
        self.cls_row = gs

    def place(self, di, dj, limit):
        gl = self.gl
        good = (np.abs(di) < limit) & (np.abs(dj) < limit)
        row = 1 + gl * np.maximum(di, 0) + np.maximum(dj, 0)
        col = 1 + gl * np.maximum(-di, 0) + np.maximum(-dj, 0)
        return np.where(good, row, 0), np.where(good, col, 0), good

    def positions(self):
        gl, gs = self.gl, self.gs
        x = np.arange(self.strip_l)
        rows, cols, goods = [], [], []
        for parity in range(2):
            m = 2 * ((x + gl) // (2 * gl)) if parity == 0 else 2 * (x // (2 * gl)) + 1
            t = x - gl * m
            r, c, g = self.place(gl - m, -t, gl)
            rows.append(r), cols.append(c), goods.append(g)
        large = [np.concatenate(v) for v in (rows, cols, goods)]
        x = np.arange(self.strip_s)
        m = x // (2 * gs)
        t = x - 2 * gs * m - gs
        small = [np.resize(np.zeros(1, v.dtype), self.line) for v in large]
        for dst, src in zip(small, self.place(gs - 1 - m, -t, gs)):
            dst[: self.strip_s] = src
        tail_r, tail_c, tail_g = np.zeros(128, int), np.zeros(128, int), np.zeros(128, bool)
        tail_r[:3], tail_c[:3], tail_g[:3] = (0, 1, 0), (1, 0, 0), True
        out = []
        for base in (large, small):
            out.append([np.concatenate(v) for v in zip(base, (tail_r, tail_c, tail_g))])
        return out

    def selector_arrays(self):
        gs = self.gs
        rows = np.zeros((self.rows, self.pad_rows), np.float32)
        cols = np.zeros((self.pad_cols, self.rows), np.float32)
        for image in range(3):
            for tok in range(self.small_len):
                r = image * self.small_len + tok
                i, j = divmod(tok - 1, gs)
                rows[r, self.cls_row if tok == 0 else 16 * i + j] = 1
                cols[self.cls_col if tok == 0 else 2 * gs * i + j, r] = 1
        return rows, cols

    def selectors(self):
        rows, cols = self.selector_arrays()
        return jnp.asarray(rows, bf16), jnp.asarray(cols, bf16)


def iota(shape, dim):
    return lax.broadcasted_iota(jnp.int32, shape, dim)


def pick_plan(plan):
    out = []
    for r, c, good in plan.positions():
        down = good & ((r - 1) // plan.gl >= (c - 1) // plan.gl)
        key = np.where(down, r, c)
        sub = np.where(down, c, r) - 1
        valid = good.copy()
        valid[plan.line :] = False
        out.append(np.stack([key, sub, down.astype(int), valid.astype(int)]))
    return jnp.asarray(np.concatenate(out), jnp.int32)


def read_labels(plan, is_large, idx_ref, pick_ref, lab_ref):
    size, gl = idx_ref.shape[0], plan.gl
    across = idx_ref[1 : 1 + gl, :]
    down = idx_ref[:, 1 : 1 + gl].astype(f32).T.astype(jnp.int32)
    sides = []
    for v in (across, down):
        sides += [(v >> 6).astype(f32), (v & 63).astype(f32)]
    sides = jnp.concatenate(sides, axis=0).astype(bf16)
    for chunk in range(plan.line // 128):
        lanes = slice(chunk * 128, (chunk + 1) * 128)
        key, sub, use_down, valid = [
            jnp.where(is_large, pick_ref[i : i + 1, lanes], pick_ref[4 + i : 5 + i, lanes])
            for i in range(4)
        ]
        hot = jnp.where(iota((size, 128), 0) == key, 1.0, 0.0).astype(bf16)
        here = iota((gl, 128), 0) == sub
        rows = mm(sides, hot)
        for digit in range(2):
            a = rows[digit * gl : (digit + 1) * gl]
            b = rows[(2 + digit) * gl : (3 + digit) * gl]
            found = jnp.where(here, jnp.where(use_down == 1, b, a), 0.0)
            found = jnp.sum(found, axis=0, keepdims=True).astype(jnp.int32)
            lab_ref[digit : digit + 1, lanes] = jnp.where(valid == 1, found, -1)
    lane = iota((1, 128), 1)
    tail = jnp.where(lane == 0, idx_ref[0:1, 1:2], -1)
    tail = jnp.where(lane == 1, idx_ref[1:2, 0:1], tail)
    tail = jnp.where(lane == 2, idx_ref[0:1, 0:1], tail)
    lab_ref[0:1, plan.line : plan.line + 128] = jnp.where(tail < 0, -1, tail >> 6)
    lab_ref[1:2, plan.line : plan.line + 128] = jnp.where(tail < 0, -1, tail & 63)


def table_lines(plan, tab, lab_ref, line_ref):
    count = tab.shape[1] // 64
    split = jnp.concatenate([tab[:, 64 * i : 64 * (i + 1)] for i in range(count)], axis=0)
    split = split.astype(bf16)
    for chunk in range(plan.lanes // 128):
        lanes = slice(chunk * 128, (chunk + 1) * 128)
        first, second = lab_ref[0:1, lanes], lab_ref[1:2, lanes]
        hot = jnp.where(iota((64, 128), 0) == second, 1.0, 0.0).astype(bf16)
        rows = mm(split, hot)
        line = jnp.zeros((16, 128), f32)
        for i in range(count):
            line = jnp.where(first == i, rows[16 * i : 16 * (i + 1)], line)
        for i in range(plan.heads):
            line_ref[i, :, lanes] = line[i : i + 1]


def table_from_lines(plan, line_of, lab_ref, buckets):
    count = buckets // 64
    total = jnp.zeros((32 * count, 64), f32)
    for chunk in range(plan.lanes // 128):
        lanes = slice(chunk * 128, (chunk + 1) * 128)
        first, second = lab_ref[0:1, lanes], lab_ref[1:2, lanes]
        hot = jnp.where(iota((64, 128), 0) == second, 1.0, 0.0).astype(bf16)
        part = line_of(chunk)
        high = part.astype(bf16)
        low = (part - high.astype(f32)).astype(bf16)
        both = jnp.concatenate([high, low], axis=0)
        stack = [jnp.where(first == i, both, jnp.zeros_like(both)) for i in range(count)]
        total = total + mm(jnp.concatenate(stack, axis=0), hot, NT)
    pieces = []
    for i in range(count):
        pieces.append(total[32 * i : 32 * i + 16] + total[32 * i + 16 : 32 * i + 32])
    return jnp.concatenate(pieces, axis=1)


def segments(plan, is_large, ids):
    n = plan.small_len
    small = jnp.where(ids >= n, 1, 0) + jnp.where(ids >= 2 * n, 1, 0) + jnp.where(ids >= 3 * n, 1, 0)
    return jnp.where(is_large, jnp.where(ids < plan.large_len, 0, 3), small)


def large_strip(plan, line_ref, h):
    gl, span = plan.gl, plan.strip_l
    rolled = []
    for parity in range(2):
        line = jnp.broadcast_to(line_ref[h, :, parity * span : (parity + 1) * span], (gl, span))
        rolled.append(pltpu.roll(line, 0, axis=1, stride=1, stride_axis=0))
    odd = (iota((gl, span), 1) + span - 1) % span // gl % 2
    odd = jnp.where(iota((gl, span), 0) == 0, 1 - odd, odd)
    strip = jnp.where(odd == 1, rolled[1], rolled[0])
    return jnp.concatenate([strip, strip[:, :128]], axis=1)


def band_move(plan, a):
    return plan.gl * (plan.gl - a)


def small_padded(plan, line_ref, h, tail):
    gs, span = plan.gs, plan.strip_s
    line = jnp.broadcast_to(line_ref[h, :, 0:span], (16, span))
    strip = pltpu.roll(line, 0, axis=1, stride=1, stride_axis=0)
    col = iota((16, plan.pad_cols), 1)
    row = iota((16, plan.pad_cols), 0)
    bands = []
    for i in range(gs):
        move = 2 * gs * (gs - 1 - i) + gs
        band = pltpu.roll(strip, (span - move) % span, axis=1)[:, : plan.pad_cols]
        band = jnp.where(col == plan.cls_col, tail[:, 1:2], band)
        if i == 0:
            edge = jnp.where(col == plan.cls_col, tail[:, 2:3], tail[:, 0:1])
            band = jnp.where(row == plan.cls_row, edge, band)
        bands.append(band)
    return jnp.concatenate(bands, axis=0).astype(bf16)


def bias_head(plan, is_large, line_ref, rowsel, colsel, h, out_ref):
    gl, rows = plan.gl, plan.rows
    wide = round_up(rows, 128)
    tail = line_ref[h, :, plan.line : plan.line + 128]
    cols = mm(small_padded(plan, line_ref, h, tail), colsel[...]).astype(bf16)
    small_all = mm(rowsel[...], cols)
    strip = large_strip(plan, line_ref, h)
    span = strip.shape[1]
    col = iota((1, wide), 1)
    seg_col = segments(plan, is_large, col)
    bands = -(-rows // gl)
    for pair in range(-(-bands // 2)):
        first = 2 * gl * pair
        count = min(2 * gl, rows - first)
        parts = []
        for a in range(2 * pair, 2 * pair + 2):
            if a >= bands:
                continue
            move = band_move(plan, a)
            low = move // 128 * 128
            piece = strip[:, low : min(low + wide + 128, span)]
            if piece.shape[1] < wide + 128:
                piece = jnp.concatenate(
                    [piece, jnp.zeros((gl, wide + 128 - piece.shape[1]), f32)], axis=1
                )
            turn = (wide + 128 - (move - low)) % (wide + 128)
            parts.append((pltpu.roll(piece, turn, axis=1) if turn else piece)[:, :wide])
        block = (jnp.concatenate(parts, axis=0) if len(parts) > 1 else parts[0])[:count]
        row = iota((count, 1), 0) + first
        block = jnp.where(col == 0, tail[:, 1:2], block)
        if first == 0:
            block = jnp.where(row == 0, jnp.where(col == 0, tail[:, 2:3], tail[:, 0:1]), block)
        if first + count > plan.large_len:
            block = jnp.where(row < plan.large_len, block, 0.0)
        small = small_all[first : first + count]
        small = jnp.concatenate([small, jnp.zeros((count, wide - rows), f32)], axis=1)
        block = jnp.where(is_large, block, small)
        block = jnp.where(segments(plan, is_large, row) == seg_col, block, neg_fill)
        out_ref[h, first : first + count, :] = block[:, :rows].astype(bf16)


params = pltpu.CompilerParams(vmem_limit_bytes=vmem_bytes)


def norm_stats(values):
    mean = jnp.mean(values, axis=1, keepdims=True)
    centred = values - mean
    var = jnp.mean(centred * centred, axis=1, keepdims=True)
    inv = lax.rsqrt(var + norm_eps)
    return centred * inv, inv


def norm_back(d_out, gain, normal, inv):
    d_normal = d_out * gain
    mean_d = jnp.mean(d_normal, axis=1, keepdims=True)
    mean_dn = jnp.mean(d_normal * normal, axis=1, keepdims=True)
    return inv * (d_normal - mean_d - normal * mean_dn)


def rows_sum(values):
    return jnp.sum(values, axis=0, keepdims=True)


def gelu_parts(v):
    size = jnp.abs(v)
    bell = jnp.exp(-0.5 * v * v)
    t = 1.0 / (1.0 + (0.3275911 * 0.7071067811865476) * size)
    poly = t * (
        0.127414796
        + t * (-0.142248368 + t * (0.7107068705 + t * (-0.7265760135 + t * 0.5307027145)))
    )
    tail = poly * bell
    phi = jnp.where(v < 0, tail, 1.0 - tail)
    return v * phi, phi + v * bell * 0.3989422804014327


(
    FIRST_GAIN,
    FIRST_SHIFT,
    QUERY_BIAS,
    VALUE_BIAS,
    OUTPUT_BIAS,
    ATTEND_SCALE,
    SECOND_GAIN,
    SECOND_SHIFT,
    REDUCE_BIAS,
    FEED_SCALE,
) = range(10)


def vec(ref, idx):
    return ref[idx : idx + 1, :]


def half_mask(rows):
    return iota((rows, 128), 1) < 64


class Spot:
    def __init__(self, n):
        self.n, self.levels = n, n // 2
        self.rep, self.f = lax.axis_index("rep"), lax.axis_index("fsdp")
        self.half, self.core = self.rep // 2, self.rep % 2
        self.level, self.side = self.f // 2, self.f % 2

    def at(self, rep=None, f=None):
        return {"rep": self.rep if rep is None else rep, "fsdp": self.f if f is None else f}

    def sibling(self):
        return self.at(rep=2 * self.half + 1 - self.core)

    def across(self):
        return self.at(rep=2 * (1 - self.half) + self.core)

    def beside(self):
        return self.at(f=2 * self.level + 1 - self.side)

    def along(self, step):
        return self.at(f=2 * ((self.level + step) % self.levels) + self.side)

    def from_along(self, step, side=None):
        side = self.side if side is None else side
        return 2 * ((self.level + self.levels - step) % self.levels) + side


MESH = pl.DeviceIdType.MESH


def greet(devices, count):
    barrier = pltpu.get_barrier_semaphore()
    for device in devices:
        pl.semaphore_signal(barrier, inc=1, device_id=device, device_id_type=MESH)
    pl.semaphore_wait(barrier, count)


def send(src, dst, send_sem, recv_sem, device):
    return pltpu.make_async_remote_copy(
        src_ref=src,
        dst_ref=dst,
        send_sem=send_sem,
        recv_sem=recv_sem,
        device_id=device,
        device_id_type=MESH,
    )


def fast_shape(reps, n, shard_rows):
    return reps == 4 and n == 8 and all(rows % 96 == 0 for rows in shard_rows)


def spread_block(refs, block_ref):
    *vectors, be_ref, table_ref = refs
    share, heads = table_ref.shape
    eye = jnp.where(iota((16, heads), 0) == iota((16, heads), 1), 1.0, 0.0).astype(bf16)
    lanes = block_ref.shape[1]
    table = mm(eye, table_ref[...], NT)
    width = vectors[0].shape[1]
    rows = [v[...].astype(f32) for v in vectors]
    rows.append(jnp.zeros((16 - len(rows), width), f32))
    block = jnp.concatenate(
        [table, jnp.zeros((16, lanes - share - width), f32), jnp.concatenate(rows, axis=0)], axis=1
    )
    wide = jnp.broadcast_to(be_ref[...].astype(f32), (16, lanes))
    block_ref[...] = jnp.where(iota((16, lanes), 0) == heads, wide, block).astype(bf16)


any_spec = pl.BlockSpec(memory_space=pl.ANY)
vmem_spec = pl.BlockSpec(memory_space=pltpu.VMEM)


def add16(left, right):
    return (left.astype(f32) + right.astype(f32)).astype(bf16)


def gather_plain(shorts, shards, n):
    gather = lambda value, axis: lax.all_gather(value, "fsdp", axis=axis, tiled=True)
    vecs = gather(jnp.concatenate(shorts[:10], axis=0), 1).astype(f32)
    vecs = jnp.pad(vecs, ((0, 6), (0, 0)))
    table = gather(shorts[11], 0).T
    table = jnp.pad(table, ((0, 16 - table.shape[0]), (0, 0)))
    return [gather(w, 0) for w in shards], vecs, gather(shorts[10], 1).astype(f32), table


def reduce_plain(grads, vec_sums, be_sums, table_sums, n):
    def whole_sum(value):
        value = lax.psum_scatter(value, "fsdp", scatter_dimension=0, tiled=True)
        return lax.psum(value, "rep")

    sums = lax.psum((vec_sums, be_sums, table_sums), ("rep", "fsdp"))
    me = lax.axis_index("fsdp")
    cut = lambda v: lax.dynamic_slice_in_dim(v, me * (v.shape[1] // n), v.shape[1] // n, axis=1)
    vec_part, be_part, table_part = [cut(v) for v in sums]
    wide = be_part.shape[1]
    space = max(wide - vec_part.shape[1] - table_part.shape[1], 0)
    body = jnp.concatenate([table_part, jnp.zeros((16, space), f32), vec_part], axis=1)
    block = jnp.where(jnp.arange(16)[:, None] == 12, jnp.pad(be_part, ((0, 0), (0, body.shape[1] - wide))), body)
    return [whole_sum(g) for g in grads], block


class Piece:
    sems = 8

    def __init__(self, spot, shard, whole, row, col, cols, ss, rs, base):
        self.level, self.side = spot.level, spot.side
        levels = spot.levels
        part, q = 48, 16
        start = row + spot.core * part
        cut = pl.ds(col, cols)
        rows = lambda first, size: pl.ds(pl.multiple_of(first, 16), size)
        plane = rows(start + spot.half * q, 2 * q)
        outer = rows(start + spot.half * 2 * q, q)
        core_rows = rows(start, part)
        side = spot.side

        def copy(idx, src, dst, device):
            return send(src, dst, ss.at[base + idx], rs.at[base + idx], device)

        own = shard.at[plane, cut]
        here = whole.at[spot.level, side, plane, cut]
        self.local = pltpu.make_async_copy(own, here, ss.at[base + levels + 3])
        self.z = [copy(step - 1, own, here, spot.along(step)) for step in range(1, levels)]
        column = whole.at[:, side, plane, cut]
        self.y = copy(levels - 1, column, column, spot.beside())
        near = whole.at[:, side, outer, cut]
        far = whole.at[:, 1 - side, outer, cut]
        self.x = [
            copy(levels, near, near, spot.across()),
            copy(levels + 1, far, far, spot.across()),
        ]
        done = whole.at[:, :, core_rows, cut]
        self.c = copy(levels + 2, done, done, spot.sibling())

    def start(self):
        self.local.start()
        for copy in self.z:
            copy.start()

    def after_z(self):
        self.local.wait()
        for copy in self.z:
            copy.wait_recv()
        self.y.start()
        self.x[0].start()

    def after_y(self):
        self.y.wait_recv()
        self.x[1].start()

    def after_x(self):
        self.x[0].wait_recv()
        self.x[1].wait_recv()
        self.c.start()

    def after_c(self):
        self.c.wait_recv()

    def finish(self):
        for copy in self.z + [self.y, self.c] + self.x:
            copy.wait_send()


def piece_cuts(shard_shapes):
    cuts = []
    for idx, (rows, cols) in enumerate(shard_shapes):
        for row in range(0, rows, 96):
            tile = next(t for t in (768, 512, 384, 256, 128) if cols % t == 0)
            for col in range(0, cols, tile):
                cuts.append((idx, row, col, tile))
    return cuts


def front_kernel(plan, n, fast, cuts, *refs):
    refs = list(refs)
    take = lambda count: [refs.pop(0) for _ in range(count)]
    (kind_ref, tok_ref, idx_ref, pick_ref, rowsel_ref, colsel_ref) = take(6)
    if fast:
        shorts, shards = take(12), take(4)
        wholes = take(4)
        vec_ref, be_ref = take(2)
    else:
        vec_ref, be_ref, tab_ref = take(3)
        wholes = take(4)
    lab_ref, normed_ref, mixed_ref, middle_ref, branch_ref = take(5)
    qkv_out, probs_out, act_out, slope_out = take(4)
    line_ref, heads_ref, qkv_ref, wt_ref, wo_ref, we_ref, act_ref, slope_ref, second_ref = take(9)
    load_sems, save_sems = take(2)
    is_large = kind_ref[0] == 1
    heads = plan.heads
    pairs = heads // 2
    width = tok_ref.shape[1]

    loads = []
    for idx, ref in enumerate((wt_ref, wo_ref, we_ref)):
        for j in range(ref.shape[0]):
            cut = pl.ds(j * width, width)
            src = wholes[idx].at[:, :, :, cut]
            loads.append(pltpu.make_async_copy(src, ref.at[j], load_sems.at[len(loads)]))
    matrix = lambda ref, j: ref[j].reshape(width, width)

    if fast:
        block, blocks, ss, rs, bss, brs = refs
        spot = Spot(n)
        peers = [spot.at(f=(spot.f + k) % n) for k in range(1, n)]
        greet(peers + [spot.sibling(), spot.across()], n + 1)
        pieces = []
        for idx, row, col, cols in cuts:
            base = len(pieces) * Piece.sems
            pieces.append(Piece(spot, shards[idx], wholes[idx], row, col, cols, ss, rs, base))
        spread_block(shorts, block)
        small = []
        for k, peer in enumerate(peers):
            small.append(send(block, blocks.at[spot.f], bss.at[k], brs.at[k], peer))
            small[k].start()
        blocks[spot.f] = block[...]
        pieces[0].start()
        pieces[1].start()

    def step(k):
        if not fast:
            if k == 0:
                for load in loads:
                    load.start()
            return
        for back, action in enumerate(("after_z", "after_y", "after_x", "after_c")):
            if 0 <= k - back < len(pieces):
                getattr(pieces[k - back], action)()
                if back == 0 and k + 2 < len(pieces):
                    pieces[k + 2].start()
                if back == 3 and k - 3 < len(loads):
                    loads[k - 3].start()

    last_step = len(cuts) + 3
    read_labels(plan, is_large, idx_ref, pick_ref, lab_ref)
    step(0)
    if fast:
        for copy in small:
            copy.wait()
        share, bshare = shorts[0].shape[1], shorts[11].shape[0]
        tab = []
        for f in range(n):
            part = blocks[f].astype(f32)
            wide = part.shape[1]
            vec_ref[:, f * share : (f + 1) * share] = part[:, wide - share :]
            tab.append(part[:, :bshare])
            be_ref[:, f * wide : (f + 1) * wide] = part[heads : heads + 1, :]
        tab = jnp.concatenate(tab, axis=1)
    else:
        tab = tab_ref[...]
    table_lines(plan, tab, lab_ref, line_ref)
    step(1)
    normal, _ = norm_stats(tok_ref[...].astype(f32))
    normed = normal * vec(vec_ref, FIRST_GAIN) + vec(vec_ref, FIRST_SHIFT)
    normed_ref[...] = normed.astype(bf16)

    third = heads // 3
    for group in range(3):

        @pl.loop(group * third, (group + 1) * third)
        def _(h):
            bias_head(plan, is_large, line_ref, rowsel_ref, colsel_ref, h, heads_ref)

        step(2 + group)

    step(5)
    saves = []

    def save(src, dst):
        saves.append(pltpu.make_async_copy(src, dst, save_sems.at[len(saves)]))
        saves[-1].start()

    normed = normed_ref[...]
    for j in range(3):
        loads[j].wait()
        triple = mm(normed, matrix(wt_ref, j))
        if j == 0:
            triple = triple + vec(vec_ref, QUERY_BIAS)
        if j == 2:
            triple = triple + vec(vec_ref, VALUE_BIAS)
        triple = triple.astype(bf16)
        if j == 0:
            triple = triple * jnp.array(0.125, bf16)
        for p in range(pairs):
            qkv_ref[j * pairs + p] = triple[:, 128 * p : 128 * (p + 1)]
    save(qkv_ref, qkv_out)
    step(6)

    def attend_pair(p):
        q, k, v = qkv_ref[p], qkv_ref[pairs + p], qkv_ref[2 * pairs + p]
        lower = half_mask(q.shape[0])
        mixed = []
        for t in range(2):
            keep = lower if t == 0 else ~lower
            scores = mm(jnp.where(keep, q, jnp.zeros_like(q)), k, NT)
            scores = scores + heads_ref[2 * p + t].astype(f32)
            top = jnp.max(scores, axis=1, keepdims=True)
            exps = jnp.exp(scores - top)
            total = jnp.sum(exps, axis=1, keepdims=True)
            probs = (exps * (1.0 / total)).astype(bf16)
            heads_ref[2 * p + t] = probs
            mixed.append(mm(probs, v))
        mixed_ref[p] = jnp.where(lower, mixed[0], mixed[1]).astype(bf16)

    share_of = pairs // 3
    for group in range(3):

        @pl.loop(group * share_of, (group + 1) * share_of)
        def _(p):
            attend_pair(p)

        cut = pl.ds(group * 2 * share_of, 2 * share_of)
        save(heads_ref.at[cut], probs_out.at[cut])
        step(7 + group)

    loads[3].wait()
    mixed = jnp.concatenate([mixed_ref[p] for p in range(pairs)], axis=1)
    branch = mm(mixed, matrix(wo_ref, 0)) + vec(vec_ref, OUTPUT_BIAS)
    branch_ref[...] = branch.astype(bf16)
    middle = tok_ref[...].astype(f32) + vec(vec_ref, ATTEND_SCALE) * branch
    middle_ref[...] = middle
    normal, _ = norm_stats(middle)
    second = normal * vec(vec_ref, SECOND_GAIN) + vec(vec_ref, SECOND_SHIFT)
    second_ref[...] = second.astype(bf16)
    for j in range(we_ref.shape[0]):
        if 10 + j <= last_step:
            step(10 + j)
        loads[4 + j].wait()
        pre = mm(second_ref[...], matrix(we_ref, j)) + be_ref[:, j * width : (j + 1) * width]
        value, slope = gelu_parts(pre)
        act_ref[j] = value.astype(bf16)
        slope_ref[j] = slope.astype(bf16)
        save(act_ref.at[j], act_out.at[j])
        save(slope_ref.at[j], slope_out.at[j])
    for k in range(10 + we_ref.shape[0], last_step):
        step(k)
    for copy in saves:
        copy.wait()
    if fast:
        for piece in pieces:
            piece.finish()


def front(plan, kind, tokens, large_index, rowsel, colsel, n, fast, shorts, shards):
    rows, width = tokens.shape
    heads = plan.heads
    sds = jax.ShapeDtypeStruct
    picks = pick_plan(plan)
    levels = n // 2
    hidden = shards[2].shape[1]
    blocks = hidden // width
    cuts = piece_cuts([w.shape for w in shards]) if fast else []
    inputs = [kind, tokens, large_index, picks, rowsel, colsel]
    in_specs = [pl.BlockSpec(memory_space=pltpu.SMEM)] + [vmem_spec] * 5
    outs, out_specs = [], []
    if fast:
        inputs += shorts + shards
        in_specs += [vmem_spec] * 12 + [any_spec] * 4
        outs += [sds((levels, 2) + w.shape, bf16) for w in shards]
        outs += [sds((16, width), f32), sds((1, hidden), f32)]
        out_specs += [any_spec] * 4 + [vmem_spec] * 2
    else:
        wholes, vecs, be, table = gather_plain(shorts, shards, n)
        wholes = [w.reshape(4, 2, w.shape[0] // 8, w.shape[1]) for w in wholes]
        inputs += [vecs, be, table.astype(f32)] + wholes
        in_specs += [vmem_spec] * 3 + [any_spec] * 4
    outs += [
        sds((2, plan.lanes), jnp.int32),
        sds((rows, width), bf16),
        sds((heads // 2, rows, 128), bf16),
        sds((rows, width), f32),
        sds((rows, width), bf16),
        sds((3 * heads // 2, rows, 128), bf16),
        sds((heads, rows, rows), bf16),
        sds((blocks, rows, width), bf16),
        sds((blocks, rows, width), bf16),
    ]
    out_specs += [vmem_spec] * 5 + [any_spec] * 4
    tile = lambda count: pltpu.VMEM((count, 4, 2, width // 8, width), bf16)
    scratch = [
        pltpu.VMEM((heads, 1, plan.lanes), f32),
        pltpu.VMEM((heads, rows, rows), bf16),
        pltpu.VMEM((3 * heads // 2, rows, 128), bf16),
        tile(3),
        tile(1),
        tile(blocks),
        pltpu.VMEM((blocks, rows, width), bf16),
        pltpu.VMEM((blocks, rows, width), bf16),
        pltpu.VMEM((rows, width), bf16),
        pltpu.SemaphoreType.DMA((4 + blocks,)),
        pltpu.SemaphoreType.DMA((4 + 2 * blocks,)),
    ]
    if fast:
        wide = shorts[10].shape[1]
        scratch += [
            pltpu.VMEM((16, wide), bf16),
            pltpu.VMEM((n, 16, wide), bf16),
            pltpu.SemaphoreType.DMA((len(cuts) * Piece.sems,)),
            pltpu.SemaphoreType.DMA((len(cuts) * Piece.sems,)),
            pltpu.SemaphoreType.DMA((n - 1,)),
            pltpu.SemaphoreType.DMA((n - 1,)),
        ]
    kernel_params = dict(vmem_limit_bytes=vmem_bytes)
    if fast:
        kernel_params.update(collective_id=1, has_side_effects=True)
    result = pl.pallas_call(
        functools.partial(front_kernel, plan, n, fast, cuts),
        in_specs=in_specs,
        out_specs=out_specs,
        out_shape=outs,
        scratch_shapes=scratch,
        compiler_params=pltpu.CompilerParams(**kernel_params),
        name="front",
    )(*inputs)
    result = list(result)
    if fast:
        wholes = result[:4]
        vecs, be = result[4:6]
        result = result[6:]
    return wholes, vecs, be, result


def image_rows(plan):
    out = []
    for image in range(3):
        first, last = image * plan.small_len, (image + 1) * plan.small_len
        rows = (first // 16 * 16, round_up(last, 16))
        lanes = (first // 128 * 128, min(round_up(last, 128), plan.rows))
        out.append((rows, lanes))
    return out


def image_selectors(plan):
    rows, _ = plan.selector_arrays()
    out = []
    for image, ((low, high), _) in enumerate(image_rows(plan)):
        part = rows.copy()
        part[: image * plan.small_len] = 0
        part[(image + 1) * plan.small_len :] = 0
        out.append(np.pad(part[low:high].T, ((0, 0), (0, 256 - (high - low)))))
    return jnp.asarray(np.concatenate(out, axis=1), bf16)


def fold_head(plan, ds_ref, pick, colsel, large_ref, small_ref, tail_ref, h, is_large):
    gl, gs, rows = plan.gl, plan.gs, plan.rows
    wide = round_up(rows, 128)
    width = plan.strip_l + 128
    bands = -(-rows // gl)
    total = jnp.zeros((gl, width), f32)
    side = jnp.zeros((2 * gl, 128), f32)
    for pair in range(-(-bands // 2)):
        first = 2 * gl * pair
        count = min(2 * gl, rows - first)
        block = ds_ref[first : first + count, :].astype(f32)
        block = jnp.concatenate([block, jnp.zeros((count, wide - rows), f32)], axis=1)
        if count < 2 * gl:
            block = jnp.concatenate([block, jnp.zeros((2 * gl - count, wide), f32)], axis=0)
        if pair == 0:
            row = iota((2 * gl, wide), 0)
            top_row = jnp.where(row == 0, block, 0.0)
            block = jnp.where(row == 0, 0.0, block)
        side = side + block[:, :128]
        block = jnp.where(iota((1, wide), 1) == 0, 0.0, block)
        for half in range(2):
            a = 2 * pair + half
            if a >= bands:
                continue
            move = band_move(plan, a)
            low = move // 128 * 128
            piece = block[half * gl : (half + 1) * gl]
            if move > low:
                piece = jnp.concatenate([piece, jnp.zeros((gl, 128), f32)], axis=1)
                piece = pltpu.roll(piece, move - low, axis=1)
            piece = piece[:, : width - low]
            parts = [jnp.zeros((gl, low), f32)] if low else []
            parts.append(piece)
            if low + piece.shape[1] < width:
                parts.append(jnp.zeros((gl, width - low - piece.shape[1]), f32))
            total = total + (jnp.concatenate(parts, axis=1) if len(parts) > 1 else piece)
    large_ref[h] = jnp.concatenate(
        [total[:, :128] + total[:, plan.strip_l :], total[:, 128 : plan.strip_l]], axis=1
    )
    lane = iota((1, wide), 1)
    full = lambda v: jnp.sum(jnp.sum(v, axis=0, keepdims=True), axis=1, keepdims=True)
    corner = full(jnp.where(lane == 0, top_row, 0.0))
    top = full(jnp.where(lane == 0, 0.0, top_row))
    side = full(jnp.where(iota((1, 128), 1) == 0, side, 0.0))

    padded, start = None, 0
    for (r0, r1), (l0, l1) in image_rows(plan):
        cols = mm(ds_ref[r0:r1, l0:l1], colsel[:, l0:l1], NT).astype(bf16)
        part = mm(pick[:, start : start + r1 - r0], cols)
        padded = part if padded is None else padded + part
        start += 256
    span = plan.strip_s
    col = iota((1, plan.pad_cols), 1)
    row = iota((16, 1), 0)
    acc = jnp.zeros((16, span), f32)
    edge = jnp.zeros((16, plan.pad_cols), f32)
    for i in range(gs):
        band = padded[16 * i : 16 * (i + 1)]
        if i == 0:
            top_s = jnp.where(row == plan.cls_row, band, 0.0)
            band = jnp.where(row == plan.cls_row, 0.0, band)
        edge = edge + band
        band = jnp.where(col < plan.cls_col, band, 0.0)
        band = jnp.concatenate([band, jnp.zeros((16, span - plan.pad_cols), f32)], axis=1)
        acc = acc + pltpu.roll(band, 2 * gs * (gs - 1 - i) + gs, axis=1)
    small_ref[h] = acc
    corner_s = full(jnp.where(col == plan.cls_col, top_s, 0.0))
    top_s = full(jnp.where(col < plan.cls_col, top_s, 0.0))
    side_s = full(jnp.where(col == plan.cls_col, edge, 0.0))
    lane = iota((1, 128), 1)
    picks = [(top, top_s), (side, side_s), (corner, corner_s)]
    tail = jnp.zeros((1, 128), f32)
    for i, (a, b) in enumerate(picks):
        tail = jnp.where(lane == i, jnp.where(is_large, a, b), tail)
    tail_ref[h] = tail


def fold_lines(plan, large_ref, small_ref, tail_ref, is_large):
    gl, heads, span = plan.gl, plan.heads, plan.strip_l
    odd = (iota((1, span), 1) + span - 1) % span // gl % 2
    lines = [None, None]
    for i in reversed(range(gl)):
        row = large_ref[:, i, :]
        for parity in range(2):
            want = parity if i else 1 - parity
            part = jnp.where(odd == want, row, 0.0)
            if lines[parity] is not None:
                part = part + pltpu.roll(lines[parity], span - 1, axis=1)
            lines[parity] = part
    small = None
    for i in reversed(range(16)):
        part = small_ref[:, i, :]
        small = part if small is None else part + pltpu.roll(small, plan.strip_s - 1, axis=1)
    small = jnp.concatenate([small, jnp.zeros((heads, plan.line - plan.strip_s), f32)], axis=1)
    line = jnp.where(is_large, jnp.concatenate(lines, axis=1), small)
    tail = tail_ref[:, 0, :]
    line = jnp.concatenate([line, tail], axis=1)
    return jnp.concatenate([line, jnp.zeros((16 - heads, plan.lanes), f32)], axis=0)


class Sum:
    sems = 9

    def __init__(self, spot, grad, out, row, cut, bufs, ss, rs, base):
        self.spot, self.grad = spot, grad
        self.out = out
        self.row, self.cut = row, cut
        self.acc, self.got_x, self.got_y, self.got_z, self.total, self.got_f = bufs
        half, core, side, level, levels = spot.half, spot.core, spot.side, spot.level, spot.levels
        q, part = 16, 48
        rows = lambda first, size: pl.ds(pl.multiple_of(first, 16), size)
        self.rows = rows
        self.plane = rows(half * q, 2 * q)
        self.mine = rows(half * 2 * q, q)
        self.own = rows(core * part, part)
        self.sent = self.joined = False

        def copy(idx, src, dst, device):
            return send(src, dst, ss.at[base + idx], rs.at[base + idx], device)

        acc = self.acc
        self.c = copy(0, grad.at[:, :, rows((1 - core) * part, part)], acc, spot.sibling())
        self.x = copy(1, acc.at[:, :, rows((1 - half) * 2 * q, q)], self.got_x, spot.across())
        self.y = copy(2, acc.at[:, 1 - side, self.plane], self.got_y, spot.beside())
        self.z = []
        for step in range(1, levels):
            src = acc.at[(level + step) % levels, side, self.plane]
            self.z.append(copy(4 + step, src, self.got_z.at[step - 1], spot.along(step)))
        self.f = copy(3, self.total, self.got_f, spot.across())
        mine = out.at[rows(row + core * part, part), cut]
        self.last = copy(4, mine, mine, spot.sibling())

    @staticmethod
    def buffers(levels, cols):
        shapes = [
            (levels, 2, 48, cols),
            (levels, 2, 16, cols),
            (levels, 32, cols),
            (levels - 1, 32, cols),
            (32, cols),
            (32, cols),
        ]
        return [pltpu.VMEM(shape, bf16) for shape in shapes]

    def start(self):
        self.c.start()

    def free(self):
        self.join()
        if not self.sent:
            self.c.wait_send()
            self.sent = True

    def stage(self, k):
        getattr(self, ("go", "after_x", "after_y", "after_z", "after_f", "after_last")[k])()

    def join(self):
        if self.joined:
            return
        self.joined = True
        self.c.wait_recv()

        @pl.loop(0, self.acc.shape[0])
        def _(level):
            for side in range(2):
                own = self.grad[level, side, self.own]
                self.acc[level, side] = add16(self.acc[level, side], own)

    def go(self):
        self.join()
        self.x.start()

    def after_x(self):
        self.x.wait_recv()

        @pl.loop(0, self.acc.shape[0])
        def _(level):
            for side in range(2):
                mine = self.acc[level, side, self.mine]
                self.acc[level, side, self.mine] = add16(mine, self.got_x[level, side])

        self.y.start()

    def after_y(self):
        side = self.spot.side
        self.y.wait_recv()

        @pl.loop(0, self.acc.shape[0])
        def _(level):
            mine = self.acc[level, side, self.plane]
            self.acc[level, side, self.plane] = add16(mine, self.got_y[level])

        for copy in self.z:
            copy.start()

    def after_z(self):
        for copy in self.z:
            copy.wait_recv()
        value = self.acc[self.spot.level, self.spot.side, self.plane].astype(f32)
        for k in range(len(self.z)):
            value = value + self.got_z[k].astype(f32)
        self.total[...] = value.astype(bf16)
        self.f.start()

    def after_f(self):
        q, half = 16, self.spot.half
        base = self.row + self.spot.core * 48
        rows = self.rows
        total, got, out, cut = self.total, self.got_f, self.out, self.cut
        self.f.wait_recv()
        out[rows(base + half * 2 * q, q), cut] = total[rows(half * q, q)]
        both = add16(total[rows((1 - half) * q, q)], got[rows(half * q, q)])
        out[rows(base + q, q), cut] = both
        out[rows(base + (1 - half) * 2 * q, q), cut] = got[rows((1 - half) * q, q)]
        self.last.start()

    def after_last(self):
        self.last.wait_recv()

    def finish(self):
        self.free()
        for copy in [self.x, self.y, self.f, self.last] + self.z:
            copy.wait_send()


def back_kernel(plan, n, fast, blocks, *refs):
    refs = list(refs)
    take = lambda count: [refs.pop(0) for _ in range(count)]
    kind_ref, cot_ref, vec_ref, lab_ref, colsel_ref, pick_ref = take(6)
    middle_in, branch_in, normed_in, mixed_in, tok_in = take(5)
    act_in, slope_in, qkv_in, probs_in = take(4)
    wt_in, wo_in, we_in, wr_in = take(4)
    out_ref, tok_out = take(2)
    if fast:
        sum_wt, sum_wo, sum_we, sum_wr, small_out = take(5)
    else:
        sum_wt, sum_wo, sum_we, sum_wr, vec_out, be_out, tab_out = take(7)
    ds_out = take(1)[0]
    (
        tile_ref,
        act_ref,
        slope_ref,
        middle_ref,
        feed_ref,
        dsec_ref,
        gwr_ref,
        stage_ref,
        qkv_ref,
        probs_ref,
        pair_ref,
        large_ref,
        strip_ref,
        tail_ref,
        small_ref,
    ) = take(15)
    tile_sems, act_sems, pair_sems, ds_sems, stage_sems = take(5)
    is_large = kind_ref[0] == 1
    heads, rows = plan.heads, plan.rows
    pairs = heads // 2
    width = cot_ref.shape[1]
    spot = Spot(n) if fast else None
    half_ref, dfeed_ref = pair_ref.at[0], pair_ref.at[1]
    branch_ref, late_ref = act_ref.at[0], dfeed_ref
    dtri = [act_ref.at[1 + j] for j in range(3)]
    dmix_ref, tok_ref = slope_ref.at[0], slope_ref.at[1]

    order = []
    for j in range(blocks):
        order += [(wr_in, j), (we_in, j)]
    order += [(wo_in, 0), (wt_in, 0), (wt_in, 1), (wt_in, 2)]
    tiles = []
    for i, (src, j) in enumerate(order):
        if src is wr_in:
            view, dst = src.at[j], tile_ref.at[i % 3].reshape(2, 4 * width // 8, width)
        else:
            view, dst = src.at[:, :, :, pl.ds(j * width, width)], tile_ref.at[i % 3]
        tiles.append(pltpu.make_async_copy(view, dst, tile_sems.at[i % 3]))

    def tile(i):
        tiles[i].wait()
        return tile_ref[i % 3].reshape(width, width)

    def more(i):
        if i + 3 < len(tiles):
            tiles[i + 3].start()

    def fetch(src, dst, idx):
        copy = pltpu.make_async_copy(src, dst, act_sems.at[idx])
        copy.start()
        return copy

    acts = [fetch(act_in.at[j], act_ref.at[j], j) for j in range(blocks)]
    for i in range(3):
        tiles[i].start()
    slopes = [pltpu.make_async_copy(slope_in.at[j], slope_ref.at[j % 2], act_sems.at[blocks + j]) for j in range(blocks)]
    slopes[0].start()
    slopes[1].start()
    base = 2 * blocks
    mid_copy = fetch(middle_in, middle_ref, base)

    jobs, waiting, done = [], [], []
    if fast:
        bufs, (block, got, reps, ss, rs, bss, brs) = refs[: 6 * 12], refs[6 * 12 :]
        peers = [spot.at(f=(spot.f + k) % n) for k in range(1, n)]
        others = [spot.at(rep=(spot.rep + k) % 4) for k in range(1, 4)]
        greet(peers + others, n + 2)

        def push(grad, out, row, cut):
            k = len(jobs)
            job = Sum(spot, grad, out, row, cut, bufs[6 * k : 6 * k + 6], ss, rs, k * Sum.sems)
            jobs.append(job)
            waiting.append([job, 0])
            job.start()
    else:

        def push(grad, out, row, cut):
            if out is sum_wr:
                if row == 0:
                    copy = pltpu.make_async_copy(gwr_ref, out, stage_sems.at[0])
                    copy.start()
                    copy.wait()
                return
            copy = pltpu.make_async_copy(grad, out.at[:, :, :, cut], stage_sems.at[0])
            copy.start()
            copy.wait()

    active = []

    def beat():
        if waiting:
            active.append(waiting.pop(0))
        for job, _ in waiting:
            job.join()
        for entry in list(active):
            entry[0].stage(entry[1])
            entry[1] += 1
            if entry[1] == 6:
                active.remove(entry)

    stage_count = [0]

    def stage(value):
        k = stage_count[0]
        stage_count[0] += 1
        slot = stage_ref.at[k % 2]
        if fast and k >= 2:
            jobs[k - 2 + 4].free()
        slot[...] = value.astype(bf16).reshape(4, 2, width // 8, width)
        return slot

    limit = jnp.where(is_large, plan.large_len, 3 * plan.small_len)
    live = iota((rows, 1), 0) < limit
    grad = jnp.where(live, cot_ref[...].astype(f32), 0.0)
    dfeed_ref[...] = (vec(vec_ref, FEED_SCALE) * grad).astype(bf16)
    d_feed = dfeed_ref[...]
    small_ref[...] = jnp.zeros_like(small_ref)
    small_ref[REDUCE_BIAS : REDUCE_BIAS + 1, 0:width] = rows_sum(d_feed.astype(f32))
    for j in range(blocks):
        acts[j].wait()
        gwr_ref[j] = mm(act_ref[j], d_feed, TN).astype(bf16).reshape(2, 4 * width // 8, width)
    for m in range(blocks):
        push(gwr_ref.at[:, :, pl.ds(96 * m, 96)], sum_wr, 96 * m, slice(0, width))

    mid_copy.wait()
    normal, _ = norm_stats(middle_ref[...])
    second = normal * vec(vec_ref, SECOND_GAIN) + vec(vec_ref, SECOND_SHIFT)
    half_ref[...] = second.astype(bf16)
    be_row = 10
    for j in range(blocks):
        second, d_feed = half_ref[...], dfeed_ref[...]
        wr = tile(2 * j)
        feed = mm(act_ref[j], wr)
        d_act = mm(d_feed, wr, NT)
        more(2 * j)
        slopes[j].wait()
        d_pre = (d_act * slope_ref[j % 2].astype(f32)).astype(bf16)
        if j + 2 < blocks:
            slopes[j + 2].start()
        we = tile(2 * j + 1)
        d_second = mm(d_pre, we, NT)
        more(2 * j + 1)
        if j == 0:
            branch_copy = fetch(branch_in, branch_ref, base + 1)
            feed_ref[...] = feed
            dsec_ref[...] = d_second
        else:
            feed_ref[...] += feed
            dsec_ref[...] += d_second
        small_ref[be_row + j : be_row + j + 1, 0:width] = rows_sum(d_pre.astype(f32))
        beat()
        push(stage(mm(second, d_pre, TN)), sum_we, 0, slice(j * width, (j + 1) * width))

    def pair_loads(p):
        slot = p % 3
        copies = [pltpu.make_async_copy(probs_in.at[pl.ds(2 * p, 2)], probs_ref.at[slot], pair_sems.at[slot, 3])]
        for part in range(3):
            copies.append(
                pltpu.make_async_copy(
                    qkv_in.at[part * pairs + p], qkv_ref.at[slot, part], pair_sems.at[slot, part]
                )
            )
        return copies

    for copy in pair_loads(0):
        copy.start()

    branch_copy.wait()
    feed_out = feed_ref[...] + vec(vec_ref, REDUCE_BIAS)
    middle = middle_ref[...]
    half_ref[...] = (middle + vec(vec_ref, FEED_SCALE) * feed_out).astype(bf16)
    out_copy = fetch(half_ref, out_ref, base)
    grad = jnp.where(live, cot_ref[...].astype(f32), 0.0)
    d_second = dsec_ref[...]
    normal, inv = norm_stats(middle)
    d_middle = grad + norm_back(d_second, vec(vec_ref, SECOND_GAIN), normal, inv)
    d_branch = (vec(vec_ref, ATTEND_SCALE) * d_middle).astype(bf16)

    def note(idx, value):
        small_ref[idx : idx + 1, 0:width] = value

    note(FEED_SCALE, rows_sum(grad * feed_out))
    note(SECOND_GAIN, rows_sum(d_second * normal))
    note(SECOND_SHIFT, rows_sum(d_second))
    note(ATTEND_SCALE, rows_sum(d_middle * branch_ref[...].astype(f32)))
    note(OUTPUT_BIAS, rows_sum(d_branch.astype(f32)))
    dsec_ref[...] = d_middle
    mixed = jnp.concatenate([mixed_in[p] for p in range(pairs)], axis=1)
    push(stage(mm(mixed, d_branch, TN)), sum_wo, 0, slice(0, width))
    dmix_ref[...] = mm(d_branch, tile(2 * blocks), NT).astype(bf16)
    more(2 * blocks)
    late = [fetch(normed_in, late_ref, 0), fetch(tok_in, tok_ref, 1)]
    beat()

    def ds_copy(p):
        slot = p % 3
        return pltpu.make_async_copy(probs_ref.at[slot], ds_out.at[pl.ds(2 * p, 2)], ds_sems.at[slot])

    def pair_back(p):
        slot = p % 3
        for copy in pair_loads(p):
            copy.wait()

        @pl.when(p >= 2)
        def _():
            ds_copy(p - 2).wait()

        @pl.when(p + 1 < pairs)
        def _():
            for copy in pair_loads(p + 1):
                copy.start()

        lanes = pl.ds(pl.multiple_of(128 * p, 128), 128)
        q, k, v = qkv_ref[slot, 0], qkv_ref[slot, 1], qkv_ref[slot, 2]
        do = dmix_ref[:, lanes]
        lower = half_mask(rows)
        prod = do.astype(f32) * mixed_in[p].astype(f32)
        dq, dk, dv = [], [], []
        for t in range(2):
            keep = lower if t == 0 else ~lower
            d_out = jnp.where(keep, do, jnp.zeros_like(do))
            delta = jnp.sum(jnp.where(keep, prod, 0.0), axis=1, keepdims=True)
            d_probs = mm(d_out, v, NT)
            probs = probs_ref[slot, t]
            dv.append(mm(probs, do, TN))
            d_scores = (probs.astype(f32) * (d_probs - delta)).astype(bf16)
            probs_ref[slot, t] = d_scores
            dq.append(mm(d_scores, k))
            dk.append(mm(d_scores, q, TN))
        dtri[0][:, lanes] = (jnp.where(lower, dq[0], dq[1]) * 0.125).astype(bf16)
        dtri[1][:, lanes] = jnp.where(lower, dk[0], dk[1]).astype(bf16)
        dtri[2][:, lanes] = jnp.where(lower, dv[0], dv[1]).astype(bf16)
        ds_copy(p).start()

    for group in range(3):

        @pl.loop(2 * group, 2 * group + 2)
        def _(p):
            pair_back(p)

        beat()

    d_normed = None
    for copy in late:
        copy.wait()
    for j in range(3):
        d_part = dtri[j][...]
        push(stage(mm(late_ref[...], d_part, TN)), sum_wt, 0, slice(j * width, (j + 1) * width))
        w = tile(2 * blocks + 1 + j)
        part = mm(d_part, w, NT)
        d_normed = part if d_normed is None else d_normed + part
        if j != 1:
            note(QUERY_BIAS if j == 0 else VALUE_BIAS, rows_sum(d_part.astype(f32)))
        beat()
    normal, inv = norm_stats(tok_ref[...].astype(f32))
    back = norm_back(d_normed, vec(vec_ref, FIRST_GAIN), normal, inv)
    late_ref[...] = (dsec_ref[...] + back).astype(bf16)
    tok_copy = fetch(late_ref, tok_out, base + 1)
    note(FIRST_GAIN, rows_sum(d_normed * normal))
    note(FIRST_SHIFT, rows_sum(d_normed))

    ds_copy(pairs - 2).wait()
    ds_copy(pairs - 1).wait()

    def ds_load(p):
        slot = p % 2
        return pltpu.make_async_copy(ds_out.at[pl.ds(2 * p, 2)], probs_ref.at[slot], pair_sems.at[slot, 3])

    ds_load(0).start()
    for group in range(3):

        @pl.loop(2 * group, 2 * group + 2)
        def _(p):
            ds_load(p).wait()

            @pl.when(p + 1 < pairs)
            def _():
                ds_load(p + 1).start()

            @pl.loop(0, 2)
            def _(t):
                fold_head(
                    plan,
                    probs_ref.at[p % 2, t],
                    pick_ref,
                    colsel_ref,
                    large_ref,
                    strip_ref,
                    tail_ref,
                    2 * p + t,
                    is_large,
                )

        beat()
    out_copy.wait()
    tok_copy.wait()
    lines = fold_lines(plan, large_ref, strip_ref, tail_ref, is_large)
    line_of = lambda chunk: lines[:, 128 * chunk : 128 * (chunk + 1)]
    buckets = plan.buckets
    d_table = table_from_lines(plan, line_of, lab_ref, buckets)

    if not fast:
        vec_out[...] = small_ref[:, 0:width]
        for j in range(blocks):
            be_out[:, j * width : (j + 1) * width] = small_ref[be_row + j : be_row + j + 1, 0:width]
        tab_out[...] = d_table
        return

    share, bshare = width // n, buckets // n
    wide = blocks * width // n
    per = width // wide
    for f in range(n):
        value = jnp.concatenate(
            [
                d_table[:, f * bshare : (f + 1) * bshare],
                jnp.zeros((16, wide - bshare - share), f32),
                small_ref[:, f * share : (f + 1) * share],
            ],
            axis=1,
        )
        where = f % per * wide
        bias = small_ref[be_row + f // per : be_row + f // per + 1, where : where + wide]
        bias = jnp.broadcast_to(bias, (16, wide))
        block[f] = jnp.where(iota((16, wide), 0) == heads, bias, value)
    small = []
    for k, peer in enumerate(peers):
        dst = (spot.f + k + 1) % n
        small.append(send(block.at[dst], got.at[k], bss.at[k], brs.at[k], peer))
        small[k].start()
    beat()
    value = block[spot.f]
    for k, copy in enumerate(small):
        copy.wait_recv()
        value = value + got[k]
    reps[spot.rep] = value
    second = []
    for k, other in enumerate(others):
        mine = reps.at[spot.rep]
        second.append(send(mine, mine, bss.at[n - 1 + k], brs.at[n - 1 + k], other))
        second[k].start()
    beat()
    for copy in second:
        copy.wait_recv()
    small_out[...] = (reps[0] + reps[1]) + (reps[2] + reps[3])
    while waiting or active:
        beat()
    for job in jobs:
        job.finish()
    for copy in small + second:
        copy.wait_send()


def back(plan, kind, tokens, cot, wholes, vecs, saved, colsel, n, fast):
    labs, normed, mixed, middle, branch, qkv, probs, acts, slopes = saved
    rows, width = tokens.shape
    heads = plan.heads
    pairs = heads // 2
    blocks = acts.shape[0]
    sds = jax.ShapeDtypeStruct
    picks = image_selectors(plan)
    wt, wo, we, wr = wholes
    inputs = [kind, cot, vecs, labs, colsel, picks, middle, branch, normed, mixed, tokens]
    inputs += [acts, slopes, qkv, probs, wt, wo, we, wr]
    in_specs = [pl.BlockSpec(memory_space=pltpu.SMEM)] + [vmem_spec] * 5
    in_specs += [any_spec] * 3 + [vmem_spec] + [any_spec] * 9
    outs = [sds((rows, width), bf16), sds((rows, width), bf16)]
    out_specs = [any_spec] * 2
    if fast:
        outs += [sds(w.shape[2:], bf16) for w in wholes]
        outs += [sds((16, blocks * width // n), f32)]
        out_specs += [vmem_spec] * 5
    else:
        outs += [sds(w.shape, bf16) for w in wholes]
        outs += [sds((16, width), f32), sds((1, blocks * width), f32), sds((16, plan.buckets), f32)]
        out_specs += [any_spec] * 4 + [vmem_spec] * 3
    outs += [sds(probs.shape, bf16)]
    out_specs += [any_spec]
    row_tile = lambda dtype: pltpu.VMEM((rows, width), dtype)
    scratch = [
        pltpu.VMEM((3, 4, 2, width // 8, width), bf16),
        pltpu.VMEM((blocks, rows, width), bf16),
        pltpu.VMEM((2, rows, width), bf16),
        row_tile(f32),
        row_tile(f32),
        row_tile(f32),
        pltpu.VMEM((4, 2, blocks * width // 8, width), bf16),
        pltpu.VMEM((2, 4, 2, width // 8, width), bf16),
        pltpu.VMEM((3, 3, rows, 128), bf16),
        pltpu.VMEM((3, 2, rows, rows), bf16),
        pltpu.VMEM((2, rows, width), bf16),
        pltpu.VMEM((heads, plan.gl, plan.strip_l), f32),
        pltpu.VMEM((heads, 16, plan.strip_s), f32),
        pltpu.VMEM((heads, 1, 128), f32),
        pltpu.VMEM((16, width), f32),
        pltpu.SemaphoreType.DMA((4,)),
        pltpu.SemaphoreType.DMA((2 * blocks + 2,)),
        pltpu.SemaphoreType.DMA((3, 4)),
        pltpu.SemaphoreType.DMA((3,)),
        pltpu.SemaphoreType.DMA((1,)),
    ]
    kernel_params = dict(vmem_limit_bytes=vmem_bytes)
    if fast:
        wide = blocks * width // n
        for _ in range(12):
            scratch += Sum.buffers(n // 2, width)
        scratch += [
            pltpu.VMEM((n, 16, wide), f32),
            pltpu.VMEM((n - 1, 16, wide), f32),
            pltpu.VMEM((4, 16, wide), f32),
            pltpu.SemaphoreType.DMA((12 * Sum.sems,)),
            pltpu.SemaphoreType.DMA((12 * Sum.sems,)),
            pltpu.SemaphoreType.DMA((n + 2,)),
            pltpu.SemaphoreType.DMA((n + 2,)),
        ]
        kernel_params.update(collective_id=2, has_side_effects=True)
    result = pl.pallas_call(
        functools.partial(back_kernel, plan, n, fast, blocks),
        in_specs=in_specs,
        out_specs=out_specs,
        out_shape=outs,
        scratch_shapes=scratch,
        compiler_params=pltpu.CompilerParams(**kernel_params),
        name="back",
    )(*inputs)
    out, token_grad = result[:2]
    if fast:
        return out, token_grad, result[2:6], result[6]
    grads = [g.reshape(-1, g.shape[3]) for g in result[2:6]]
    sums, block = reduce_plain(grads, result[6], result[7], result[8], n)
    return out, token_grad, sums, block


def per_device(
    tokens,
    slot_kinds,
    small_index,
    large_index,
    first_gain,
    first_shift,
    triple_weight,
    query_bias,
    value_bias,
    bias_table,
    output_weight,
    output_bias,
    attend_scale,
    second_gain,
    second_shift,
    expand_weight,
    expand_bias,
    reduce_weight,
    reduce_bias,
    feed_scale,
    cotangent,
):
    _, rows, width = tokens.shape
    heads = bias_table.shape[2]
    buckets = bias_table.shape[1] * lax.axis_size("fsdp")
    plan = Plan(small_index.shape[0], large_index.shape[0], rows, heads, buckets)
    tokens, cotangent = tokens[0], cotangent[0]
    short = [
        first_gain,
        first_shift,
        query_bias,
        value_bias,
        output_bias,
        attend_scale,
        second_gain,
        second_shift,
        reduce_bias,
        feed_scale,
    ]
    n = width // first_gain.shape[1]
    fast = fast_shape(
        lax.axis_size("rep"), n, [w.shape[1] for w in (triple_weight, output_weight, reduce_weight)]
    )
    shards = [w[0] for w in (triple_weight, output_weight, expand_weight, reduce_weight)]
    shorts = short + [expand_bias, bias_table[0]]
    rowsel, colsel = plan.selectors()
    wholes, vecs, be, saved = front(
        plan, slot_kinds, tokens, large_index, rowsel, colsel, n, fast, shorts, shards
    )
    block_output, token_grad, sums, block = back(
        plan, slot_kinds, tokens, cotangent, wholes, vecs, saved, colsel, n, fast
    )
    dwt, dwo, dwe, dwr = sums
    share, bshare = first_gain.shape[1], bias_table.shape[1]
    row = lambda idx: block[idx : idx + 1, block.shape[1] - share :]
    full = lambda value: value.astype(f32)[None]
    return (
        block_output[None],
        token_grad[None],
        row(FIRST_GAIN),
        row(FIRST_SHIFT),
        full(dwt),
        row(QUERY_BIAS),
        row(VALUE_BIAS),
        block[:heads, :bshare].T[None],
        full(dwo),
        row(OUTPUT_BIAS),
        row(ATTEND_SCALE),
        row(SECOND_GAIN),
        row(SECOND_SHIFT),
        full(dwe),
        block[heads : heads + 1],
        full(dwr),
        row(REDUCE_BIAS),
        row(FEED_SCALE),
    )


def solution(mesh):
    rows = P(("rep", "fsdp"), None, None)
    vector = P(None, "fsdp")
    matrix = P(None, "fsdp", None)
    weights = (
        vector,
        vector,
        matrix,
        vector,
        vector,
        matrix,
        matrix,
        vector,
        vector,
        vector,
        vector,
        matrix,
        vector,
        matrix,
        vector,
        vector,
    )
    return jax.shard_map(
        per_device,
        mesh=mesh,
        in_specs=(rows, P(("rep", "fsdp")), P(), P()) + weights + (rows,),
        out_specs=(rows, rows) + weights,
        check_vma=False,
    )
```

time: 929 us -> 225 us (0.24)
  waiting for transfers between devices: 704 us -> 0 us
  Pallas kernels: 121 us -> 205 us
  blocking collectives: 41.1 us -> 0 us
  local copies, waits for them, and re-layouts: 35 us -> 7.66 us
  between operations: 15.5 us -> 1.61 us
    reduce_scatter x4 -> x0, waiting for transfers between devices: 287 us -> none  [reduce_weight_part(): value = lax.psum_scatter(value, 'fsdp', scatter_dimension=0, tiled=True)]
    all_gather x4 -> x0, waiting for transfers between devices: 232 us -> none  [per_device(): gather = lambda value: lax.all_gather(value, 'fsdp', axis=0, tiled=True)]
    psum x2 -> x0, waiting for transfers between devices: 134 us -> none  [the longest x1 84.1 us: per_device(): smalls = lax.psum((smalls, dbe, d_table[:heads]), ('rep', 'fsdp'))]
    pallas_call x7 -> x2, Pallas kernels: 121 us -> 205 us  [the longest x1 118 us: back(): pl.pallas_call(functools.partial(back_kernel, plan, n, fast, blocks), in_...]
    unnamed x12 -> x0, waiting for transfers between devices: 52.4 us -> none
    psum x1 -> x0, blocking collectives: 41.1 us -> none  [per_device(): smalls = lax.psum((smalls, dbe, d_table[:heads]), ('rep', 'fsdp'))]
    gather x1 -> x0, local copies, waits for them, and re-layouts: 18.8 us -> none  [table_labels(): return jnp.where(good, large_index[row, col], -1).reshape(1, plan.lanes)]
  transfers between devices with their start and end apart: 11 -> 0, of which waited for: 11 -> 0; matrix products, arithmetic and copies ran while one was open for 3% -> 0% of each run, Pallas kernels for 9% -> 0%
where the time goes in v3:
time: 225 us; the launch traced here: 221 us
  Pallas kernels  205 us (91%)
  local copies, waits for them, and re-layouts  7.66 us (3%)
  other arithmetic  6.97 us (3%)
    pallas_call x1, Pallas kernels, back(): pl.pallas_call(functools.partial(back_kernel, plan, n, fast, blocks), in_...  118 us
    pallas_call x1, Pallas kernels, front(): pl.pallas_call(functools.partial(front_kernel, plan, n, fast, cuts), in_s...  87.5 us
    broadcast_in_dim x4, other arithmetic, per_device(): full = lambda value: value.astype(f32)[None]  6.97 us

profile of v3, /device:TPU:0, one launch (start us, length us, event | category | flops | bytes accessed | tf_op | source)
XLA Modules:
  0.0 221.2 jit_solution(10774133491870483889)
XLA Ops:
  1.3 1.5 copy.42
  2.8 87.5 %front.1 = (bf16[4,2,96,2304]{3,2,1,0:T(8,128)(2,1)}, bf16[4,2,96,768]{3,2,1,0:T(8,128)(2,1)}, bf16[4,2,96,3072]{3,2,1,0:T(8,128)(2,1)}, bf16[4,2,384,768]{3,2,1...) custom-call(s32[1]{0:T(128)S(6)} %copy.46.refs_0_, ...), custom_call_target="tpu_custom_call" | custom-call | tf_op jit(solution)/shard_map/front/pallas_call | solution.py:719
  90.2 117.5 %back.1 = (bf16[592,768]{1,0:T(8,128)(2,1)}, bf16[592,768]{1,0:T(8,128)(2,1)}, bf16[96,2304]{1,0:T(8,128)(2,1)}, bf16[96,768]{1,0:T(8,128)(2,1)}, bf16[96,3072]{...) custom-call(s32[1]{0:T(128)S(6)} %copy.46.refs_0_, ...), custom_call_target="tpu_custom_call" | custom-call | tf_op jit(solution)/shard_map/back/pallas_call | solution.py:1411
  207.8 0.0 copy-start.2
  207.8 0.0 copy-start.1
  207.8 1.4 slice.45
  209.2 1.6 fusion
  210.8 0.7 slice_bitcast_fusion
  211.5 0.6 copy.43
  212.1 1.6 bitcast_convert_fusion.3
  213.8 2.0 bitcast_convert_fusion.2
  215.8 0.0 copy-start
  215.8 2.3 %bitcast_convert_fusion.1 = f32[1,96,3072]{2,1,0:T(8,128)} fusion(bf16[96,3072]{1,0:T(8,128)(2,1)} %get-tuple-element.58), kind=kLoop, calls=%fused_computation.1 | loop fusion | flops 294912 | bytes 1769472 | tf_op jit(solution)/shard_map/broadcast_in_dim | solution.py:1484
  218.0 0.0 copy-done.2
  218.0 1.1 bitcast_convert_fusion
  219.1 0.0 copy-done.1
  219.1 0.9 copy.47
  220.0 0.0 copy-done
  220.0 0.9 copy.48
Async XLA Ops:
  207.8 10.3 %copy-start.2 = (bf16[384,768]{1,0:T(8,128)(2,1)S(1)}, bf16[384,768]{1,0:T(8,128)(2,1)}, u32[]{:S(2)}) copy-start(bf16[384,768]{1,0:T(8,128)(2,1)} %get-tuple-element.59) | copy-start | bytes 1769476
  207.8 11.3 %copy-start.1 = (bf16[592,768]{1,0:T(8,128)(2,1)S(1)}, bf16[592,768]{1,0:T(8,128)(2,1)}, u32[]{:S(2)}) copy-start(bf16[592,768]{1,0:T(8,128)(2,1)} %get-tuple-element.53) | copy-start | bytes 2727940
  215.8 4.3 %copy-start = (bf16[592,768]{1,0:T(8,128)(2,1)S(1)}, bf16[592,768]{1,0:T(8,128)(2,1)}, u32[]{:S(2)}) copy-start(bf16[592,768]{1,0:T(8,128)(2,1)} %get-tuple-element.54) | copy-start | bytes 2727940

commit v4 on v3

v4 whole, which is shorter than its diff:
```python
import functools

import jax
import jax.numpy as jnp
import numpy as np
from jax import lax
from jax.experimental import pallas as pl
from jax.experimental.pallas import tpu as pltpu
from jax.sharding import PartitionSpec as P

f32 = jnp.float32
bf16 = jnp.bfloat16
norm_eps = 1e-06
neg_fill = -1000000000.0
vmem_bytes = 60 << 20

NN = (((1,), (0,)), ((), ()))
NT = (((1,), (1,)), ((), ()))
TN = (((0,), (0,)), ((), ()))


def mm(left, right, dims=NN):
    return lax.dot_general(left, right, dims, preferred_element_type=f32)


def round_up(value, unit):
    return -(-value // unit) * unit


class Plan:
    def __init__(self, small_len, large_len, rows, heads, buckets):
        self.heads, self.buckets = heads, buckets
        self.rows = rows
        self.small_len, self.large_len = small_len, large_len
        self.gs = int(round((small_len - 1) ** 0.5))
        self.gl = int(round((large_len - 1) ** 0.5))
        gl, gs = self.gl, self.gs
        self.strip_l = round_up(2 * gl * gl, 128)
        self.strip_s = round_up(2 * gs * (2 * gs - 1) + gs, 128)
        self.line = 2 * self.strip_l
        self.lanes = self.line + 128
        self.pad_cols = round_up(2 * gs * gs + 1, 128)
        self.pad_rows = 16 * gs
        self.cls_col = 2 * gs * gs
        self.cls_row = gs

    def place(self, di, dj, limit):
        gl = self.gl
        good = (np.abs(di) < limit) & (np.abs(dj) < limit)
        row = 1 + gl * np.maximum(di, 0) + np.maximum(dj, 0)
        col = 1 + gl * np.maximum(-di, 0) + np.maximum(-dj, 0)
        return np.where(good, row, 0), np.where(good, col, 0), good

    def positions(self):
        gl, gs = self.gl, self.gs
        x = np.arange(self.strip_l)
        rows, cols, goods = [], [], []
        for parity in range(2):
            m = 2 * ((x + gl) // (2 * gl)) if parity == 0 else 2 * (x // (2 * gl)) + 1
            t = x - gl * m
            r, c, g = self.place(gl - m, -t, gl)
            rows.append(r), cols.append(c), goods.append(g)
        large = [np.concatenate(v) for v in (rows, cols, goods)]
        x = np.arange(self.strip_s)
        m = x // (2 * gs)
        t = x - 2 * gs * m - gs
        small = [np.resize(np.zeros(1, v.dtype), self.line) for v in large]
        for dst, src in zip(small, self.place(gs - 1 - m, -t, gs)):
            dst[: self.strip_s] = src
        tail_r, tail_c, tail_g = np.zeros(128, int), np.zeros(128, int), np.zeros(128, bool)
        tail_r[:3], tail_c[:3], tail_g[:3] = (0, 1, 0), (1, 0, 0), True
        out = []
        for base in (large, small):
            out.append([np.concatenate(v) for v in zip(base, (tail_r, tail_c, tail_g))])
        return out

    def selector_arrays(self):
        gs = self.gs
        rows = np.zeros((self.rows, self.pad_rows), np.float32)
        cols = np.zeros((self.pad_cols, self.rows), np.float32)
        for image in range(3):
            for tok in range(self.small_len):
                r = image * self.small_len + tok
                i, j = divmod(tok - 1, gs)
                rows[r, self.cls_row if tok == 0 else 16 * i + j] = 1
                cols[self.cls_col if tok == 0 else 2 * gs * i + j, r] = 1
        return rows, cols

    def selectors(self):
        rows, cols = self.selector_arrays()
        return jnp.asarray(rows, bf16), jnp.asarray(cols, bf16)


def iota(shape, dim):
    return lax.broadcasted_iota(jnp.int32, shape, dim)


def pick_plan(plan):
    out = []
    for r, c, good in plan.positions():
        down = good & ((r - 1) // plan.gl >= (c - 1) // plan.gl)
        key = np.where(down, r, c)
        sub = np.where(down, c, r) - 1
        valid = good.copy()
        valid[plan.line :] = False
        out.append(np.stack([key, sub, down.astype(int), valid.astype(int)]))
    return jnp.asarray(np.concatenate(out), jnp.int32)


def lane_chunks(lanes, size=512):
    return [(low, min(low + size, lanes)) for low in range(0, lanes, size)]


def read_labels(plan, is_large, idx_ref, pick_ref, lab_ref):
    size, gl = idx_ref.shape[0], plan.gl
    across = idx_ref[1 : 1 + gl, :]
    down = idx_ref[:, 1 : 1 + gl].astype(f32).T.astype(jnp.int32)
    sides = []
    for v in (across, down):
        sides += [(v >> 6).astype(f32), (v & 63).astype(f32)]
    sides = jnp.concatenate(sides, axis=0).astype(bf16)
    for low, high in lane_chunks(plan.line):
        lanes, count = slice(low, high), high - low
        key, sub, use_down, valid = [
            jnp.where(is_large, pick_ref[i : i + 1, lanes], pick_ref[4 + i : 5 + i, lanes])
            for i in range(4)
        ]
        hot = jnp.where(iota((size, count), 0) == key, 1.0, 0.0).astype(bf16)
        here = iota((gl, count), 0) == sub
        rows = mm(sides, hot)
        for digit in range(2):
            a = rows[digit * gl : (digit + 1) * gl]
            b = rows[(2 + digit) * gl : (3 + digit) * gl]
            found = jnp.where(here, jnp.where(use_down == 1, b, a), 0.0)
            found = jnp.sum(found, axis=0, keepdims=True).astype(jnp.int32)
            lab_ref[digit : digit + 1, lanes] = jnp.where(valid == 1, found, -1)
    lane = iota((1, 128), 1)
    tail = jnp.where(lane == 0, idx_ref[0:1, 1:2], -1)
    tail = jnp.where(lane == 1, idx_ref[1:2, 0:1], tail)
    tail = jnp.where(lane == 2, idx_ref[0:1, 0:1], tail)
    lab_ref[0:1, plan.line : plan.line + 128] = jnp.where(tail < 0, -1, tail >> 6)
    lab_ref[1:2, plan.line : plan.line + 128] = jnp.where(tail < 0, -1, tail & 63)


def table_lines(plan, tab, lab_ref, line_ref):
    count = tab.shape[1] // 64
    split = jnp.concatenate([tab[:, 64 * i : 64 * (i + 1)] for i in range(count)], axis=0)
    split = split.astype(bf16)
    for low, high in lane_chunks(plan.lanes):
        first, second = lab_ref[0:1, low:high], lab_ref[1:2, low:high]
        hot = jnp.where(iota((64, high - low), 0) == second, 1.0, 0.0).astype(bf16)
        rows = mm(split, hot)
        parts = [jnp.zeros((16, high - low), f32)] * 4
        for i in range(count):
            parts[i % 4] = jnp.where(first == i, rows[16 * i : 16 * (i + 1)], parts[i % 4])
        line_ref[:, low:high] = (parts[0] + parts[1]) + (parts[2] + parts[3])


def table_from_lines(plan, line_of, lab_ref, buckets):
    count = buckets // 64
    total = jnp.zeros((32 * count, 64), f32)
    for chunk in range(plan.lanes // 128):
        lanes = slice(chunk * 128, (chunk + 1) * 128)
        first, second = lab_ref[0:1, lanes], lab_ref[1:2, lanes]
        hot = jnp.where(iota((64, 128), 0) == second, 1.0, 0.0).astype(bf16)
        part = line_of(chunk)
        high = part.astype(bf16)
        low = (part - high.astype(f32)).astype(bf16)
        both = jnp.concatenate([high, low], axis=0)
        stack = [jnp.where(first == i, both, jnp.zeros_like(both)) for i in range(count)]
        total = total + mm(jnp.concatenate(stack, axis=0), hot, NT)
    pieces = []
    for i in range(count):
        pieces.append(total[32 * i : 32 * i + 16] + total[32 * i + 16 : 32 * i + 32])
    return jnp.concatenate(pieces, axis=1)


def segments(plan, is_large, ids):
    n = plan.small_len
    small = jnp.where(ids >= n, 1, 0) + jnp.where(ids >= 2 * n, 1, 0) + jnp.where(ids >= 3 * n, 1, 0)
    return jnp.where(is_large, jnp.where(ids < plan.large_len, 0, 3), small)


def line_of_head(ref, h):
    return jnp.sum(jnp.where(iota((16, 1), 0) == h, ref[...], 0.0), axis=0, keepdims=True)


def large_strip(plan, line):
    gl, span = plan.gl, plan.strip_l
    rolled = []
    for parity in range(2):
        part = jnp.broadcast_to(line[:, parity * span : (parity + 1) * span], (gl, span))
        rolled.append(pltpu.roll(part, 0, axis=1, stride=1, stride_axis=0))
    odd = (iota((1, span), 1) + span - 1) % span // gl % 2
    odd = jnp.where(iota((gl, 1), 0) == 0, 1 - odd, odd)
    strip = jnp.where(odd == 1, rolled[1], rolled[0])
    return jnp.concatenate([strip, strip[:, :128]], axis=1)


def band_move(plan, a):
    return plan.gl * (plan.gl - a)


def small_padded(plan, line, tail):
    gs, span = plan.gs, plan.strip_s
    line = jnp.broadcast_to(line[:, 0:span], (16, span))
    strip = pltpu.roll(line, 0, axis=1, stride=1, stride_axis=0)
    col = iota((1, plan.pad_cols), 1)
    is_col = col == plan.cls_col
    is_row = iota((16, 1), 0) == plan.cls_row
    bands = []
    for i in range(gs):
        move = 2 * gs * (gs - 1 - i) + gs
        band = pltpu.roll(strip, (span - move) % span, axis=1)[:, : plan.pad_cols]
        band = jnp.where(is_col, tail[:, 1:2], band)
        if i == 0:
            edge = jnp.where(is_col, tail[:, 2:3], tail[:, 0:1])
            band = jnp.where(is_row, edge, band)
        bands.append(band)
    return jnp.concatenate(bands, axis=0).astype(bf16)


def small_blocks(plan, line, tail, pick, colsel):
    rows = plan.rows
    wide = round_up(rows, 128)
    cols = mm(small_padded(plan, line, tail), colsel[:, 0:256]).astype(bf16)
    out = []
    for image, ((r0, r1), (l0, _)) in enumerate(image_rows(plan)):
        start = 256 * image
        block = mm(pick[:, start : start + r1 - r0], cols, TN)
        shift = image * plan.small_len - l0
        last = l0 + round_up(shift + plan.small_len, 128)
        if last - l0 > 256:
            block = jnp.concatenate([block, jnp.zeros((r1 - r0, last - l0 - 256), f32)], axis=1)
        if shift:
            block = pltpu.roll(block, shift, axis=1)
        parts = [block]
        if l0:
            parts.insert(0, jnp.zeros((r1 - r0, l0), f32))
        if last < wide:
            parts.append(jnp.zeros((r1 - r0, wide - last), f32))
        out.append((r0, r1, jnp.concatenate(parts, axis=1)))
    return out


def bias_head(plan, is_large, line_ref, pick, colsel, h, out_ref):
    gl, rows = plan.gl, plan.rows
    wide = round_up(rows, 128)
    line = line_of_head(line_ref, h)
    tail = line[:, plan.line : plan.line + 128]
    blocks = small_blocks(plan, line, tail, pick, colsel)
    strip = large_strip(plan, line)
    span = strip.shape[1]
    col = iota((1, wide), 1)
    seg_col = segments(plan, is_large, col)
    bands = -(-rows // gl)
    for pair in range(-(-bands // 2)):
        first = 2 * gl * pair
        count = min(2 * gl, rows - first)
        parts = []
        for a in range(2 * pair, 2 * pair + 2):
            if a >= bands:
                continue
            move = band_move(plan, a)
            low = move // 128 * 128
            piece = strip[:, low : min(low + wide + 128, span)]
            if piece.shape[1] < wide + 128:
                piece = jnp.concatenate(
                    [piece, jnp.zeros((gl, wide + 128 - piece.shape[1]), f32)], axis=1
                )
            turn = (wide + 128 - (move - low)) % (wide + 128)
            parts.append((pltpu.roll(piece, turn, axis=1) if turn else piece)[:, :wide])
        block = (jnp.concatenate(parts, axis=0) if len(parts) > 1 else parts[0])[:count]
        row = iota((count, 1), 0) + first
        edge = jnp.where(col[:, :128] == 0, tail[:, 1:2], block[:, :128])
        block = jnp.concatenate([edge, block[:, 128:]], axis=1)
        if first == 0:
            block = jnp.where(row == 0, jnp.where(col == 0, tail[:, 2:3], tail[:, 0:1]), block)
        if first + count > plan.large_len:
            block = jnp.where(row < plan.large_len, block, 0.0)
        small = None
        for r0, r1, value in blocks:
            low, high = max(first, r0), min(first + count, r1)
            if low >= high:
                continue
            part = [value[low - r0 : high - r0]]
            if low > first:
                part.insert(0, jnp.zeros((low - first, wide), f32))
            if high < first + count:
                part.append(jnp.zeros((first + count - high, wide), f32))
            part = jnp.concatenate(part, axis=0) if len(part) > 1 else part[0]
            small = part if small is None else small + part
        block = jnp.where(is_large, block, small)
        block = jnp.where(segments(plan, is_large, row) == seg_col, block, neg_fill)
        out_ref[h, first : first + count, :] = block[:, :rows].astype(bf16)


def norm_stats(values):
    mean = jnp.mean(values, axis=1, keepdims=True)
    centred = values - mean
    var = jnp.mean(centred * centred, axis=1, keepdims=True)
    inv = lax.rsqrt(var + norm_eps)
    return centred * inv, inv


def norm_back(d_out, gain, normal, inv):
    d_normal = d_out * gain
    mean_d = jnp.mean(d_normal, axis=1, keepdims=True)
    mean_dn = jnp.mean(d_normal * normal, axis=1, keepdims=True)
    return inv * (d_normal - mean_d - normal * mean_dn)


def rows_sum(values):
    return jnp.sum(values, axis=0, keepdims=True)


def gelu_parts(v):
    size = jnp.abs(v)
    bell = jnp.exp(-0.5 * v * v)
    t = 1.0 / (1.0 + (0.3275911 * 0.7071067811865476) * size)
    poly = t * (
        0.127414796
        + t * (-0.142248368 + t * (0.7107068705 + t * (-0.7265760135 + t * 0.5307027145)))
    )
    tail = poly * bell
    phi = jnp.where(v < 0, tail, 1.0 - tail)
    return v * phi, phi + v * bell * 0.3989422804014327


BE_ROW = 10
(
    FIRST_GAIN,
    FIRST_SHIFT,
    QUERY_BIAS,
    VALUE_BIAS,
    OUTPUT_BIAS,
    ATTEND_SCALE,
    SECOND_GAIN,
    SECOND_SHIFT,
    REDUCE_BIAS,
    FEED_SCALE,
) = range(10)


def vec(ref, idx):
    return ref[idx : idx + 1, :]


def half_mask(rows):
    return iota((rows, 128), 1) < 64


class Spot:
    def __init__(self, n):
        self.n, self.levels = n, n // 2
        self.rep, self.f = lax.axis_index("rep"), lax.axis_index("fsdp")
        self.half, self.core = self.rep // 2, self.rep % 2
        self.level, self.side = self.f // 2, self.f % 2

    def at(self, rep=None, f=None):
        return {"rep": self.rep if rep is None else rep, "fsdp": self.f if f is None else f}

    def sibling(self):
        return self.at(rep=2 * self.half + 1 - self.core)

    def across(self):
        return self.at(rep=2 * (1 - self.half) + self.core)

    def beside(self):
        return self.at(f=2 * self.level + 1 - self.side)

    def along(self, step):
        return self.at(f=2 * ((self.level + step) % self.levels) + self.side)

    def from_along(self, step, side=None):
        side = self.side if side is None else side
        return 2 * ((self.level + self.levels - step) % self.levels) + side


MESH = pl.DeviceIdType.MESH


def greet(devices, count):
    barrier = pltpu.get_barrier_semaphore()
    for device in devices:
        pl.semaphore_signal(barrier, inc=1, device_id=device, device_id_type=MESH)
    pl.semaphore_wait(barrier, count)


def send(src, dst, send_sem, recv_sem, device):
    return pltpu.make_async_remote_copy(
        src_ref=src,
        dst_ref=dst,
        send_sem=send_sem,
        recv_sem=recv_sem,
        device_id=device,
        device_id_type=MESH,
    )


def fast_shape(reps, n, shard_rows):
    return reps == 4 and n == 8 and all(rows % 96 == 0 for rows in shard_rows)


def spread_block(refs, block_ref):
    *vectors, be_ref, table_ref = refs
    heads, share = table_ref.shape
    lanes = block_ref.shape[1]
    table = jnp.concatenate([table_ref[...].astype(f32), jnp.zeros((16 - heads, share), f32)], axis=0)
    width = vectors[0].shape[1]
    rows = [v[...].astype(f32) for v in vectors]
    rows.append(jnp.zeros((16 - len(rows), width), f32))
    block = jnp.concatenate(
        [table, jnp.zeros((16, lanes - share - width), f32), jnp.concatenate(rows, axis=0)], axis=1
    )
    wide = jnp.broadcast_to(be_ref[...].astype(f32), (16, lanes))
    block_ref[...] = jnp.where(iota((16, lanes), 0) == heads, wide, block).astype(bf16)


smem_spec = pl.BlockSpec(memory_space=pltpu.SMEM)
any_spec = pl.BlockSpec(memory_space=pl.ANY)
vmem_spec = pl.BlockSpec(memory_space=pltpu.VMEM)


def add16(left, right):
    return (left.astype(f32) + right.astype(f32)).astype(bf16)


def gather_plain(shorts, shards, n):
    gather = lambda value, axis: lax.all_gather(value, "fsdp", axis=axis, tiled=True)
    vecs = gather(jnp.concatenate(shorts[:10], axis=0), 1).astype(f32)
    vecs = jnp.pad(vecs, ((0, 6), (0, 0)))
    table = gather(shorts[11], 1)
    table = jnp.pad(table, ((0, 16 - table.shape[0]), (0, 0)))
    return [gather(w, 0) for w in shards], vecs, gather(shorts[10], 1).astype(f32), table


def reduce_plain(grads, vec_sums, be_sums, table_sums, n):
    def whole_sum(value):
        value = lax.psum_scatter(value, "fsdp", scatter_dimension=0, tiled=True)
        return lax.psum(value, "rep")

    sums = lax.psum((vec_sums, be_sums, table_sums), ("rep", "fsdp"))
    me = lax.axis_index("fsdp")
    cut = lambda v: lax.dynamic_slice_in_dim(v, me * (v.shape[1] // n), v.shape[1] // n, axis=1)
    vec_part, be_part, table_part = [cut(v) for v in sums]
    wide = be_part.shape[1]
    space = max(wide - vec_part.shape[1] - table_part.shape[1], 0)
    body = jnp.concatenate([table_part, jnp.zeros((16, space), f32), vec_part], axis=1)
    block = jnp.where(jnp.arange(16)[:, None] == 12, jnp.pad(be_part, ((0, 0), (0, body.shape[1] - wide))), body)
    return [whole_sum(g) for g in grads], block


class Piece:
    sems = 8

    def __init__(self, spot, shard, whole, row, col, cols, ss, rs, base):
        self.level, self.side = spot.level, spot.side
        levels = spot.levels
        part, q = 48, 16
        start = row + spot.core * part
        cut = pl.ds(col, cols)
        rows = lambda first, size: pl.ds(pl.multiple_of(first, 16), size)
        plane = rows(start + spot.half * q, 2 * q)
        outer = rows(start + spot.half * 2 * q, q)
        core_rows = rows(start, part)
        side = spot.side

        def copy(idx, src, dst, device):
            return send(src, dst, ss.at[base + idx], rs.at[base + idx], device)

        own = shard.at[plane, cut]
        here = whole.at[spot.level, side, plane, cut]
        self.local = pltpu.make_async_copy(own, here, ss.at[base + levels + 3])
        self.z = [copy(step - 1, own, here, spot.along(step)) for step in range(1, levels)]
        column = whole.at[:, side, plane, cut]
        self.y = copy(levels - 1, column, column, spot.beside())
        near = whole.at[:, side, outer, cut]
        far = whole.at[:, 1 - side, outer, cut]
        self.x = [
            copy(levels, near, near, spot.across()),
            copy(levels + 1, far, far, spot.across()),
        ]
        done = whole.at[:, :, core_rows, cut]
        self.c = copy(levels + 2, done, done, spot.sibling())

    def start(self):
        self.local.start()
        for copy in self.z:
            copy.start()

    def after_z(self):
        self.local.wait()
        for copy in self.z:
            copy.wait_recv()
        self.y.start()
        self.x[0].start()

    def after_y(self):
        self.y.wait_recv()
        self.x[1].start()

    def after_x(self):
        self.x[0].wait_recv()
        self.x[1].wait_recv()
        self.c.start()

    def after_c(self):
        self.c.wait_recv()

    def finish(self):
        for copy in self.z + [self.y, self.c] + self.x:
            copy.wait_send()


def piece_cuts(shard_shapes):
    cuts = []
    for idx, (rows, cols) in enumerate(shard_shapes):
        for row in range(0, rows, 96):
            tile = 384 if idx == 0 else 768
            for col in range(0, cols, tile):
                cuts.append((idx, row, col, tile))
    return cuts


def image_rows(plan):
    out = []
    for image in range(3):
        first, last = image * plan.small_len, (image + 1) * plan.small_len
        rows = (first // 16 * 16, round_up(last, 16))
        lanes = (first // 128 * 128, min(round_up(last, 128), plan.rows))
        out.append((rows, lanes))
    return out


def image_selectors(plan):
    rows, _ = plan.selector_arrays()
    out = []
    for image, ((low, high), _) in enumerate(image_rows(plan)):
        part = rows.copy()
        part[: image * plan.small_len] = 0
        part[(image + 1) * plan.small_len :] = 0
        out.append(np.pad(part[low:high].T, ((0, 0), (0, 256 - (high - low)))))
    return jnp.asarray(np.concatenate(out, axis=1), bf16)


def fold_head(plan, ds_ref, pick, colsel, large_ref, small_ref, tail_ref, h, is_large):
    gl, gs, rows = plan.gl, plan.gs, plan.rows
    wide = round_up(rows, 128)
    width = plan.strip_l + 128
    bands = -(-rows // gl)
    total = jnp.zeros((gl, width), f32)
    side = jnp.zeros((2 * gl, 128), f32)
    for pair in range(-(-bands // 2)):
        first = 2 * gl * pair
        count = min(2 * gl, rows - first)
        block = ds_ref[first : first + count, :].astype(f32)
        block = jnp.concatenate([block, jnp.zeros((count, wide - rows), f32)], axis=1)
        if count < 2 * gl:
            block = jnp.concatenate([block, jnp.zeros((2 * gl - count, wide), f32)], axis=0)
        if pair == 0:
            row = iota((2 * gl, 1), 0)
            top_row = jnp.where(row == 0, block, 0.0)
            block = jnp.where(row == 0, 0.0, block)
        side = side + block[:, :128]
        block = jnp.concatenate(
            [jnp.where(iota((1, 128), 1) == 0, 0.0, block[:, :128]), block[:, 128:]], axis=1
        )
        for half in range(2):
            a = 2 * pair + half
            if a >= bands:
                continue
            move = band_move(plan, a)
            low = move // 128 * 128
            piece = block[half * gl : (half + 1) * gl]
            if move > low:
                piece = jnp.concatenate([piece, jnp.zeros((gl, 128), f32)], axis=1)
                piece = pltpu.roll(piece, move - low, axis=1)
            piece = piece[:, : width - low]
            high = low + piece.shape[1]
            parts = [total[:, low:high] + piece]
            if low:
                parts.insert(0, total[:, :low])
            if high < width:
                parts.append(total[:, high:])
            total = jnp.concatenate(parts, axis=1) if len(parts) > 1 else parts[0]
    large_ref[h] = jnp.concatenate(
        [total[:, :128] + total[:, plan.strip_l :], total[:, 128 : plan.strip_l]], axis=1
    )
    lane = iota((1, wide), 1)
    full = lambda v: jnp.sum(jnp.sum(v, axis=0, keepdims=True), axis=1, keepdims=True)
    corner = full(jnp.where(lane == 0, top_row, 0.0))
    top = full(jnp.where(lane == 0, 0.0, top_row))
    side = full(jnp.where(iota((1, 128), 1) == 0, side, 0.0))

    gathered = jnp.zeros((plan.pad_rows, 256), f32)
    for image, ((r0, r1), (l0, l1)) in enumerate(image_rows(plan)):
        block = ds_ref[r0:r1, l0:l1]
        shift = image * plan.small_len - l0
        if shift:
            pad = round_up(l1 - l0, 128) - (l1 - l0)
            block = block.astype(f32)
            if pad:
                block = jnp.concatenate([block, jnp.zeros((r1 - r0, pad), f32)], axis=1)
            block = pltpu.roll(block, block.shape[1] - shift, axis=1)[:, :256].astype(bf16)
        start = 256 * image
        gathered = gathered + mm(pick[:, start : start + r1 - r0], block)
    high = gathered.astype(bf16)
    low = (gathered - high.astype(f32)).astype(bf16)
    select = colsel[:, 0:256]
    padded = mm(high, select, NT) + mm(low, select, NT)
    span = plan.strip_s
    col = iota((1, plan.pad_cols), 1)
    row = iota((16, 1), 0)
    acc = jnp.zeros((16, span), f32)
    edge = jnp.zeros((16, plan.pad_cols), f32)
    for i in range(gs):
        band = padded[16 * i : 16 * (i + 1)]
        if i == 0:
            top_s = jnp.where(row == plan.cls_row, band, 0.0)
            band = jnp.where(row == plan.cls_row, 0.0, band)
        edge = edge + band
        band = jnp.where(col < plan.cls_col, band, 0.0)
        band = jnp.concatenate([band, jnp.zeros((16, span - plan.pad_cols), f32)], axis=1)
        acc = acc + pltpu.roll(band, 2 * gs * (gs - 1 - i) + gs, axis=1)
    small_ref[h] = acc
    corner_s = full(jnp.where(col == plan.cls_col, top_s, 0.0))
    top_s = full(jnp.where(col < plan.cls_col, top_s, 0.0))
    side_s = full(jnp.where(col == plan.cls_col, edge, 0.0))
    lane = iota((1, 128), 1)
    picks = [(top, top_s), (side, side_s), (corner, corner_s)]
    tail = jnp.zeros((1, 128), f32)
    for i, (a, b) in enumerate(picks):
        tail = jnp.where(lane == i, jnp.where(is_large, a, b), tail)
    tail_ref[h] = tail


def fold_lines(plan, large_ref, small_ref, tail_ref, is_large):
    gl, heads, span = plan.gl, plan.heads, plan.strip_l
    odd = (iota((1, span), 1) + span - 1) % span // gl % 2
    lines = [None, None]
    for i in reversed(range(gl)):
        row = large_ref[:, i, :]
        for parity in range(2):
            want = parity if i else 1 - parity
            part = jnp.where(odd == want, row, 0.0)
            if lines[parity] is not None:
                part = part + pltpu.roll(lines[parity], span - 1, axis=1)
            lines[parity] = part
    small = None
    for i in reversed(range(16)):
        part = small_ref[:, i, :]
        small = part if small is None else part + pltpu.roll(small, plan.strip_s - 1, axis=1)
    small = jnp.concatenate([small, jnp.zeros((heads, plan.line - plan.strip_s), f32)], axis=1)
    line = jnp.where(is_large, jnp.concatenate(lines, axis=1), small)
    tail = tail_ref[:, 0, :]
    line = jnp.concatenate([line, tail], axis=1)
    return jnp.concatenate([line, jnp.zeros((16 - heads, plan.lanes), f32)], axis=0)


class Sum:
    sems = 9

    def __init__(self, spot, grad, out, row, cut, bufs, ss, rs, base):
        self.spot, self.grad = spot, grad
        self.out = out
        self.row, self.cut = row, cut
        self.acc, self.got_x, self.got_y, self.got_z, self.total, self.got_f = bufs
        half, core, side, level, levels = spot.half, spot.core, spot.side, spot.level, spot.levels
        q, part = 16, 48
        rows = lambda first, size: pl.ds(pl.multiple_of(first, 16), size)
        self.rows = rows
        self.plane = rows(half * q, 2 * q)
        self.mine = rows(half * 2 * q, q)
        self.own = rows(core * part, part)
        self.sent = self.joined = False

        def copy(idx, src, dst, device):
            return send(src, dst, ss.at[base + idx], rs.at[base + idx], device)

        acc = self.acc
        self.c = copy(0, grad.at[:, :, rows((1 - core) * part, part)], acc, spot.sibling())
        self.x = copy(1, acc.at[:, :, rows((1 - half) * 2 * q, q)], self.got_x, spot.across())
        self.y = copy(2, acc.at[:, 1 - side, self.plane], self.got_y, spot.beside())
        self.z = []
        for step in range(1, levels):
            src = acc.at[(level + step) % levels, side, self.plane]
            self.z.append(copy(4 + step, src, self.got_z.at[step - 1], spot.along(step)))
        self.f = copy(3, self.total, self.got_f, spot.across())
        mine = out.at[rows(row + core * part, part), cut]
        self.last = copy(4, mine, mine, spot.sibling())

    @staticmethod
    def buffers(levels, cols):
        shapes = [
            (levels, 2, 48, cols),
            (levels, 2, 16, cols),
            (levels, 32, cols),
            (levels - 1, 32, cols),
            (32, cols),
            (32, cols),
        ]
        return [pltpu.VMEM(shape, bf16) for shape in shapes]

    def start(self):
        self.c.start()

    def free(self):
        self.join()
        if not self.sent:
            self.c.wait_send()
            self.sent = True

    def stage(self, k):
        getattr(self, ("go", "after_x", "after_y", "after_z", "after_f", "after_last")[k])()

    def join(self):
        if self.joined:
            return
        self.joined = True
        self.c.wait_recv()

        @pl.loop(0, self.acc.shape[0])
        def _(level):
            for side in range(2):
                own = self.grad[level, side, self.own]
                self.acc[level, side] = add16(self.acc[level, side], own)

    def go(self):
        self.join()
        self.x.start()

    def after_x(self):
        self.x.wait_recv()

        @pl.loop(0, self.acc.shape[0])
        def _(level):
            for side in range(2):
                mine = self.acc[level, side, self.mine]
                self.acc[level, side, self.mine] = add16(mine, self.got_x[level, side])

        self.y.start()

    def after_y(self):
        side = self.spot.side
        self.y.wait_recv()

        @pl.loop(0, self.acc.shape[0])
        def _(level):
            mine = self.acc[level, side, self.plane]
            self.acc[level, side, self.plane] = add16(mine, self.got_y[level])

        for copy in self.z:
            copy.start()

    def after_z(self):
        for copy in self.z:
            copy.wait_recv()
        value = self.acc[self.spot.level, self.spot.side, self.plane].astype(f32)
        for k in range(len(self.z)):
            value = value + self.got_z[k].astype(f32)
        self.total[...] = value.astype(bf16)
        self.f.start()

    def after_f(self):
        q, half = 16, self.spot.half
        base = self.row + self.spot.core * 48
        rows = self.rows
        total, got, out, cut = self.total, self.got_f, self.out, self.cut
        self.f.wait_recv()
        out[rows(base + half * 2 * q, q), cut] = total[rows(half * q, q)]
        both = add16(total[rows((1 - half) * q, q)], got[rows(half * q, q)])
        out[rows(base + q, q), cut] = both
        out[rows(base + (1 - half) * 2 * q, q), cut] = got[rows((1 - half) * q, q)]
        self.last.start()

    def after_last(self):
        self.last.wait_recv()

    def finish(self):
        self.free()
        for copy in [self.x, self.y, self.f, self.last] + self.z:
            copy.wait_send()


ADMIT, HOLD = 2, 2


class Queue:
    def __init__(self):
        self.waiting, self.active, self.beats, self.last = [], [], 0, -9

    def add(self, job):
        self.waiting.append([job, 0])
        job.start()

    def beat(self, hold=None):
        hold = HOLD if hold is None else hold
        self.beats += 1
        for entry in self.waiting:
            if entry[1] >= hold - 1:
                entry[0].join()
            entry[1] += 1
        for entry in list(self.active):
            entry[1] += 1
            if entry[1] >= hold:
                entry[1] = 0
                entry[2] += 1
                entry[0].stage(entry[2])
                if entry[2] == 5:
                    self.active.remove(entry)
        admit = ADMIT if hold > 1 else 1
        if self.waiting and self.waiting[0][0].joined and self.beats - self.last >= admit:
            self.last = self.beats
            job, _ = self.waiting.pop(0)
            self.active.append([job, 0, 0])
            job.stage(0)

    def drain(self):
        while self.waiting or self.active:
            self.beat(1)


def layer_kernel(plan, n, fast, cuts, blocks, *refs):
    refs = list(refs)
    take = lambda count: [refs.pop(0) for _ in range(count)]
    kind_ref, tok_in, cot_in, idx_in, pick_ref, colsel_ref, image_ref = take(7)
    if fast:
        shorts, shards = take(12), take(4)
    else:
        vec_in, be_in, tab_in = take(3)
        wholes = take(4)
    out_ref, tok_out = take(2)
    sum_wt, sum_wo, sum_we, sum_wr = take(4)
    if fast:
        (small_out,) = take(1)
        wholes = take(4)
    else:
        vec_out, be_out, tab_out = take(3)
    normed_out, branch_out, qkv_out, probs_out, slope_out, ds_out = take(6)
    vec_ref, be_ref, lab_ref, act_ref, slope_ref, middle_ref, pair_ref, mixed_ref, small_ref = take(9)
    load_sems, save_sems, tile_sems, slope_sems, late_sems, pair_sems, ds_sems, stage_sems = take(8)
    wt_in, wo_in, we_in, wr_in = wholes
    is_large = kind_ref[0] == 1
    heads, rows = plan.heads, plan.rows
    pairs = heads // 2
    width = tok_in.shape[1]
    eighth = width // 8
    matrix = lambda ref: ref[...].reshape(width, width)
    half_ref, dfeed_ref = pair_ref.at[0], pair_ref.at[1]
    branch_ref, late_ref, cot_ref = act_ref.at[0], dfeed_ref, act_ref.at[1]
    dtri = [act_ref.at[1 + j] for j in range(3)]
    dmix_ref, tok_ref = slope_ref.at[0], slope_ref.at[1]

    def fetch(src, dst, sem):
        copy = pltpu.make_async_copy(src, dst, sem)
        copy.start()
        return copy

    saves = []

    def save(src, dst):
        copy = fetch(src, dst, save_sems.at[len(saves)])
        saves.append(copy)
        return copy

    queue = Queue()
    jobs, pieces = [], []
    if fast:
        bufs = take(6 * (blocks + blocks + 4))
        short, shorts_got, block, got, reps = take(5)
        gss, grs, ass, ars, rss, rrs, bss, brs = take(8)
        spot = Spot(n)
        peers = [spot.at(f=(spot.f + k) % n) for k in range(1, n)]
        others = [spot.at(rep=(spot.rep + k) % 4) for k in range(1, 4)]
        greet(peers + others, n + 2)
        for idx, row, col, cols in cuts:
            base = len(pieces) * Piece.sems
            pieces.append(Piece(spot, shards[idx], wholes[idx], row, col, cols, gss, grs, base))
        spread_block(shorts, short)
        small = []
        for k, peer in enumerate(peers):
            small.append(send(short, shorts_got.at[spot.f], ass.at[k], ars.at[k], peer))
            small[k].start()
        pieces[0].start()
        pieces[1].start()
        shorts_got[spot.f] = short[...]


    def forward(line_ref, heads_ref, qkv_ref, wt_ref, wo_ref, we_ref, idx_ref, tok, normed_ref):
        idx_copy = fetch(idx_in, idx_ref, late_sems.at[0])
        tok_copy = fetch(tok_in, tok, late_sems.at[1])
        loads = []
        for src, ref, span in zip((wt_in, wo_in, we_in), (wt_ref, wo_ref, we_ref), (384, width, width)):
            for col in range(0, src.shape[3], span):
                dst = ref.at[col // width, :, :, :, pl.ds(col % width, span)]
                view = src.at[:, :, :, pl.ds(col, span)]
                loads.append(pltpu.make_async_copy(view, dst, load_sems.at[len(loads)]))
        wt_loads, wo_load, we_loads = loads[: 6], loads[6], loads[7:]
        if not fast:
            for load in loads:
                load.start()

        def step(k):
            gather_step(k)
            if fast and 0 <= k - 3 < len(loads):
                loads[k - 3].start()

        idx_copy.wait()
        read_labels(plan, is_large, idx_ref, pick_ref, lab_ref)
        if fast:
            for copy in small:
                copy.wait()
            share, bshare = shorts[0].shape[1], shorts[11].shape[1]
            tab = []
            for f in range(n):
                part = shorts_got[f].astype(f32)
                wide = part.shape[1]
                vec_ref[:, f * share : (f + 1) * share] = part[:, wide - share :]
                tab.append(part[:, :bshare])
                be_ref[:, f * wide : (f + 1) * wide] = part[heads : heads + 1, :]
            tab = jnp.concatenate(tab, axis=1)
        else:
            vec_ref[...] = vec_in[...]
            be_ref[...] = be_in[...]
            tab = tab_in[...]
        table_lines(plan, tab, lab_ref, line_ref)
        step(0)
        tok_copy.wait()
        normal, _ = norm_stats(tok[...].astype(f32))
        normed = normal * vec(vec_ref, FIRST_GAIN) + vec(vec_ref, FIRST_SHIFT)
        normed_ref[...] = normed.astype(bf16)
        save(normed_ref, normed_out)
        step(1)
        for group in range(heads // 2):

            @pl.loop(2 * group, 2 * group + 2)
            def _(h):
                bias_head(plan, is_large, line_ref, image_ref, colsel_ref, h, heads_ref)

            step(2 + group)

        step(8)
        normed = normed_ref[...]
        for j in range(3):
            wt_loads[2 * j].wait()
            wt_loads[2 * j + 1].wait()
            triple = mm(normed, matrix(wt_ref.at[j]))
            if j == 0:
                triple = triple + vec(vec_ref, QUERY_BIAS)
            if j == 2:
                triple = triple + vec(vec_ref, VALUE_BIAS)
            triple = triple.astype(bf16)
            if j == 0:
                triple = triple * jnp.array(0.125, bf16)
            for p in range(pairs):
                qkv_ref[j * pairs + p] = triple[:, 128 * p : 128 * (p + 1)]
        save(qkv_ref, qkv_out)
        step(9)

        def attend_pair(p):
            q, k, v = qkv_ref[p], qkv_ref[pairs + p], qkv_ref[2 * pairs + p]
            lower = half_mask(rows)
            mixed = []
            for t in range(2):
                keep = lower if t == 0 else ~lower
                scores = mm(jnp.where(keep, q, jnp.zeros_like(q)), k, NT)
                scores = scores + heads_ref[2 * p + t].astype(f32)
                top = jnp.max(scores, axis=1, keepdims=True)
                exps = jnp.exp(scores - top)
                total = jnp.sum(exps, axis=1, keepdims=True)
                probs = (exps * (1.0 / total)).astype(bf16)
                heads_ref[2 * p + t] = probs
                mixed.append(mm(probs, v))
            mixed_ref[p] = jnp.where(lower, mixed[0], mixed[1]).astype(bf16)

        share_of = pairs // 3
        for group in range(3):

            @pl.loop(group * share_of, (group + 1) * share_of)
            def _(p):
                attend_pair(p)

            cut = pl.ds(group * 2 * share_of, 2 * share_of)
            save(heads_ref.at[cut], probs_out.at[cut])
            step(10 + group)

        wo_load.wait()
        mixed = jnp.concatenate([mixed_ref[p] for p in range(pairs)], axis=1)
        branch = mm(mixed, matrix(wo_ref.at[0])) + vec(vec_ref, OUTPUT_BIAS)
        saves[0].wait()
        normed_ref[...] = branch.astype(bf16)
        save(normed_ref, branch_out)
        middle = tok[...].astype(f32) + vec(vec_ref, ATTEND_SCALE) * branch
        middle_ref[...] = middle
        normal, _ = norm_stats(middle)
        second = normal * vec(vec_ref, SECOND_GAIN) + vec(vec_ref, SECOND_SHIFT)
        half_ref[...] = second.astype(bf16)
        slope_saves = []
        for j in range(blocks):
            if j == blocks - 2:
                step(13)
            we_loads[j].wait()
            pre = mm(half_ref[...], matrix(we_ref.at[j])) + be_ref[:, j * width : (j + 1) * width]
            value, slope = gelu_parts(pre)
            act_ref[j] = value.astype(bf16)
            if j >= 2:
                slope_saves[j - 2].wait()
            slope_ref[j % 2] = slope.astype(bf16)
            slope_saves.append(fetch(slope_ref.at[j % 2], slope_out.at[j], slope_sems.at[j % 2]))
        for copy in slope_saves[-2:]:
            copy.wait()
        for copy in saves[1:]:
            copy.wait()

    def gather_step(k):
        for back, action in enumerate(("after_z", "after_y", "after_x", "after_c")):
            if 0 <= k - back < len(pieces):
                getattr(pieces[k - back], action)()
                if back == 0 and k + 2 < len(pieces):
                    pieces[k + 2].start()

    pl.run_scoped(
        forward,
        pltpu.VMEM((16, plan.lanes), f32),
        pltpu.VMEM((heads, rows, rows), bf16),
        pltpu.VMEM((3 * pairs, rows, 128), bf16),
        pltpu.VMEM((3, 4, 2, eighth, width), bf16),
        pltpu.VMEM((1, 4, 2, eighth, width), bf16),
        pltpu.VMEM((blocks, 4, 2, eighth, width), bf16),
        pltpu.VMEM(idx_in.shape, jnp.int32),
        pltpu.VMEM((rows, width), bf16),
        pltpu.VMEM((rows, width), bf16),
    )


    def backward(
        tile_ref, feed_ref, dsec_ref, gwr_ref, stage_ref, qkv_ref, probs_ref, large_ref, strip_ref, tail_ref
    ):
        order = []
        for j in range(blocks):
            order += [(wr_in, j), (we_in, j)]
        order += [(wo_in, 0), (wt_in, 0), (wt_in, 1), (wt_in, 2)]
        tiles = []
        for i, (src, j) in enumerate(order):
            slot = i % 3
            if src is wr_in:
                view, dst = src.at[j], tile_ref.at[slot].reshape(2, 4 * eighth, width)
            else:
                view, dst = src.at[:, :, :, pl.ds(j * width, width)], tile_ref.at[slot]
            tiles.append(pltpu.make_async_copy(view, dst, tile_sems.at[slot]))

        def tile(i):
            tiles[i].wait()
            return matrix(tile_ref.at[i % 3])

        def more(i):
            if i + 3 < len(tiles):
                tiles[i + 3].start()

        def push(grad, out, row, cut):
            if fast:
                k = len(jobs)
                job = Sum(spot, grad, out, row, cut, bufs[6 * k : 6 * k + 6], rss, rrs, k * Sum.sems)
                jobs.append(job)
                queue.add(job)
            elif out is sum_wr:
                if row == 0:
                    fetch(gwr_ref, out, stage_sems.at[0]).wait()
            else:
                dst = out[0] if isinstance(out, tuple) else out.at[:, :, :, cut]
                fetch(grad, dst, stage_sems.at[0]).wait()

        stage_count = [0]

        def stage(value):
            k = stage_count[0]
            stage_count[0] += 1
            slot = stage_ref.at[k % 2]
            if fast and k >= 2:
                jobs[k - 2 + blocks].free()
            slot[...] = value.astype(bf16).reshape(4, 2, eighth, width)
            return slot

        def note(idx, value):
            small_ref[idx : idx + 1, 0:width] = value

        first_cot = stage_ref.at[1].reshape(width, width).at[pl.ds(0, rows)]
        cot_copy = fetch(cot_in, first_cot, late_sems.at[0])
        if fast:
            for i in (1,):
                tiles[i].start()
        else:
            tiles[0].start()
            tiles[1].start()
            tiles[2].start()
        slopes = []
        for j in range(blocks):
            copy = pltpu.make_async_copy(slope_out.at[j], slope_ref.at[j % 2], slope_sems.at[j % 2])
            slopes.append(copy)
        slopes[0].start()
        slopes[1].start()
        limit = jnp.where(is_large, plan.large_len, 3 * plan.small_len)
        live = iota((rows, 1), 0) < limit
        cot_copy.wait()
        grad = jnp.where(live, first_cot[...].astype(f32), 0.0)
        dfeed_ref[...] = (vec(vec_ref, FEED_SCALE) * grad).astype(bf16)
        small_ref[...] = jnp.zeros_like(small_ref)
        note(REDUCE_BIAS, rows_sum(dfeed_ref[...].astype(f32)))
        gather_step(14)
        for j in range(blocks):
            d_feed = dfeed_ref[...]
            value = mm(act_ref[j], d_feed, TN).astype(bf16)
            gwr_ref[j] = value.reshape(2, 4 * eighth, width)
            if j == 1:
                gather_step(15)
        for m in range(blocks):
            push(gwr_ref.at[:, :, pl.ds(eighth * m, eighth)], sum_wr, eighth * m, slice(0, width))
        gather_step(16)
        queue.beat()
        gather_step(17)
        if fast:
            tiles[0].start()
            tiles[2].start()
        for j in range(blocks):
            second, d_feed = half_ref[...], dfeed_ref[...]
            wr = tile(2 * j)
            feed = mm(act_ref[j], wr)
            d_act = mm(d_feed, wr, NT)
            more(2 * j)
            slopes[j].wait()
            d_pre = (d_act * slope_ref[j % 2].astype(f32)).astype(bf16)
            if j + 2 < blocks:
                slopes[j + 2].start()
            queue.beat()
            we = tile(2 * j + 1)
            d_second = mm(d_pre, we, NT)
            more(2 * j + 1)
            if j == 0:
                branch_copy = fetch(branch_out, branch_ref, late_sems.at[1])
                feed_ref[...] = feed
                dsec_ref[...] = d_second
            else:
                feed_ref[...] += feed
                dsec_ref[...] += d_second
            if j == 1:
                cot_copy = fetch(cot_in, cot_ref, late_sems.at[0])
            note(BE_ROW + j, rows_sum(d_pre.astype(f32)))
            push(stage(mm(second, d_pre, TN)), sum_we, 0, slice(j * width, (j + 1) * width))
            queue.beat()

        def pair_loads(p):
            slot = p % 3
            probs = probs_out.at[pl.ds(2 * p, 2)]
            copies = [pltpu.make_async_copy(probs, probs_ref.at[slot], pair_sems.at[slot, 3])]
            for part in range(3):
                src, dst = qkv_out.at[part * pairs + p], qkv_ref.at[slot, part]
                copies.append(pltpu.make_async_copy(src, dst, pair_sems.at[slot, part]))
            return copies

        for copy in pair_loads(0):
            copy.start()

        branch_copy.wait()
        cot_copy.wait()
        feed_out = feed_ref[...] + vec(vec_ref, REDUCE_BIAS)
        middle = middle_ref[...]
        half_ref[...] = (middle + vec(vec_ref, FEED_SCALE) * feed_out).astype(bf16)
        out_copy = fetch(half_ref, out_ref, slope_sems.at[0])
        grad = jnp.where(live, cot_ref[...].astype(f32), 0.0)
        d_second = dsec_ref[...]
        normal, inv = norm_stats(middle)
        d_middle = grad + norm_back(d_second, vec(vec_ref, SECOND_GAIN), normal, inv)
        d_branch = (vec(vec_ref, ATTEND_SCALE) * d_middle).astype(bf16)
        note(FEED_SCALE, rows_sum(grad * feed_out))
        note(SECOND_GAIN, rows_sum(d_second * normal))
        note(SECOND_SHIFT, rows_sum(d_second))
        note(ATTEND_SCALE, rows_sum(d_middle * branch_ref[...].astype(f32)))
        note(OUTPUT_BIAS, rows_sum(d_branch.astype(f32)))
        dsec_ref[...] = d_middle
        dmix_ref[...] = mm(d_branch, tile(2 * blocks), NT).astype(bf16)
        more(2 * blocks)
        mixed = jnp.concatenate([mixed_ref[p] for p in range(pairs)], axis=1)
        push(stage(mm(mixed, d_branch, TN)), sum_wo, 0, slice(0, width))
        late = [fetch(normed_out, late_ref, late_sems.at[0]), fetch(tok_in, tok_ref, late_sems.at[1])]
        queue.beat()

        def ds_copy(p):
            slot = p % 3
            dst = ds_out.at[pl.ds(2 * p, 2)]
            return pltpu.make_async_copy(probs_ref.at[slot], dst, ds_sems.at[slot])

        def pair_back(p):
            slot = p % 3
            for copy in pair_loads(p):
                copy.wait()

            @pl.when(p >= 2)
            def _():
                ds_copy(p - 2).wait()

            @pl.when(p + 1 < pairs)
            def _():
                for copy in pair_loads(p + 1):
                    copy.start()

            lanes = pl.ds(pl.multiple_of(128 * p, 128), 128)
            q, k, v = qkv_ref[slot, 0], qkv_ref[slot, 1], qkv_ref[slot, 2]
            do = dmix_ref[:, lanes]
            lower = half_mask(rows)
            prod = do.astype(f32) * mixed_ref[p].astype(f32)
            dq, dk, dv = [], [], []
            for t in range(2):
                keep = lower if t == 0 else ~lower
                d_out = jnp.where(keep, do, jnp.zeros_like(do))
                delta = jnp.sum(jnp.where(keep, prod, 0.0), axis=1, keepdims=True)
                d_probs = mm(d_out, v, NT)
                probs = probs_ref[slot, t]
                dv.append(mm(probs, do, TN))
                d_scores = (probs.astype(f32) * (d_probs - delta)).astype(bf16)
                probs_ref[slot, t] = d_scores
                dq.append(mm(d_scores, k))
                dk.append(mm(d_scores, q, TN))
            dtri[0][:, lanes] = (jnp.where(lower, dq[0], dq[1]) * 0.125).astype(bf16)
            dtri[1][:, lanes] = jnp.where(lower, dk[0], dk[1]).astype(bf16)
            dtri[2][:, lanes] = jnp.where(lower, dv[0], dv[1]).astype(bf16)
            ds_copy(p).start()

        span = width // 3
        for group in range(3):

            @pl.loop(2 * group, 2 * group + 2)
            def _(p):
                pair_back(p)

                @pl.when(p == 2 * group)
                def _():
                    queue.beat()

            if group == 0:
                for copy in late:
                    copy.wait()
            d_part = [dtri[j][:, group * span : (group + 1) * span] for j in range(3)]
            d_part = jnp.concatenate(d_part, axis=1)
            cut = slice(0, width)
            value = stage(mm(late_ref[...], d_part, TN))
            push(value, sum_wt.at[group] if fast else (sum_wt.at[group],), 0, cut)
            queue.beat()

        d_normed = None
        for j in range(3):
            d_part = dtri[j][...]
            part = mm(d_part, tile(2 * blocks + 1 + j), NT)
            d_normed = part if d_normed is None else d_normed + part
            if j != 1:
                note(QUERY_BIAS if j == 0 else VALUE_BIAS, rows_sum(d_part.astype(f32)))
            if j == 1:
                queue.beat()
        normal, inv = norm_stats(tok_ref[...].astype(f32))
        back = norm_back(d_normed, vec(vec_ref, FIRST_GAIN), normal, inv)
        late_ref[...] = (dsec_ref[...] + back).astype(bf16)
        tok_copy = fetch(late_ref, tok_out, slope_sems.at[1])
        note(FIRST_GAIN, rows_sum(d_normed * normal))
        note(FIRST_SHIFT, rows_sum(d_normed))
        queue.beat()

        ds_copy(pairs - 2).wait()
        ds_copy(pairs - 1).wait()

        def ds_load(p):
            src, slot = ds_out.at[pl.ds(2 * p, 2)], p % 3
            return pltpu.make_async_copy(src, probs_ref.at[slot], pair_sems.at[slot, 3])

        ds_load(0).start()

        @pl.loop(0, pairs)
        def _(p):
            ds_load(p).wait()

            @pl.when(p + 1 < pairs)
            def _():
                ds_load(p + 1).start()

            for t in range(2):
                ds = probs_ref.at[p % 3, t]
                args = (image_ref, colsel_ref, large_ref, strip_ref, tail_ref, 2 * p + t, is_large)
                fold_head(plan, ds, *args)

            for i in range(pairs):

                @pl.when(p == i)
                def _():
                    queue.beat()

        out_copy.wait()
        tok_copy.wait()
        lines = fold_lines(plan, large_ref, strip_ref, tail_ref, is_large)
        line_of = lambda chunk: lines[:, 128 * chunk : 128 * (chunk + 1)]
        buckets = plan.buckets
        d_table = table_from_lines(plan, line_of, lab_ref, buckets)
        if not fast:
            vec_out[...] = small_ref[:, 0:width]
            for j in range(blocks):
                be_out[:, j * width : (j + 1) * width] = small_ref[BE_ROW + j : BE_ROW + j + 1, 0:width]
            tab_out[...] = d_table
            return

        share, bshare = width // n, buckets // n
        wide = blocks * width // n
        per = width // wide
        for f in range(n):
            value = jnp.concatenate(
                [
                    d_table[:, f * bshare : (f + 1) * bshare],
                    jnp.zeros((16, wide - bshare - share), f32),
                    small_ref[:, f * share : (f + 1) * share],
                ],
                axis=1,
            )
            where, row = f % per * wide, BE_ROW + f // per
            bias = jnp.broadcast_to(small_ref[row : row + 1, where : where + wide], (16, wide))
            block[f] = jnp.where(iota((16, wide), 0) == heads, bias, value)
        sums = []
        for k, peer in enumerate(peers):
            dst = (spot.f + k + 1) % n
            sums.append(send(block.at[dst], got.at[k], bss.at[k], brs.at[k], peer))
            sums[k].start()
        queue.beat(1)
        value = block[spot.f]
        for k, copy in enumerate(sums):
            copy.wait_recv()
            value = value + got[k]
        reps[spot.rep] = value
        for k, other in enumerate(others):
            mine = reps.at[spot.rep]
            sums.append(send(mine, mine, bss.at[n - 1 + k], brs.at[n - 1 + k], other))
            sums[-1].start()
        queue.beat(1)
        for copy in sums[n - 1 :]:
            copy.wait_recv()
        small_out[...] = (reps[0] + reps[1]) + (reps[2] + reps[3])
        queue.drain()
        for copy in sums:
            copy.wait_send()
        for job in jobs:
            job.finish()
        for piece in pieces:
            piece.finish()

    pl.run_scoped(
        backward,
        pltpu.VMEM((3, 4, 2, eighth, width), bf16),
        pltpu.VMEM((rows, width), f32),
        pltpu.VMEM((rows, width), f32),
        pltpu.VMEM((4, 2, blocks * eighth, width), bf16),
        pltpu.VMEM((2, 4, 2, eighth, width), bf16),
        pltpu.VMEM((3, 3, rows, 128), bf16),
        pltpu.VMEM((3, 2, rows, rows), bf16),
        pltpu.VMEM((heads, plan.gl, plan.strip_l), f32),
        pltpu.VMEM((heads, 16, plan.strip_s), f32),
        pltpu.VMEM((heads, 1, 128), f32),
    )


def layer(plan, kind, tokens, cot, large_index, n, fast, shorts, shards):
    rows, width = tokens.shape
    heads = plan.heads
    pairs = heads // 2
    sds = jax.ShapeDtypeStruct
    hidden = shards[2].shape[1]
    blocks = hidden // width
    cuts = piece_cuts([w.shape for w in shards]) if fast else []
    colsel = jnp.asarray(plan.selector_arrays()[1], bf16)
    inputs = [kind, tokens, cot, large_index, pick_plan(plan), colsel, image_selectors(plan)]
    in_specs = [smem_spec] + [any_spec] * 3 + [vmem_spec] * 3
    outs, out_specs = [sds((rows, width), bf16)] * 2, [any_spec] * 2
    group = (3, width // 8, width)
    if fast:
        wide = hidden // n
        inputs += shorts + shards
        in_specs += [vmem_spec] * 12 + [any_spec] * 4
        outs += [sds(group, bf16)] + [sds(w.shape, bf16) for w in shards[1:]]
        outs += [sds((16, wide), f32)]
        out_specs += [vmem_spec] * 5
        outs += [sds((4, 2) + w.shape, bf16) for w in shards]
        out_specs += [any_spec] * 4
    else:
        wholes, vecs, be, table = gather_plain(shorts, shards, n)
        wholes = [w.reshape(4, 2, w.shape[0] // 8, w.shape[1]) for w in wholes]
        inputs += [vecs, be, table.astype(f32)] + wholes
        in_specs += [vmem_spec] * 3 + [any_spec] * 4
        outs += [sds((3, 4, 2, width // 8, width), bf16)] + [sds(w.shape, bf16) for w in wholes[1:]]
        outs += [sds((16, width), f32), sds((1, hidden), f32), sds((16, plan.buckets), f32)]
        out_specs += [any_spec] * 4 + [vmem_spec] * 3
    kept = len(outs)
    square = sds((heads, rows, rows), bf16)
    flat = sds((rows, width), bf16)
    outs += [flat, flat, sds((3 * pairs, rows, 128), bf16), square]
    outs += [sds((blocks, rows, width), bf16), square]
    out_specs += [any_spec] * 6
    dma = pltpu.SemaphoreType.DMA
    scratch = [
        pltpu.VMEM((16, width), f32),
        pltpu.VMEM((1, hidden), f32),
        pltpu.VMEM((2, plan.lanes), jnp.int32),
        pltpu.VMEM((blocks, rows, width), bf16),
        pltpu.VMEM((2, rows, width), bf16),
        pltpu.VMEM((rows, width), f32),
        pltpu.VMEM((2, rows, width), bf16),
        pltpu.VMEM((pairs, rows, 128), bf16),
        pltpu.VMEM((16, width), f32),
        dma((7 + blocks,)),
        dma((8,)),
        dma((3,)),
        dma((2,)),
        dma((3,)),
        dma((3, 4)),
        dma((3,)),
        dma((1,)),
    ]
    kernel_params = dict(vmem_limit_bytes=vmem_bytes)
    if fast:
        sums = 2 * blocks + 4
        for _ in range(sums):
            scratch += Sum.buffers(n // 2, width)
        scratch += [
            pltpu.VMEM((16, wide), bf16),
            pltpu.VMEM((n, 16, wide), bf16),
            pltpu.VMEM((n, 16, wide), f32),
            pltpu.VMEM((n - 1, 16, wide), f32),
            pltpu.VMEM((4, 16, wide), f32),
            dma((len(cuts) * Piece.sems,)),
            dma((len(cuts) * Piece.sems,)),
            dma((n - 1,)),
            dma((n - 1,)),
            dma((sums * Sum.sems,)),
            dma((sums * Sum.sems,)),
            dma((n + 2,)),
            dma((n + 2,)),
        ]
        kernel_params.update(collective_id=1, has_side_effects=True)
    result = pl.pallas_call(
        functools.partial(layer_kernel, plan, n, fast, cuts, blocks),
        in_specs=in_specs,
        out_specs=out_specs,
        out_shape=outs,
        scratch_shapes=scratch,
        compiler_params=pltpu.CompilerParams(**kernel_params),
        name="layer",
    )(*inputs)[:kept]
    out, token_grad, wt = result[:3]
    if fast:
        return out, token_grad, result[2:6], result[6]
    wt = wt.reshape(3, width, 3, width // 3).transpose(1, 2, 0, 3).reshape(width, 3 * width)
    grads = [wt] + [g.reshape(-1, g.shape[3]) for g in result[3:6]]
    sums, block = reduce_plain(grads, *result[6:9], n)
    wt = sums[0].reshape(-1, 3, 3, width // 3).transpose(2, 0, 1, 3).reshape(3, -1, width)
    return out, token_grad, [wt] + sums[1:], block


def per_device(
    tokens,
    slot_kinds,
    small_index,
    large_index,
    first_gain,
    first_shift,
    triple_weight,
    query_bias,
    value_bias,
    bias_table,
    output_weight,
    output_bias,
    attend_scale,
    second_gain,
    second_shift,
    expand_weight,
    expand_bias,
    reduce_weight,
    reduce_bias,
    feed_scale,
    cotangent,
):
    _, rows, width = tokens.shape
    heads = bias_table.shape[2]
    buckets = bias_table.shape[1] * lax.axis_size("fsdp")
    plan = Plan(small_index.shape[0], large_index.shape[0], rows, heads, buckets)
    tokens, cotangent = tokens[0], cotangent[0]
    short = [
        first_gain,
        first_shift,
        query_bias,
        value_bias,
        output_bias,
        attend_scale,
        second_gain,
        second_shift,
        reduce_bias,
        feed_scale,
    ]
    n = width // first_gain.shape[1]
    fast = fast_shape(
        lax.axis_size("rep"), n, [w.shape[1] for w in (triple_weight, output_weight, reduce_weight)]
    )
    shards = [w[0] for w in (triple_weight, output_weight, expand_weight, reduce_weight)]
    shorts = short + [expand_bias, bias_table[0].T]
    block_output, token_grad, sums, block = layer(
        plan, slot_kinds, tokens, cotangent, large_index, n, fast, shorts, shards
    )
    return wrap(block_output, token_grad, sums, block, first_gain.shape[1], bias_table.shape[1:])


def wrap_kernel(share, heads, out_in, tok_in, wt_in, wo_in, we_in, wr_in, block_ref, *outs):
    (
        out,
        tok,
        first_gain,
        first_shift,
        triple_weight,
        query_bias,
        value_bias,
        bias_table,
        output_weight,
        output_bias,
        attend_scale,
        second_gain,
        second_shift,
        expand_weight,
        expand_bias,
        reduce_weight,
        reduce_bias,
        feed_scale,
    ) = outs
    out[0] = out_in[...]
    tok[0] = tok_in[...]
    groups, _, width = wt_in.shape
    span = width // groups
    for g in range(groups):
        for part in range(3):
            value = wt_in[g, :, part * span : (part + 1) * span].astype(f32)
            triple_weight[0, :, part * width + g * span : part * width + (g + 1) * span] = value
    output_weight[0] = wo_in[...].astype(f32)
    expand_weight[0] = we_in[...].astype(f32)
    reduce_weight[0] = wr_in[...].astype(f32)
    first = block_ref.shape[1] - share
    rows = {
        FIRST_GAIN: first_gain,
        FIRST_SHIFT: first_shift,
        QUERY_BIAS: query_bias,
        VALUE_BIAS: value_bias,
        OUTPUT_BIAS: output_bias,
        ATTEND_SCALE: attend_scale,
        SECOND_GAIN: second_gain,
        SECOND_SHIFT: second_shift,
        REDUCE_BIAS: reduce_bias,
        FEED_SCALE: feed_scale,
    }
    for idx, ref in rows.items():
        ref[...] = block_ref[idx : idx + 1, first:]
    expand_bias[...] = block_ref[heads : heads + 1, :]
    for h in range(heads):
        bias_table[h] = block_ref[h : h + 1, : bias_table.shape[2]]


def wrap(block_output, token_grad, sums, block, share, table_shape):
    wt, wo, we, wr = sums
    sds = jax.ShapeDtypeStruct
    vector = sds((1, share), f32)
    whole_of = lambda w: sds((1,) + w.shape, f32)
    bshare, heads = table_shape
    triple = sds((1, wt.shape[1], 3 * wt.shape[2]), f32)
    outs = [sds((1,) + block_output.shape, bf16)] * 2
    outs += [vector, vector, triple, vector, vector, sds((heads, 1, bshare), f32)]
    outs += [whole_of(wo)] + [vector] * 4 + [whole_of(we), sds((1, block.shape[1]), f32)]
    outs += [whole_of(wr), vector, vector]
    result = pl.pallas_call(
        functools.partial(wrap_kernel, share, heads),
        in_specs=[vmem_spec] * 7,
        out_specs=[vmem_spec] * 18,
        out_shape=outs,
        compiler_params=pltpu.CompilerParams(vmem_limit_bytes=vmem_bytes),
        name="wrap",
    )(block_output, token_grad, wt, wo, we, wr, block)
    result = list(result)
    result[7] = result[7].transpose(1, 2, 0)
    return tuple(result)


def solution(mesh):
    rows = P(("rep", "fsdp"), None, None)
    vector = P(None, "fsdp")
    matrix = P(None, "fsdp", None)
    weights = (
        vector,
        vector,
        matrix,
        vector,
        vector,
        matrix,
        matrix,
        vector,
        vector,
        vector,
        vector,
        matrix,
        vector,
        matrix,
        vector,
        vector,
    )
    return jax.shard_map(
        per_device,
        mesh=mesh,
        in_specs=(rows, P(("rep", "fsdp")), P(), P()) + weights + (rows,),
        out_specs=(rows, rows) + weights,
        check_vma=False,
    )
```

time: 225 us -> 202 us (0.90)
  local copies, waits for them, and re-layouts: 7.66 us -> 0 us
  Pallas kernels: 205 us -> 198 us
  other arithmetic: 6.97 us -> 0 us
    pallas_call x2, Pallas kernels: 205 us -> 198 us  [the longest x1 193 us: layer(): pl.pallas_call(functools.partial(layer_kernel, plan, n, fast, cuts, block...]
    broadcast_in_dim x4 -> x0, other arithmetic: 6.97 us -> none  [per_device(): full = lambda value: value.astype(f32)[None]]
    unnamed x10 -> x0, local copies, waits for them, and re-layouts: 3.94 us -> none
    slice x2 -> x0, local copies, waits for them, and re-layouts: 2.98 us -> none  [the longest x1 1.59 us: per_device(): row = lambda idx: block[idx:idx + 1, block.shape[1] - share:]]
where the time goes in v4:
time: 202 us; the launch traced here: 199 us
  Pallas kernels  198 us (98%)
    pallas_call x1, Pallas kernels, layer(): pl.pallas_call(functools.partial(layer_kernel, plan, n, fast, cuts, block...  193 us
    pallas_call x1, Pallas kernels, wrap(): pl.pallas_call(functools.partial(wrap_kernel, share, heads), in_specs=[vm...  4.47 us

profile of v4, /device:TPU:0, one launch (start us, length us, event | category | flops | bytes accessed | tf_op | source)
XLA Modules:
  0.0 199.2 jit_solution(4703279831160411071)
XLA Ops:
  1.3 193.2 %layer.1 = (bf16[592,768]{1,0:T(8,128)(2,1)}, bf16[592,768]{1,0:T(8,128)(2,1)}, bf16[3,96,768]{2,1,0:T(8,128)(2,1)}, bf16[96,768]{1,0:T(8,128)(2,1)}, bf16[96,30...) custom-call(s32[1]{0:T(128)S(6)} %copy.41.refs_0_, ...), custom_call_target="tpu_custom_call" | custom-call | tf_op jit(solution)/shard_map/layer/pallas_call | solution.py:1442
  194.6 4.5 %wrap.1 = (bf16[1,592,768]{2,1,0:T(8,128)(2,1)}, bf16[1,592,768]{2,1,0:T(8,128)(2,1)}, f32[1,96]{1,0:T(1,128)}, f32[1,96]{1,0:T(1,128)}, f32[1,96,2304]{2,1,0:T(...) custom-call(bf16[592,768]{1,0:T(8,128)(2,1)} %get-tuple-element.43.o, ...), custom_call_target="tpu_custom_call" | custom-call | tf_op jit(solution)/shard_map/wrap/pallas_call | solution.py:1576

commit v5 on v4

--- a/solution.py
+++ b/solution.py
@@ -12,7 +12,7 @@
 bf16 = jnp.bfloat16
 norm_eps = 1e-06
 neg_fill = -1000000000.0
-vmem_bytes = 60 << 20
+vmem_bytes = 62 << 20
 
 NN = (((1,), (0,)), ((), ()))
 NT = (((1,), (1,)), ((), ()))
@@ -317,7 +317,9 @@
 def gelu_parts(v):
     size = jnp.abs(v)
     bell = jnp.exp(-0.5 * v * v)
-    t = 1.0 / (1.0 + (0.3275911 * 0.7071067811865476) * size)
+    below = 1.0 + (0.3275911 * 0.7071067811865476) * size
+    t = pl.reciprocal(below, approx=True)
+    t = t * (2.0 - below * t)
     poly = t * (
         0.127414796
         + t * (-0.142248368 + t * (0.7107068705 + t * (-0.7265760135 + t * 0.5307027145)))
@@ -380,11 +382,14 @@
 MESH = pl.DeviceIdType.MESH
 
 
-def greet(devices, count):
-    barrier = pltpu.get_barrier_semaphore()
+def greet(devices):
     for device in devices:
+        barrier = pltpu.get_barrier_semaphore()
         pl.semaphore_signal(barrier, inc=1, device_id=device, device_id_type=MESH)
-    pl.semaphore_wait(barrier, count)
+
+
+def met(count):
+    pl.semaphore_wait(pltpu.get_barrier_semaphore(), count)
 
 
 def send(src, dst, send_sem, recv_sem, device):
@@ -452,37 +457,47 @@
 
 
 class Piece:
-    sems = 8
-
-    def __init__(self, spot, shard, whole, row, col, cols, ss, rs, base):
-        self.level, self.side = spot.level, spot.side
+    sems = 6
+
+    def __init__(self, spot, shard, whole, row, col, cols, sent, rs, base):
+        self.size = cols // 384
         levels = spot.levels
         part, q = 48, 16
         start = row + spot.core * part
-        cut = pl.ds(col, cols)
+        cut = slice(col, col + cols)
         rows = lambda first, size: pl.ds(pl.multiple_of(first, 16), size)
         plane = rows(start + spot.half * q, 2 * q)
         outer = rows(start + spot.half * 2 * q, q)
         core_rows = rows(start, part)
         side = spot.side
 
-        def copy(idx, src, dst, device):
-            return send(src, dst, ss.at[base + idx], rs.at[base + idx], device)
+        def copy(idx, kind, src, dst, device):
+            return send(src, dst, sent.at[kind], rs.at[base + idx], device)
 
         own = shard.at[plane, cut]
         here = whole.at[spot.level, side, plane, cut]
-        self.local = pltpu.make_async_copy(own, here, ss.at[base + levels + 3])
-        self.z = [copy(step - 1, own, here, spot.along(step)) for step in range(1, levels)]
+        self.local = pltpu.make_async_copy(own, here, rs.at[base + 5])
+        self.z = [copy(0, 0, own, here, spot.along(step)) for step in range(1, levels)]
+        three = whole.at[0 : levels - 1, 0, 0 : 2 * q, cut]
+        self.z_all = pltpu.make_async_copy(three, three, rs.at[base])
         column = whole.at[:, side, plane, cut]
-        self.y = copy(levels - 1, column, column, spot.beside())
+        self.y = copy(1, 1, column, column, spot.beside())
         near = whole.at[:, side, outer, cut]
         far = whole.at[:, 1 - side, outer, cut]
-        self.x = [
-            copy(levels, near, near, spot.across()),
-            copy(levels + 1, far, far, spot.across()),
+        self.x = [copy(2, 2, near, near, spot.across()), copy(3, 2, far, far, spot.across())]
+        done = whole.at[:, :, core_rows, cut]
+        self.c = copy(4, 3, done, done, spot.sibling())
+
+    @staticmethod
+    def sent_waits(levels, whole, sent):
+        part = whole.shape[2] // 96
+        views = [
+            whole.at[0 : levels - 1, 0, 0 : 32 * part],
+            whole.at[:, 0, 0 : 32 * part],
+            whole.at[:, :, 0 : 16 * part],
+            whole.at[:, :, 0 : 48 * part],
         ]
-        done = whole.at[:, :, core_rows, cut]
-        self.c = copy(levels + 2, done, done, spot.sibling())
+        return [pltpu.make_async_copy(v, v, sent.at[kind]) for kind, v in enumerate(views)]
 
     def start(self):
         self.local.start()
@@ -491,8 +506,7 @@
 
     def after_z(self):
         self.local.wait()
-        for copy in self.z:
-            copy.wait_recv()
+        self.z_all.wait()
         self.y.start()
         self.x[0].start()
 
@@ -508,18 +522,16 @@
     def after_c(self):
         self.c.wait_recv()
 
-    def finish(self):
-        for copy in self.z + [self.y, self.c] + self.x:
-            copy.wait_send()
-
 
 def piece_cuts(shard_shapes):
     cuts = []
     for idx, (rows, cols) in enumerate(shard_shapes):
         for row in range(0, rows, 96):
-            tile = 384 if idx == 0 else 768
-            for col in range(0, cols, tile):
-                cuts.append((idx, row, col, tile))
+            starts = list(range(0, cols, 384))
+            if idx == 0:
+                starts = starts[0::2] + starts[1::2]
+            for col in starts:
+                cuts.append((idx, row, col, 384))
     return cuts
 
 
@@ -659,46 +671,52 @@
 
 
 class Sum:
-    sems = 9
-
-    def __init__(self, spot, grad, out, row, cut, bufs, ss, rs, base):
-        self.spot, self.grad = spot, grad
-        self.out = out
+    sems = 6
+    outer = 16
+
+    def __init__(self, spot, grad, out, row, cut, bufs, sent, c_sem, rs, base):
+        self.spot, self.grad, self.out = spot, grad, out
         self.row, self.cut = row, cut
         self.acc, self.got_x, self.got_y, self.got_z, self.total, self.got_f = bufs
         half, core, side, level, levels = spot.half, spot.core, spot.side, spot.level, spot.levels
-        q, part = 16, 48
+        q, part = self.outer, self.acc.shape[2]
+        self.middle = m = part - 2 * q
         rows = lambda first, size: pl.ds(pl.multiple_of(first, 16), size)
         self.rows = rows
-        self.plane = rows(half * q, 2 * q)
-        self.mine = rows(half * 2 * q, q)
+        self.plane = rows(half * q, q + m)
+        self.mine = rows(half * (q + m), q)
         self.own = rows(core * part, part)
         self.sent = self.joined = False
 
         def copy(idx, src, dst, device):
-            return send(src, dst, ss.at[base + idx], rs.at[base + idx], device)
+            out_sem = sent.at[idx] if idx else c_sem
+            return send(src, dst, out_sem, rs.at[base + idx], device)
 
         acc = self.acc
-        self.c = copy(0, grad.at[:, :, rows((1 - core) * part, part)], acc, spot.sibling())
-        self.x = copy(1, acc.at[:, :, rows((1 - half) * 2 * q, q)], self.got_x, spot.across())
+        other = rows((1 - core) * part, part)
+        self.c = copy(0, grad.at[:, :, other, cut[0]], acc, spot.sibling())
+        self.x = copy(1, acc.at[:, :, rows((1 - half) * (q + m), q)], self.got_x, spot.across())
         self.y = copy(2, acc.at[:, 1 - side, self.plane], self.got_y, spot.beside())
         self.z = []
         for step in range(1, levels):
             src = acc.at[(level + step) % levels, side, self.plane]
-            self.z.append(copy(4 + step, src, self.got_z.at[step - 1], spot.along(step)))
+            self.z.append(copy(5, src, self.got_z.at[step - 1], spot.along(step)))
+        self.z_all = pltpu.make_async_copy(self.got_z, self.got_z, rs.at[base + 5])
         self.f = copy(3, self.total, self.got_f, spot.across())
-        mine = out.at[rows(row + core * part, part), cut]
+        mine = out.at[rows(row + core * part, part), cut[1]]
         self.last = copy(4, mine, mine, spot.sibling())
 
-    @staticmethod
-    def buffers(levels, cols):
+    @classmethod
+    def buffers(cls, levels, shard_rows, cols):
+        part = shard_rows // 2
+        kept = part - cls.outer
         shapes = [
-            (levels, 2, 48, cols),
-            (levels, 2, 16, cols),
-            (levels, 32, cols),
-            (levels - 1, 32, cols),
-            (32, cols),
-            (32, cols),
+            (levels, 2, part, cols),
+            (levels, 2, cls.outer, cols),
+            (levels, kept, cols),
+            (levels - 1, kept, cols),
+            (kept, cols),
+            (kept, cols),
         ]
         return [pltpu.VMEM(shape, bf16) for shape in shapes]
 
@@ -723,7 +741,7 @@
         @pl.loop(0, self.acc.shape[0])
         def _(level):
             for side in range(2):
-                own = self.grad[level, side, self.own]
+                own = self.grad[level, side, self.own, self.cut[0]]
                 self.acc[level, side] = add16(self.acc[level, side], own)
 
     def go(self):
@@ -754,8 +772,7 @@
             copy.start()
 
     def after_z(self):
-        for copy in self.z:
-            copy.wait_recv()
+        self.z_all.wait()
         value = self.acc[self.spot.level, self.spot.side, self.plane].astype(f32)
         for k in range(len(self.z)):
             value = value + self.got_z[k].astype(f32)
@@ -763,27 +780,29 @@
         self.f.start()
 
     def after_f(self):
-        q, half = 16, self.spot.half
-        base = self.row + self.spot.core * 48
+        q, m, half = self.outer, self.middle, self.spot.half
+        base = self.row + self.spot.core * self.acc.shape[2]
         rows = self.rows
-        total, got, out, cut = self.total, self.got_f, self.out, self.cut
+        total, got, out, cut = self.total, self.got_f, self.out, self.cut[1]
         self.f.wait_recv()
-        out[rows(base + half * 2 * q, q), cut] = total[rows(half * q, q)]
-        both = add16(total[rows((1 - half) * q, q)], got[rows(half * q, q)])
-        out[rows(base + q, q), cut] = both
-        out[rows(base + (1 - half) * 2 * q, q), cut] = got[rows((1 - half) * q, q)]
+        out[rows(base + half * (q + m), q), cut] = total[rows(half * m, q)]
+        both = add16(total[rows((1 - half) * q, m)], got[rows(half * q, m)])
+        out[rows(base + q, m), cut] = both
+        out[rows(base + (1 - half) * (q + m), q), cut] = got[rows((1 - half) * m, q)]
         self.last.start()
 
     def after_last(self):
         self.last.wait_recv()
 
-    def finish(self):
-        self.free()
-        for copy in [self.x, self.y, self.f, self.last] + self.z:
-            copy.wait_send()
-
-
-ADMIT, HOLD = 2, 2
+    @classmethod
+    def sent_rows(cls, levels, shard_rows):
+        part = shard_rows // 2
+        kept = part - cls.outer
+        return [2 * levels * cls.outer, levels * kept, kept, part, (levels - 1) * kept]
+
+
+ADMIT, HOLD = 1, 3
+HIDDEN_BLOCKS = 3
 
 
 class Queue:
@@ -821,7 +840,7 @@
             self.beat(1)
 
 
-def layer_kernel(plan, n, fast, cuts, blocks, *refs):
+def layer_kernel(plan, n, fast, cuts, sum_shapes, *refs):
     refs = list(refs)
     take = lambda count: [refs.pop(0) for _ in range(count)]
     kind_ref, tok_in, cot_in, idx_in, pick_ref, colsel_ref, image_ref = take(7)
@@ -837,20 +856,21 @@
         wholes = take(4)
     else:
         vec_out, be_out, tab_out = take(3)
-    normed_out, branch_out, qkv_out, probs_out, slope_out, ds_out = take(6)
-    vec_ref, be_ref, lab_ref, act_ref, slope_ref, middle_ref, pair_ref, mixed_ref, small_ref = take(9)
-    load_sems, save_sems, tile_sems, slope_sems, late_sems, pair_sems, ds_sems, stage_sems = take(8)
+    normed_out, branch_out, qkv_out, probs_out, ds_out = take(5)
+    vec_ref, be_ref, lab_ref, middle_ref, pair_ref, mixed_ref, small_ref, dbe_ref = take(8)
+    rows_ref, cols_ref = take(2)
+    load_sems, save_sems, tile_sems, late_sems, pair_sems, ds_sems, stage_sems = take(7)
     wt_in, wo_in, we_in, wr_in = wholes
     is_large = kind_ref[0] == 1
     heads, rows = plan.heads, plan.rows
     pairs = heads // 2
     width = tok_in.shape[1]
     eighth = width // 8
+    hidden = wr_in.shape[2] * 8
+    unit = hidden // 8 // HIDDEN_BLOCKS
+    tile_cols = 8 * unit
     matrix = lambda ref: ref[...].reshape(width, width)
     half_ref, dfeed_ref = pair_ref.at[0], pair_ref.at[1]
-    branch_ref, late_ref, cot_ref = act_ref.at[0], dfeed_ref, act_ref.at[1]
-    dtri = [act_ref.at[1 + j] for j in range(3)]
-    dmix_ref, tok_ref = slope_ref.at[0], slope_ref.at[1]
 
     def fetch(src, dst, sem):
         copy = pltpu.make_async_copy(src, dst, sem)
@@ -867,50 +887,112 @@
     queue = Queue()
     jobs, pieces = [], []
     if fast:
-        bufs = take(6 * (blocks + blocks + 4))
+        bufs = take(6 * len(sum_shapes))
+        sum_kinds = sorted(set(sum_shapes))
         short, shorts_got, block, got, reps = take(5)
-        gss, grs, ass, ars, rss, rrs, bss, brs = take(8)
+        gss, grs, ass, ars, rss, css, rrs, bss, brs = take(9)
         spot = Spot(n)
         peers = [spot.at(f=(spot.f + k) % n) for k in range(1, n)]
         others = [spot.at(rep=(spot.rep + k) % 4) for k in range(1, 4)]
-        greet(peers + others, n + 2)
+        greet(peers + others)
         for idx, row, col, cols in cuts:
             base = len(pieces) * Piece.sems
-            pieces.append(Piece(spot, shards[idx], wholes[idx], row, col, cols, gss, grs, base))
+            at = GATHER_ORDER[idx]
+            args = (row, col, cols, gss.at[at], grs, base)
+            pieces.append(Piece(spot, shards[at], wholes[at], *args))
+        formed = []
+        for j in range(HIDDEN_BLOCKS):
+            formed.append((rows_ref, sum_wr, j * unit, 0))
+            formed.append((cols_ref, sum_we, 0, j * tile_cols))
+        formed.append((rows_ref, sum_wo, 0, 0))
+        for j in range(3):
+            formed.append((rows_ref, sum_wt, 0, j * width))
+        counts = {}
+        for ring, out, row, col in formed:
+            k = counts[id(ring)] = counts.get(id(ring), -1) + 1
+            cols = ring.shape[4] // 2
+            for first in (0, cols):
+                i = len(jobs)
+                cut = (slice(first, first + cols), slice(col + first, col + first + cols))
+                kind = sum_kinds.index(sum_shapes[i])
+                args = (bufs[6 * i : 6 * i + 6], rss.at[kind], css.at[i], rrs, i * Sum.sems)
+                jobs.append(Sum(spot, ring.at[k % 2], out, row, cut, *args))
         spread_block(shorts, short)
         small = []
         for k, peer in enumerate(peers):
             small.append(send(short, shorts_got.at[spot.f], ass.at[k], ars.at[k], peer))
-            small[k].start()
+
+    def set_out():
+        met(n + 2)
+        for copy in small:
+            copy.start()
         pieces[0].start()
-        pieces[1].start()
         shorts_got[spot.f] = short[...]
 
-
-    def forward(line_ref, heads_ref, qkv_ref, wt_ref, wo_ref, we_ref, idx_ref, tok, normed_ref):
+    events = []
+    for i in range(len(pieces)):
+        for kind, lag in enumerate((0,) + LAGS):
+            events.append((i + lag, kind, i))
+    events.sort()
+    gone = [0]
+    whole_at = {i: pos for pos, (_, kind, i) in enumerate(events) if kind == 3}
+    on_whole = []
+
+    def run_event():
+        _, kind, i = events[gone[0]]
+        gone[0] += 1
+        getattr(pieces[i], ("after_z", "after_y", "after_x", "after_c")[kind])()
+        if kind == 0:
+            for ahead in (range(2, AHEAD + 1) if i == 0 else (i + AHEAD,)):
+                if ahead < len(pieces):
+                    pieces[ahead].start()
+        if kind == 3:
+            for call in on_whole:
+                call(i)
+
+    now = [-1]
+
+    def step(count=1):
+        now[0] += count
+        while gone[0] < len(events) and events[gone[0]][0] <= now[0]:
+            run_event()
+
+    def gather_until(piece):
+        while events and gone[0] <= whole_at[min(piece, len(pieces) - 1)]:
+            step()
+
+
+    def forward(line_ref, heads_ref, qkv_ref, wt_ref, wo_ref, idx_ref, tok, normed_ref):
         idx_copy = fetch(idx_in, idx_ref, late_sems.at[0])
         tok_copy = fetch(tok_in, tok, late_sems.at[1])
         loads = []
-        for src, ref, span in zip((wt_in, wo_in, we_in), (wt_ref, wo_ref, we_ref), (384, width, width)):
-            for col in range(0, src.shape[3], span):
-                dst = ref.at[col // width, :, :, :, pl.ds(col % width, span)]
-                view = src.at[:, :, :, pl.ds(col, span)]
+        for src, ref in ((wt_in, wt_ref), (wo_in, wo_ref)):
+            starts = range(0, src.shape[3], width // 2)
+            for col in list(starts[0::2]) + list(starts[1::2]):
+                first = col % width
+                dst = ref.at[col // width, :, :, :, first : first + width // 2]
+                view = src.at[:, :, :, col : col + width // 2]
                 loads.append(pltpu.make_async_copy(view, dst, load_sems.at[len(loads)]))
-        wt_loads, wo_load, we_loads = loads[: 6], loads[6], loads[7:]
         if not fast:
             for load in loads:
                 load.start()
 
-        def step(k):
-            gather_step(k)
-            if fast and 0 <= k - 3 < len(loads):
-                loads[k - 3].start()
-
+        def begin(i):
+            if i < len(loads):
+                loads[i].start()
+
+        on_whole.append(begin)
         idx_copy.wait()
         read_labels(plan, is_large, idx_ref, pick_ref, lab_ref)
         if fast:
+            set_out()
+        tok_copy.wait()
+        normal, _ = norm_stats(tok[...].astype(f32))
+        if fast:
+            pieces[1].start()
             for copy in small:
                 copy.wait()
+            step()
             share, bshare = shorts[0].shape[1], shorts[11].shape[1]
             tab = []
             for f in range(n):
@@ -925,38 +1007,34 @@
             be_ref[...] = be_in[...]
             tab = tab_in[...]
         table_lines(plan, tab, lab_ref, line_ref)
-        step(0)
-        tok_copy.wait()
-        normal, _ = norm_stats(tok[...].astype(f32))
+        step()
         normed = normal * vec(vec_ref, FIRST_GAIN) + vec(vec_ref, FIRST_SHIFT)
         normed_ref[...] = normed.astype(bf16)
         save(normed_ref, normed_out)
-        step(1)
         for group in range(heads // 2):
 
             @pl.loop(2 * group, 2 * group + 2)
             def _(h):
                 bias_head(plan, is_large, line_ref, image_ref, colsel_ref, h, heads_ref)
 
-            step(2 + group)
-
-        step(8)
-        normed = normed_ref[...]
-        for j in range(3):
-            wt_loads[2 * j].wait()
-            wt_loads[2 * j + 1].wait()
-            triple = mm(normed, matrix(wt_ref.at[j]))
-            if j == 0:
-                triple = triple + vec(vec_ref, QUERY_BIAS)
-            if j == 2:
-                triple = triple + vec(vec_ref, VALUE_BIAS)
-            triple = triple.astype(bf16)
-            if j == 0:
-                triple = triple * jnp.array(0.125, bf16)
-            for p in range(pairs):
-                qkv_ref[j * pairs + p] = triple[:, 128 * p : 128 * (p + 1)]
-        save(qkv_ref, qkv_out)
-        step(9)
+            step()
+        def project(group):
+            low, high = group * width // 2, (group + 1) * width // 2
+            normed = normed_ref[...]
+            gather_until(3 * group + 2)
+            for j in range(3):
+                loads[3 * group + j].wait()
+                triple = mm(normed, wt_ref[j, :, :, :, low:high].reshape(width, width // 2))
+                if j == 0:
+                    triple = triple + vec_ref[QUERY_BIAS : QUERY_BIAS + 1, low:high]
+                if j == 2:
+                    triple = triple + vec_ref[VALUE_BIAS : VALUE_BIAS + 1, low:high]
+                triple = triple.astype(bf16)
+                if j == 0:
+                    triple = triple * jnp.array(0.125, bf16)
+                for p in range(pairs // 2):
+                    where = j * pairs + group * (pairs // 2) + p
+                    qkv_ref[where] = triple[:, 128 * p : 128 * (p + 1)]
 
         def attend_pair(p):
             q, k, v = qkv_ref[p], qkv_ref[pairs + p], qkv_ref[2 * pairs + p]
@@ -974,18 +1052,28 @@
                 mixed.append(mm(probs, v))
             mixed_ref[p] = jnp.where(lower, mixed[0], mixed[1]).astype(bf16)
 
-        share_of = pairs // 3
-        for group in range(3):
-
-            @pl.loop(group * share_of, (group + 1) * share_of)
+        for group in range(2):
+            project(group)
+            step()
+
+            @pl.loop(group * pairs // 2, (group + 1) * pairs // 2)
             def _(p):
                 attend_pair(p)
-
-            cut = pl.ds(group * 2 * share_of, 2 * share_of)
-            save(heads_ref.at[cut], probs_out.at[cut])
-            step(10 + group)
-
-        wo_load.wait()
+                for i in range(group * pairs // 2, (group + 1) * pairs // 2):
+
+                    @pl.when(p == i)
+                    def _():
+                        step()
+
+                cut = pl.ds(2 * p, 2)
+                dst = probs_out.at[cut]
+                pltpu.make_async_copy(heads_ref.at[cut], dst, pair_sems.at[0, 3]).start()
+
+        save(qkv_ref, qkv_out)
+
+        gather_until(7)
+        loads[6].wait()
+        loads[7].wait()
         mixed = jnp.concatenate([mixed_ref[p] for p in range(pairs)], axis=1)
         branch = mm(mixed, matrix(wo_ref.at[0])) + vec(vec_ref, OUTPUT_BIAS)
         saves[0].wait()
@@ -996,29 +1084,12 @@
         normal, _ = norm_stats(middle)
         second = normal * vec(vec_ref, SECOND_GAIN) + vec(vec_ref, SECOND_SHIFT)
         half_ref[...] = second.astype(bf16)
-        slope_saves = []
-        for j in range(blocks):
-            if j == blocks - 2:
-                step(13)
-            we_loads[j].wait()
-            pre = mm(half_ref[...], matrix(we_ref.at[j])) + be_ref[:, j * width : (j + 1) * width]
-            value, slope = gelu_parts(pre)
-            act_ref[j] = value.astype(bf16)
-            if j >= 2:
-                slope_saves[j - 2].wait()
-            slope_ref[j % 2] = slope.astype(bf16)
-            slope_saves.append(fetch(slope_ref.at[j % 2], slope_out.at[j], slope_sems.at[j % 2]))
-        for copy in slope_saves[-2:]:
-            copy.wait()
+        gather_until(7)
+        on_whole.pop()
+        step()
+        pltpu.make_async_copy(heads_ref, probs_out, pair_sems.at[0, 3]).wait()
         for copy in saves[1:]:
             copy.wait()
-
-    def gather_step(k):
-        for back, action in enumerate(("after_z", "after_y", "after_x", "after_c")):
-            if 0 <= k - back < len(pieces):
-                getattr(pieces[k - back], action)()
-                if back == 0 and k + 2 < len(pieces):
-                    pieces[k + 2].start()
 
     pl.run_scoped(
         forward,
@@ -1027,287 +1098,335 @@
         pltpu.VMEM((3 * pairs, rows, 128), bf16),
         pltpu.VMEM((3, 4, 2, eighth, width), bf16),
         pltpu.VMEM((1, 4, 2, eighth, width), bf16),
-        pltpu.VMEM((blocks, 4, 2, eighth, width), bf16),
         pltpu.VMEM(idx_in.shape, jnp.int32),
         pltpu.VMEM((rows, width), bf16),
         pltpu.VMEM((rows, width), bf16),
     )
 
 
-    def backward(
-        tile_ref, feed_ref, dsec_ref, gwr_ref, stage_ref, qkv_ref, probs_ref, large_ref, strip_ref, tail_ref
-    ):
-        order = []
-        for j in range(blocks):
-            order += [(wr_in, j), (we_in, j)]
-        order += [(wo_in, 0), (wt_in, 0), (wt_in, 1), (wt_in, 2)]
-        tiles = []
-        for i, (src, j) in enumerate(order):
-            slot = i % 3
-            if src is wr_in:
-                view, dst = src.at[j], tile_ref.at[slot].reshape(2, 4 * eighth, width)
+    def note(idx, value):
+        small_ref[idx : idx + 1, 0:width] = value
+
+    limit = jnp.where(is_large, plan.large_len, 3 * plan.small_len)
+    live = iota((rows, 1), 0) < limit
+
+    def backward(feed_ref, dsec_ref, dtri_ref, lines_ref):
+        used = {"rows": [], "cols": [], "all": 0}
+
+        def push(kind, value, out, row, col):
+            k = used[kind]
+            if fast and len(k) >= 2:
+                for job in k[-2]:
+                    job.free()
+            slot = (rows_ref if kind == "rows" else cols_ref).at[len(k) % 2]
+            shard, cols = value.shape[0] // 8, value.shape[1]
+            slot[:, :, 0:shard, :] = value.astype(bf16).reshape(4, 2, shard, cols)
+            added = []
+            if fast:
+                added = jobs[used["all"] : used["all"] + 2]
+                used["all"] += 2
+                for job in added:
+                    queue.add(job)
             else:
-                view, dst = src.at[:, :, :, pl.ds(j * width, width)], tile_ref.at[slot]
-            tiles.append(pltpu.make_async_copy(view, dst, tile_sems.at[slot]))
-
-        def tile(i):
-            tiles[i].wait()
-            return matrix(tile_ref.at[i % 3])
-
-        def more(i):
-            if i + 3 < len(tiles):
-                tiles[i + 3].start()
-
-        def push(grad, out, row, cut):
-            if fast:
-                k = len(jobs)
-                job = Sum(spot, grad, out, row, cut, bufs[6 * k : 6 * k + 6], rss, rrs, k * Sum.sems)
-                jobs.append(job)
-                queue.add(job)
-            elif out is sum_wr:
-                if row == 0:
-                    fetch(gwr_ref, out, stage_sems.at[0]).wait()
-            else:
-                dst = out[0] if isinstance(out, tuple) else out.at[:, :, :, cut]
-                fetch(grad, dst, stage_sems.at[0]).wait()
-
-        stage_count = [0]
-
-        def stage(value):
-            k = stage_count[0]
-            stage_count[0] += 1
-            slot = stage_ref.at[k % 2]
-            if fast and k >= 2:
-                jobs[k - 2 + blocks].free()
-            slot[...] = value.astype(bf16).reshape(4, 2, eighth, width)
-            return slot
-
-        def note(idx, value):
-            small_ref[idx : idx + 1, 0:width] = value
-
-        first_cot = stage_ref.at[1].reshape(width, width).at[pl.ds(0, rows)]
-        cot_copy = fetch(cot_in, first_cot, late_sems.at[0])
-        if fast:
-            for i in (1,):
-                tiles[i].start()
-        else:
+                view = out.at[:, :, pl.ds(row, shard), pl.ds(col, cols)]
+                fetch(slot.at[:, :, pl.ds(0, shard)], view, stage_sems.at[0]).wait()
+            k.append(added)
+
+        branch_ref, cot_ref = dtri_ref.at[0], dtri_ref.at[1]
+        cot_copy = fetch(cot_in, cot_ref, late_sems.at[0])
+        branch_copy = fetch(branch_out, branch_ref, late_sems.at[1])
+
+        def feed_forward(we_ref, wr_ref, pre_ref, act_ref, slope_ref):
+
+            def we_loads(j):
+                copies = []
+                for f in range(8):
+                    src = we_in.at[:, :, :, pl.ds((f * HIDDEN_BLOCKS + j) * unit, unit)]
+                    dst = we_ref.at[j % 2, :, :, :, pl.ds(f * unit, unit)]
+                    copies.append(pltpu.make_async_copy(src, dst, tile_sems.at[j % 2, f]))
+                return copies
+
+            def wr_load(j):
+                src = wr_in.at[:, :, pl.ds(j * unit, unit)]
+                return pltpu.make_async_copy(src, wr_ref.at[j % 2], tile_sems.at[j % 2, 8])
+
+            gather_until(15)
+            for j in range(2):
+                for copy in we_loads(j):
+                    copy.start()
+            cot_copy.wait()
+            grad = jnp.where(live, cot_ref[...].astype(f32), 0.0)
+            dfeed_ref[...] = (vec(vec_ref, FEED_SCALE) * grad).astype(bf16)
+            small_ref[...] = jnp.zeros_like(small_ref)
+            note(REDUCE_BIAS, rows_sum(dfeed_ref[...].astype(f32)))
+
+            def we_tile(j):
+                return we_ref[j % 2].reshape(width, tile_cols)
+
+            def before(j):
+                for copy in we_loads(j):
+                    copy.wait()
+                bias = []
+                for f in range(8):
+                    first = (f * HIDDEN_BLOCKS + j) * unit
+                    bias.append(be_ref[:, first : first + unit])
+                pre_ref[...] = mm(half_ref[...], we_tile(j)) + jnp.concatenate(bias, axis=1)
+
+            part = 16 * (-(-rows // 64))
+            spans = [(low, min(low + part, rows)) for low in range(0, rows, part)]
+
+            def activate(j, which):
+                low, high = spans[which]
+                value, slope = gelu_parts(pre_ref[low:high, :])
+                act_ref[j % 2, low:high, :] = value.astype(bf16)
+                slope_ref[j % 2, low:high, :] = slope.astype(bf16)
+
+            before(0)
+            for i in range(len(spans)):
+                activate(0, i)
+                step()
+            for j in range(HIDDEN_BLOCKS):
+                ahead = j + 1 < HIDDEN_BLOCKS
+                gather_until(16 + 2 * (((j + 1) * unit - 1) // 96) + 1)
+                wr_load(j).start()
+                if ahead:
+                    before(j + 1)
+                d_feed = dfeed_ref[...]
+                act = act_ref[j % 2]
+                push("rows", mm(act, d_feed, TN), sum_wr, j * unit, 0)
+                if ahead:
+                    activate(j + 1, 0)
+                queue.beat()
+                step()
+                wr_load(j).wait()
+                wr = wr_ref[j % 2].reshape(tile_cols, width)
+                feed = mm(act, wr)
+                feed_ref[...] = feed if j == 0 else feed_ref[...] + feed
+                if ahead:
+                    activate(j + 1, 1)
+                queue.beat()
+                step()
+                d_act = mm(d_feed, wr, NT)
+                d_pre = (d_act * slope_ref[j % 2].astype(f32)).astype(bf16)
+                dbe_ref[j : j + 1, :] = rows_sum(d_pre.astype(f32))
+                if ahead:
+                    activate(j + 1, 2)
+                queue.beat()
+                step()
+                push("cols", mm(half_ref[...], d_pre, TN), sum_we, 0, j * tile_cols)
+                if ahead:
+                    activate(j + 1, 3)
+                queue.beat()
+                step()
+                d_second = mm(d_pre, we_tile(j), NT)
+                dsec_ref[...] = d_second if j == 0 else dsec_ref[...] + d_second
+                if j + 2 < HIDDEN_BLOCKS:
+                    for copy in we_loads(j + 2):
+                        copy.start()
+                queue.beat()
+
+        pl.run_scoped(
+            feed_forward,
+            pltpu.VMEM((2, 4, 2, eighth, tile_cols), bf16),
+            pltpu.VMEM((2, 4, 2, unit, width), bf16),
+            pltpu.VMEM((rows, tile_cols), f32),
+            pltpu.VMEM((2, rows, tile_cols), bf16),
+            pltpu.VMEM((2, rows, tile_cols), bf16),
+        )
+
+        def attention(
+            tile_ref, qkv_ref, probs_ref, dmix_ref, large_ref, strip_ref, tail_ref
+        ):
+            def pair_loads(p):
+                slot = p % 3
+                probs = probs_out.at[pl.ds(2 * p, 2)]
+                copies = [pltpu.make_async_copy(probs, probs_ref.at[slot], pair_sems.at[slot, 3])]
+                for part in range(3):
+                    src, dst = qkv_out.at[part * pairs + p], qkv_ref.at[p % 2, part]
+                    copies.append(pltpu.make_async_copy(src, dst, pair_sems.at[slot, part]))
+                return copies
+
+            tiles = [pltpu.make_async_copy(wo_in, tile_ref.at[0], tile_sems.at[0, 0])]
+            for j in range(3):
+                src = wt_in.at[:, :, :, pl.ds(j * width, width)]
+                slot = (1 + j) % 2
+                tiles.append(pltpu.make_async_copy(src, tile_ref.at[slot], tile_sems.at[slot, 0]))
+
+            def tile(i):
+                tiles[i].wait()
+                return matrix(tile_ref.at[i % 2])
+
             tiles[0].start()
             tiles[1].start()
+            for copy in pair_loads(0):
+                copy.start()
+            branch_copy.wait()
+            feed_out = feed_ref[...] + vec(vec_ref, REDUCE_BIAS)
+            middle = middle_ref[...]
+            half_ref[...] = (middle + vec(vec_ref, FEED_SCALE) * feed_out).astype(bf16)
+            out_copy = fetch(half_ref, out_ref, save_sems.at[0])
+            grad = jnp.where(live, cot_ref[...].astype(f32), 0.0)
+            d_second = dsec_ref[...]
+            normal, inv = norm_stats(middle)
+            d_middle = grad + norm_back(d_second, vec(vec_ref, SECOND_GAIN), normal, inv)
+            d_branch = (vec(vec_ref, ATTEND_SCALE) * d_middle).astype(bf16)
+            queue.beat()
+            note(FEED_SCALE, rows_sum(grad * feed_out))
+            note(SECOND_GAIN, rows_sum(d_second * normal))
+            note(SECOND_SHIFT, rows_sum(d_second))
+            note(ATTEND_SCALE, rows_sum(d_middle * branch_ref[...].astype(f32)))
+            note(OUTPUT_BIAS, rows_sum(d_branch.astype(f32)))
+            dsec_ref[...] = d_middle
+            dmix_ref[...] = mm(d_branch, tile(0), NT).astype(bf16)
             tiles[2].start()
-        slopes = []
-        for j in range(blocks):
-            copy = pltpu.make_async_copy(slope_out.at[j], slope_ref.at[j % 2], slope_sems.at[j % 2])
-            slopes.append(copy)
-        slopes[0].start()
-        slopes[1].start()
-        limit = jnp.where(is_large, plan.large_len, 3 * plan.small_len)
-        live = iota((rows, 1), 0) < limit
-        cot_copy.wait()
-        grad = jnp.where(live, first_cot[...].astype(f32), 0.0)
-        dfeed_ref[...] = (vec(vec_ref, FEED_SCALE) * grad).astype(bf16)
-        small_ref[...] = jnp.zeros_like(small_ref)
-        note(REDUCE_BIAS, rows_sum(dfeed_ref[...].astype(f32)))
-        gather_step(14)
-        for j in range(blocks):
-            d_feed = dfeed_ref[...]
-            value = mm(act_ref[j], d_feed, TN).astype(bf16)
-            gwr_ref[j] = value.reshape(2, 4 * eighth, width)
-            if j == 1:
-                gather_step(15)
-        for m in range(blocks):
-            push(gwr_ref.at[:, :, pl.ds(eighth * m, eighth)], sum_wr, eighth * m, slice(0, width))
-        gather_step(16)
+            mixed = jnp.concatenate([mixed_ref[p] for p in range(pairs)], axis=1)
+            push("rows", mm(mixed, d_branch, TN), sum_wo, 0, 0)
+            normed_ref = dfeed_ref
+            normed_copy = fetch(normed_out, normed_ref, late_sems.at[0])
+            queue.beat()
+
+            def ds_copy(p):
+                slot = p % 3
+                dst = ds_out.at[pl.ds(2 * p, 2)]
+                return pltpu.make_async_copy(probs_ref.at[slot], dst, ds_sems.at[slot])
+
+            def pair_back(p):
+                slot = p % 3
+                for copy in pair_loads(p):
+                    copy.wait()
+
+                @pl.when(p >= 2)
+                def _():
+                    ds_copy(p - 2).wait()
+
+                @pl.when(p + 1 < pairs)
+                def _():
+                    for copy in pair_loads(p + 1):
+                        copy.start()
+
+                lanes = pl.ds(pl.multiple_of(128 * p, 128), 128)
+                q, k, v = [qkv_ref[p % 2, part] for part in range(3)]
+                do = dmix_ref[:, lanes]
+                lower = half_mask(rows)
+                prod = do.astype(f32) * mixed_ref[p].astype(f32)
+                dq, dk, dv = [], [], []
+                for t in range(2):
+                    keep = lower if t == 0 else ~lower
+                    d_out = jnp.where(keep, do, jnp.zeros_like(do))
+                    delta = jnp.sum(jnp.where(keep, prod, 0.0), axis=1, keepdims=True)
+                    d_probs = mm(d_out, v, NT)
+                    probs = probs_ref[slot, t]
+                    dv.append(mm(probs, do, TN))
+                    d_scores = (probs.astype(f32) * (d_probs - delta)).astype(bf16)
+                    probs_ref[slot, t] = d_scores
+                    dq.append(mm(d_scores, k))
+                    dk.append(mm(d_scores, q, TN))
+                dtri_ref[0, :, lanes] = (jnp.where(lower, dq[0], dq[1]) * 0.125).astype(bf16)
+                dtri_ref[1, :, lanes] = jnp.where(lower, dk[0], dk[1]).astype(bf16)
+                dtri_ref[2, :, lanes] = jnp.where(lower, dv[0], dv[1]).astype(bf16)
+                ds_copy(p).start()
+
+            span = width // 3
+            for group in range(3):
+
+                @pl.loop(2 * group, 2 * group + 2)
+                def _(p):
+                    pair_back(p)
+
+                    @pl.when(p == 2 * group)
+                    def _():
+                        queue.beat()
+
+                queue.beat()
+                if group == 0:
+                    normed_copy.wait()
+                d_part = [dtri_ref[j, :, group * span : (group + 1) * span] for j in range(3)]
+                d_part = jnp.concatenate(d_part, axis=1)
+                push("rows", mm(normed_ref[...], d_part, TN), sum_wt, 0, group * width)
+                queue.beat()
+
+            out_copy.wait()
+            tok_ref = half_ref
+            tok_copy = fetch(tok_in, tok_ref, late_sems.at[1])
+            for j in range(3):
+                d_part = dtri_ref[j]
+                part = mm(d_part, tile(1 + j), NT)
+                feed_ref[...] = part if j == 0 else feed_ref[...] + part
+                if j == 0:
+                    tiles[3].start()
+                if j != 1:
+                    note(QUERY_BIAS if j == 0 else VALUE_BIAS, rows_sum(d_part.astype(f32)))
+                queue.beat()
+            tok_copy.wait()
+            normal, inv = norm_stats(tok_ref[...].astype(f32))
+            note(FIRST_GAIN, rows_sum(feed_ref[...] * normal))
+            note(FIRST_SHIFT, rows_sum(feed_ref[...]))
+            queue.beat()
+
+            ds_copy(pairs - 2).wait()
+            ds_copy(pairs - 1).wait()
+
+            def ds_load(p):
+                src, slot = ds_out.at[pl.ds(2 * p, 2)], p % 3
+                return pltpu.make_async_copy(src, probs_ref.at[slot], pair_sems.at[slot, 3])
+
+            ds_load(0).start()
+
+            @pl.loop(0, pairs)
+            def _(p):
+                ds_load(p).wait()
+
+                @pl.when(p + 1 < pairs)
+                def _():
+                    ds_load(p + 1).start()
+
+                for t in range(2):
+                    ds = probs_ref.at[p % 3, t]
+                    args = (image_ref, colsel_ref, large_ref, strip_ref, tail_ref, 2 * p + t, is_large)
+                    fold_head(plan, ds, *args)
+                for i in range(pairs):
+
+                    @pl.when(p == i)
+                    def _():
+                        queue.beat()
+
+            lines_ref[...] = fold_lines(plan, large_ref, strip_ref, tail_ref, is_large)
+
+        def first_norm_back():
+            tok_ref, normed_ref = half_ref, dfeed_ref
+            normal, inv = norm_stats(tok_ref[...].astype(f32))
+            back = norm_back(feed_ref[...], vec(vec_ref, FIRST_GAIN), normal, inv)
+            normed_ref[...] = (dsec_ref[...] + back).astype(bf16)
+            return fetch(normed_ref, tok_out, save_sems.at[1])
+
+        pl.run_scoped(
+            attention,
+            pltpu.VMEM((2, 4, 2, eighth, width), bf16),
+            pltpu.VMEM((2, 3, rows, 128), bf16),
+            pltpu.VMEM((3, 2, rows, rows), bf16),
+            pltpu.VMEM((rows, width), bf16),
+            pltpu.VMEM((heads, plan.gl, plan.strip_l), f32),
+            pltpu.VMEM((heads, 16, plan.strip_s), f32),
+            pltpu.VMEM((heads, 1, 128), f32),
+        )
         queue.beat()
-        gather_step(17)
-        if fast:
-            tiles[0].start()
-            tiles[2].start()
-        for j in range(blocks):
-            second, d_feed = half_ref[...], dfeed_ref[...]
-            wr = tile(2 * j)
-            feed = mm(act_ref[j], wr)
-            d_act = mm(d_feed, wr, NT)
-            more(2 * j)
-            slopes[j].wait()
-            d_pre = (d_act * slope_ref[j % 2].astype(f32)).astype(bf16)
-            if j + 2 < blocks:
-                slopes[j + 2].start()
-            queue.beat()
-            we = tile(2 * j + 1)
-            d_second = mm(d_pre, we, NT)
-            more(2 * j + 1)
-            if j == 0:
-                branch_copy = fetch(branch_out, branch_ref, late_sems.at[1])
-                feed_ref[...] = feed
-                dsec_ref[...] = d_second
-            else:
-                feed_ref[...] += feed
-                dsec_ref[...] += d_second
-            if j == 1:
-                cot_copy = fetch(cot_in, cot_ref, late_sems.at[0])
-            note(BE_ROW + j, rows_sum(d_pre.astype(f32)))
-            push(stage(mm(second, d_pre, TN)), sum_we, 0, slice(j * width, (j + 1) * width))
-            queue.beat()
-
-        def pair_loads(p):
-            slot = p % 3
-            probs = probs_out.at[pl.ds(2 * p, 2)]
-            copies = [pltpu.make_async_copy(probs, probs_ref.at[slot], pair_sems.at[slot, 3])]
-            for part in range(3):
-                src, dst = qkv_out.at[part * pairs + p], qkv_ref.at[slot, part]
-                copies.append(pltpu.make_async_copy(src, dst, pair_sems.at[slot, part]))
-            return copies
-
-        for copy in pair_loads(0):
-            copy.start()
-
-        branch_copy.wait()
-        cot_copy.wait()
-        feed_out = feed_ref[...] + vec(vec_ref, REDUCE_BIAS)
-        middle = middle_ref[...]
-        half_ref[...] = (middle + vec(vec_ref, FEED_SCALE) * feed_out).astype(bf16)
-        out_copy = fetch(half_ref, out_ref, slope_sems.at[0])
-        grad = jnp.where(live, cot_ref[...].astype(f32), 0.0)
-        d_second = dsec_ref[...]
-        normal, inv = norm_stats(middle)
-        d_middle = grad + norm_back(d_second, vec(vec_ref, SECOND_GAIN), normal, inv)
-        d_branch = (vec(vec_ref, ATTEND_SCALE) * d_middle).astype(bf16)
-        note(FEED_SCALE, rows_sum(grad * feed_out))
-        note(SECOND_GAIN, rows_sum(d_second * normal))
-        note(SECOND_SHIFT, rows_sum(d_second))
-        note(ATTEND_SCALE, rows_sum(d_middle * branch_ref[...].astype(f32)))
-        note(OUTPUT_BIAS, rows_sum(d_branch.astype(f32)))
-        dsec_ref[...] = d_middle
-        dmix_ref[...] = mm(d_branch, tile(2 * blocks), NT).astype(bf16)
-        more(2 * blocks)
-        mixed = jnp.concatenate([mixed_ref[p] for p in range(pairs)], axis=1)
-        push(stage(mm(mixed, d_branch, TN)), sum_wo, 0, slice(0, width))
-        late = [fetch(normed_out, late_ref, late_sems.at[0]), fetch(tok_in, tok_ref, late_sems.at[1])]
-        queue.beat()
-
-        def ds_copy(p):
-            slot = p % 3
-            dst = ds_out.at[pl.ds(2 * p, 2)]
-            return pltpu.make_async_copy(probs_ref.at[slot], dst, ds_sems.at[slot])
-
-        def pair_back(p):
-            slot = p % 3
-            for copy in pair_loads(p):
-                copy.wait()
-
-            @pl.when(p >= 2)
-            def _():
-                ds_copy(p - 2).wait()
-
-            @pl.when(p + 1 < pairs)
-            def _():
-                for copy in pair_loads(p + 1):
-                    copy.start()
-
-            lanes = pl.ds(pl.multiple_of(128 * p, 128), 128)
-            q, k, v = qkv_ref[slot, 0], qkv_ref[slot, 1], qkv_ref[slot, 2]
-            do = dmix_ref[:, lanes]
-            lower = half_mask(rows)
-            prod = do.astype(f32) * mixed_ref[p].astype(f32)
-            dq, dk, dv = [], [], []
-            for t in range(2):
-                keep = lower if t == 0 else ~lower
-                d_out = jnp.where(keep, do, jnp.zeros_like(do))
-                delta = jnp.sum(jnp.where(keep, prod, 0.0), axis=1, keepdims=True)
-                d_probs = mm(d_out, v, NT)
-                probs = probs_ref[slot, t]
-                dv.append(mm(probs, do, TN))
-                d_scores = (probs.astype(f32) * (d_probs - delta)).astype(bf16)
-                probs_ref[slot, t] = d_scores
-                dq.append(mm(d_scores, k))
-                dk.append(mm(d_scores, q, TN))
-            dtri[0][:, lanes] = (jnp.where(lower, dq[0], dq[1]) * 0.125).astype(bf16)
-            dtri[1][:, lanes] = jnp.where(lower, dk[0], dk[1]).astype(bf16)
-            dtri[2][:, lanes] = jnp.where(lower, dv[0], dv[1]).astype(bf16)
-            ds_copy(p).start()
-
-        span = width // 3
-        for group in range(3):
-
-            @pl.loop(2 * group, 2 * group + 2)
-            def _(p):
-                pair_back(p)
-
-                @pl.when(p == 2 * group)
-                def _():
-                    queue.beat()
-
-            if group == 0:
-                for copy in late:
-                    copy.wait()
-            d_part = [dtri[j][:, group * span : (group + 1) * span] for j in range(3)]
-            d_part = jnp.concatenate(d_part, axis=1)
-            cut = slice(0, width)
-            value = stage(mm(late_ref[...], d_part, TN))
-            push(value, sum_wt.at[group] if fast else (sum_wt.at[group],), 0, cut)
-            queue.beat()
-
-        d_normed = None
-        for j in range(3):
-            d_part = dtri[j][...]
-            part = mm(d_part, tile(2 * blocks + 1 + j), NT)
-            d_normed = part if d_normed is None else d_normed + part
-            if j != 1:
-                note(QUERY_BIAS if j == 0 else VALUE_BIAS, rows_sum(d_part.astype(f32)))
-            if j == 1:
-                queue.beat()
-        normal, inv = norm_stats(tok_ref[...].astype(f32))
-        back = norm_back(d_normed, vec(vec_ref, FIRST_GAIN), normal, inv)
-        late_ref[...] = (dsec_ref[...] + back).astype(bf16)
-        tok_copy = fetch(late_ref, tok_out, slope_sems.at[1])
-        note(FIRST_GAIN, rows_sum(d_normed * normal))
-        note(FIRST_SHIFT, rows_sum(d_normed))
-        queue.beat()
-
-        ds_copy(pairs - 2).wait()
-        ds_copy(pairs - 1).wait()
-
-        def ds_load(p):
-            src, slot = ds_out.at[pl.ds(2 * p, 2)], p % 3
-            return pltpu.make_async_copy(src, probs_ref.at[slot], pair_sems.at[slot, 3])
-
-        ds_load(0).start()
-
-        @pl.loop(0, pairs)
-        def _(p):
-            ds_load(p).wait()
-
-            @pl.when(p + 1 < pairs)
-            def _():
-                ds_load(p + 1).start()
-
-            for t in range(2):
-                ds = probs_ref.at[p % 3, t]
-                args = (image_ref, colsel_ref, large_ref, strip_ref, tail_ref, 2 * p + t, is_large)
-                fold_head(plan, ds, *args)
-
-            for i in range(pairs):
-
-                @pl.when(p == i)
-                def _():
-                    queue.beat()
-
-        out_copy.wait()
-        tok_copy.wait()
-        lines = fold_lines(plan, large_ref, strip_ref, tail_ref, is_large)
-        line_of = lambda chunk: lines[:, 128 * chunk : 128 * (chunk + 1)]
-        buckets = plan.buckets
-        d_table = table_from_lines(plan, line_of, lab_ref, buckets)
+        line_of = lambda chunk: lines_ref[:, 128 * chunk : 128 * (chunk + 1)]
+        d_table = table_from_lines(plan, line_of, lab_ref, plan.buckets)
+        wide = hidden // 8
+
+        def bias_sum(f):
+            parts = [dbe_ref[j : j + 1, f * unit : (f + 1) * unit] for j in range(HIDDEN_BLOCKS)]
+            return jnp.concatenate(parts, axis=1)
+
         if not fast:
-            vec_out[...] = small_ref[:, 0:width]
-            for j in range(blocks):
-                be_out[:, j * width : (j + 1) * width] = small_ref[BE_ROW + j : BE_ROW + j + 1, 0:width]
+            vec_out[...] = small_ref[...]
+            for f in range(8):
+                be_out[:, f * wide : (f + 1) * wide] = bias_sum(f)
             tab_out[...] = d_table
+            first_norm_back().wait()
             return
 
-        share, bshare = width // n, buckets // n
-        wide = blocks * width // n
-        per = width // wide
+        share, bshare = width // n, plan.buckets // n
         for f in range(n):
             value = jnp.concatenate(
                 [
@@ -1317,15 +1436,15 @@
                 ],
                 axis=1,
             )
-            where, row = f % per * wide, BE_ROW + f // per
-            bias = jnp.broadcast_to(small_ref[row : row + 1, where : where + wide], (16, wide))
+            bias = jnp.broadcast_to(bias_sum(f), (16, wide))
             block[f] = jnp.where(iota((16, wide), 0) == heads, bias, value)
         sums = []
         for k, peer in enumerate(peers):
             dst = (spot.f + k + 1) % n
             sums.append(send(block.at[dst], got.at[k], bss.at[k], brs.at[k], peer))
             sums[k].start()
-        queue.beat(1)
+        tok_copy = first_norm_back()
+        queue.beat()
         value = block[spot.f]
         for k, copy in enumerate(sums):
             copy.wait_recv()
@@ -1335,31 +1454,38 @@
             mine = reps.at[spot.rep]
             sums.append(send(mine, mine, bss.at[n - 1 + k], brs.at[n - 1 + k], other))
             sums[-1].start()
-        queue.beat(1)
+        queue.beat()
         for copy in sums[n - 1 :]:
             copy.wait_recv()
         small_out[...] = (reps[0] + reps[1]) + (reps[2] + reps[3])
         queue.drain()
+        tok_copy.wait()
         for copy in sums:
             copy.wait_send()
         for job in jobs:
-            job.finish()
-        for piece in pieces:
-            piece.finish()
+            job.free()
+        flat = normed_out
+        for kind, shape in enumerate(sum_kinds):
+            count = sum_shapes.count(shape)
+            for idx, out_rows in enumerate(Sum.sent_rows(n // 2, shape[0])):
+                total = count * out_rows * shape[1] // width
+                view = flat.at[pl.ds(0, total)]
+                pltpu.make_async_copy(view, view, rss.at[kind, idx + 1]).wait()
+        for at, whole in enumerate(wholes):
+            for copy in Piece.sent_waits(n // 2, whole, gss.at[at]):
+                copy.wait()
 
     pl.run_scoped(
         backward,
-        pltpu.VMEM((3, 4, 2, eighth, width), bf16),
         pltpu.VMEM((rows, width), f32),
         pltpu.VMEM((rows, width), f32),
-        pltpu.VMEM((4, 2, blocks * eighth, width), bf16),
-        pltpu.VMEM((2, 4, 2, eighth, width), bf16),
-        pltpu.VMEM((3, 3, rows, 128), bf16),
-        pltpu.VMEM((3, 2, rows, rows), bf16),
-        pltpu.VMEM((heads, plan.gl, plan.strip_l), f32),
-        pltpu.VMEM((heads, 16, plan.strip_s), f32),
-        pltpu.VMEM((heads, 1, 128), f32),
+        pltpu.VMEM((3, rows, width), bf16),
+        pltpu.VMEM((16, plan.lanes), f32),
     )
+
+
+AHEAD, LAGS = 3, (2, 4, 5)
+GATHER_ORDER = (0, 1, 2, 3)
 
 
 def layer(plan, kind, tokens, cot, large_index, n, fast, shorts, shards):
@@ -1368,18 +1494,20 @@
     pairs = heads // 2
     sds = jax.ShapeDtypeStruct
     hidden = shards[2].shape[1]
-    blocks = hidden // width
+    unit = hidden // 8 // HIDDEN_BLOCKS
+    eighth = width // 8
     cuts = piece_cuts([w.shape for w in shards]) if fast else []
+    sum_shapes = [(unit, width // 2)] * 2 + [(eighth, 4 * unit)] * 2
+    sum_shapes = sum_shapes * HIDDEN_BLOCKS + [(eighth, width // 2)] * 8
     colsel = jnp.asarray(plan.selector_arrays()[1], bf16)
     inputs = [kind, tokens, cot, large_index, pick_plan(plan), colsel, image_selectors(plan)]
     in_specs = [smem_spec] + [any_spec] * 3 + [vmem_spec] * 3
     outs, out_specs = [sds((rows, width), bf16)] * 2, [any_spec] * 2
-    group = (3, width // 8, width)
     if fast:
         wide = hidden // n
         inputs += shorts + shards
         in_specs += [vmem_spec] * 12 + [any_spec] * 4
-        outs += [sds(group, bf16)] + [sds(w.shape, bf16) for w in shards[1:]]
+        outs += [sds(w.shape, bf16) for w in shards]
         outs += [sds((16, wide), f32)]
         out_specs += [vmem_spec] * 5
         outs += [sds((4, 2) + w.shape, bf16) for w in shards]
@@ -1389,58 +1517,57 @@
         wholes = [w.reshape(4, 2, w.shape[0] // 8, w.shape[1]) for w in wholes]
         inputs += [vecs, be, table.astype(f32)] + wholes
         in_specs += [vmem_spec] * 3 + [any_spec] * 4
-        outs += [sds((3, 4, 2, width // 8, width), bf16)] + [sds(w.shape, bf16) for w in wholes[1:]]
+        outs += [sds(w.shape, bf16) for w in wholes]
         outs += [sds((16, width), f32), sds((1, hidden), f32), sds((16, plan.buckets), f32)]
         out_specs += [any_spec] * 4 + [vmem_spec] * 3
     kept = len(outs)
     square = sds((heads, rows, rows), bf16)
     flat = sds((rows, width), bf16)
-    outs += [flat, flat, sds((3 * pairs, rows, 128), bf16), square]
-    outs += [sds((blocks, rows, width), bf16), square]
-    out_specs += [any_spec] * 6
+    outs += [flat, flat, sds((3 * pairs, rows, 128), bf16), square, square]
+    out_specs += [any_spec] * 5
     dma = pltpu.SemaphoreType.DMA
     scratch = [
         pltpu.VMEM((16, width), f32),
         pltpu.VMEM((1, hidden), f32),
         pltpu.VMEM((2, plan.lanes), jnp.int32),
-        pltpu.VMEM((blocks, rows, width), bf16),
-        pltpu.VMEM((2, rows, width), bf16),
         pltpu.VMEM((rows, width), f32),
         pltpu.VMEM((2, rows, width), bf16),
         pltpu.VMEM((pairs, rows, 128), bf16),
         pltpu.VMEM((16, width), f32),
-        dma((7 + blocks,)),
+        pltpu.VMEM((8, 8 * unit), f32),
+        pltpu.VMEM((2, 4, 2, unit, width), bf16),
+        pltpu.VMEM((2, 4, 2, eighth, 8 * unit), bf16),
         dma((8,)),
-        dma((3,)),
+        dma((4,)),
+        dma((2, 9)),
         dma((2,)),
-        dma((3,)),
         dma((3, 4)),
         dma((3,)),
         dma((1,)),
     ]
     kernel_params = dict(vmem_limit_bytes=vmem_bytes)
     if fast:
-        sums = 2 * blocks + 4
-        for _ in range(sums):
-            scratch += Sum.buffers(n // 2, width)
+        for shape in sum_shapes:
+            scratch += Sum.buffers(n // 2, *shape)
         scratch += [
             pltpu.VMEM((16, wide), bf16),
             pltpu.VMEM((n, 16, wide), bf16),
             pltpu.VMEM((n, 16, wide), f32),
             pltpu.VMEM((n - 1, 16, wide), f32),
             pltpu.VMEM((4, 16, wide), f32),
-            dma((len(cuts) * Piece.sems,)),
+            dma((4, 4)),
             dma((len(cuts) * Piece.sems,)),
             dma((n - 1,)),
             dma((n - 1,)),
-            dma((sums * Sum.sems,)),
-            dma((sums * Sum.sems,)),
+            dma((len(set(sum_shapes)), 6)),
+            dma((len(sum_shapes),)),
+            dma((len(sum_shapes) * Sum.sems,)),
             dma((n + 2,)),
             dma((n + 2,)),
         ]
         kernel_params.update(collective_id=1, has_side_effects=True)
     result = pl.pallas_call(
-        functools.partial(layer_kernel, plan, n, fast, cuts, blocks),
+        functools.partial(layer_kernel, plan, n, fast, cuts, sum_shapes),
         in_specs=in_specs,
         out_specs=out_specs,
         out_shape=outs,
@@ -1448,14 +1575,17 @@
         compiler_params=pltpu.CompilerParams(**kernel_params),
         name="layer",
     )(*inputs)[:kept]
-    out, token_grad, wt = result[:3]
+    out, token_grad = result[:2]
     if fast:
         return out, token_grad, result[2:6], result[6]
-    wt = wt.reshape(3, width, 3, width // 3).transpose(1, 2, 0, 3).reshape(width, 3 * width)
-    grads = [wt] + [g.reshape(-1, g.shape[3]) for g in result[3:6]]
-    sums, block = reduce_plain(grads, *result[6:9], n)
-    wt = sums[0].reshape(-1, 3, 3, width // 3).transpose(2, 0, 1, 3).reshape(3, -1, width)
-    return out, token_grad, [wt] + sums[1:], block
+    wt, wo, we, wr = [g.reshape(-1, g.shape[3]) for g in result[2:6]]
+    wt = wt.reshape(width, 3, 3, width // 3).transpose(0, 2, 1, 3).reshape(width, 3 * width)
+    we = we.reshape(width, HIDDEN_BLOCKS, 8, unit).transpose(0, 2, 1, 3).reshape(width, hidden)
+    sums, block = reduce_plain([wt, wo, we, wr], *result[6:9], n)
+    wt, wo, we, wr = sums
+    wt = wt.reshape(-1, 3, 3, width // 3).transpose(0, 2, 1, 3).reshape(wt.shape)
+    we = we.reshape(-1, 8, HIDDEN_BLOCKS, unit).transpose(0, 2, 1, 3).reshape(we.shape)
+    return out, token_grad, [wt, wo, we, wr], block
 
 
 def per_device(
@@ -1533,15 +1663,22 @@
     ) = outs
     out[0] = out_in[...]
     tok[0] = tok_in[...]
-    groups, _, width = wt_in.shape
-    span = width // groups
-    for g in range(groups):
+    width = wt_in.shape[1] // 3
+    span = width // 3
+    for g in range(3):
         for part in range(3):
-            value = wt_in[g, :, part * span : (part + 1) * span].astype(f32)
+            first = g * width + part * span
+            value = wt_in[:, first : first + span].astype(f32)
             triple_weight[0, :, part * width + g * span : part * width + (g + 1) * span] = value
     output_weight[0] = wo_in[...].astype(f32)
-    expand_weight[0] = we_in[...].astype(f32)
     reduce_weight[0] = wr_in[...].astype(f32)
+    unit = 128
+    count = we_in.shape[1] // (unit * HIDDEN_BLOCKS)
+    for g in range(HIDDEN_BLOCKS):
+        for f in range(count):
+            value = we_in[:, (g * count + f) * unit : (g * count + f + 1) * unit].astype(f32)
+            first = (f * HIDDEN_BLOCKS + g) * unit
+            expand_weight[0, :, first : first + unit] = value
     first = block_ref.shape[1] - share
     rows = {
         FIRST_GAIN: first_gain,
@@ -1568,7 +1705,7 @@
     vector = sds((1, share), f32)
     whole_of = lambda w: sds((1,) + w.shape, f32)
     bshare, heads = table_shape
-    triple = sds((1, wt.shape[1], 3 * wt.shape[2]), f32)
+    triple = whole_of(wt)
     outs = [sds((1,) + block_output.shape, bf16)] * 2
     outs += [vector, vector, triple, vector, vector, sds((heads, 1, bshare), f32)]
     outs += [whole_of(wo)] + [vector] * 4 + [whole_of(we), sds((1, block.shape[1]), f32)]

time: 202 us -> 180 us (0.89)
  Pallas kernels: 198 us -> 176 us
    pallas_call x1, Pallas kernels: 193 us -> 171 us  [layer(): pl.pallas_call(functools.partial(layer_kernel, plan, n, fast, cuts, sum_s...]
where the time goes in v5:
time: 180 us; the launch traced here: 177 us
  Pallas kernels  176 us (98%)
    pallas_call x1, Pallas kernels, layer(): pl.pallas_call(functools.partial(layer_kernel, plan, n, fast, cuts, sum_s...  171 us
    pallas_call x1, Pallas kernels, wrap(): pl.pallas_call(functools.partial(wrap_kernel, share, heads), in_specs=[vm...  4.47 us

profile of v5, /device:TPU:0, one launch (start us, length us, event | category | flops | bytes accessed | tf_op | source)
XLA Modules:
  0.0 177.3 jit_solution(13605407802507801094)
XLA Ops:
  1.3 171.3 %layer.1 = (bf16[592,768]{1,0:T(8,128)(2,1)}, bf16[592,768]{1,0:T(8,128)(2,1)}, bf16[96,2304]{1,0:T(8,128)(2,1)}, bf16[96,768]{1,0:T(8,128)(2,1)}, bf16[96,3072]...) custom-call(s32[1]{0:T(128)S(6)} %copy.41.refs_0_, ...), custom_call_target="tpu_custom_call" | custom-call | tf_op jit(solution)/shard_map/layer/pallas_call | solution.py:1569
  172.6 4.5 %wrap.1 = (bf16[1,592,768]{2,1,0:T(8,128)(2,1)}, bf16[1,592,768]{2,1,0:T(8,128)(2,1)}, f32[1,96]{1,0:T(1,128)}, f32[1,96]{1,0:T(1,128)}, f32[1,96,2304]{2,1,0:T(...) custom-call(bf16[592,768]{1,0:T(8,128)(2,1)} %get-tuple-element.43.o, ...), custom_call_target="tpu_custom_call" | custom-call | tf_op jit(solution)/shard_map/wrap/pallas_call | solution.py:1713

commit v6 on v5

--- a/solution.py
+++ b/solution.py
@@ -687,6 +687,8 @@
         self.mine = rows(half * (q + m), q)
         self.own = rows(core * part, part)
         self.sent = self.joined = False
+        unit = 4 * self.acc.shape[3] / LINK_BYTES_PER_US
+        self.link_us = (2 * levels * q * unit, levels * (q + m) * unit, (q + m) * unit)
 
         def copy(idx, src, dst, device):
             out_sem = sent.at[idx] if idx else c_sem
@@ -801,43 +803,60 @@
         return [2 * levels * cls.outer, levels * kept, kept, part, (levels - 1) * kept]
 
 
-ADMIT, HOLD = 1, 3
+LATENCY_US, LINK_BYTES_PER_US = 2.2, 82e3
 HIDDEN_BLOCKS = 3
+BLOCK_ORDER = [("rows", 0), ("rows", 1), ("cols", 0), ("rows", 2), ("cols", 1), ("cols", 2)]
 
 
 class Queue:
     def __init__(self):
-        self.waiting, self.active, self.beats, self.last = [], [], 0, -9
+        self.clock, self.entries = 0.0, []
+        self.free = {"x": 0.0, "y": 0.0, "z": 0.0, "core": 0.0}
+
+    def book(self, link, us):
+        begin = max(self.clock, self.free[link])
+        self.free[link] = begin + us
+        return begin + us + LATENCY_US
 
     def add(self, job):
-        self.waiting.append([job, 0])
         job.start()
-
-    def beat(self, hold=None):
-        hold = HOLD if hold is None else hold
-        self.beats += 1
-        for entry in self.waiting:
-            if entry[1] >= hold - 1:
-                entry[0].join()
-            entry[1] += 1
-        for entry in list(self.active):
-            entry[1] += 1
-            if entry[1] >= hold:
-                entry[1] = 0
-                entry[2] += 1
-                entry[0].stage(entry[2])
-                if entry[2] == 5:
-                    self.active.remove(entry)
-        admit = ADMIT if hold > 1 else 1
-        if self.waiting and self.waiting[0][0].joined and self.beats - self.last >= admit:
-            self.last = self.beats
-            job, _ = self.waiting.pop(0)
-            self.active.append([job, 0, 0])
+        self.entries.append([self.book("core", 1.0), 0, job])
+
+    def take(self, entry):
+        _, stage, job = entry
+        if stage == 0:
+            job.join()
+        else:
+            job.stage(stage)
+        x, y, f = job.link_us
+        if stage == 0:
             job.stage(0)
+            entry[0] = self.book("x", x)
+        elif stage == 1:
+            entry[0] = self.book("y", y)
+        elif stage == 2:
+            entry[0] = self.book("z", y)
+        elif stage == 3:
+            entry[0] = self.book("x", f)
+        elif stage == 4:
+            entry[0] = self.book("core", 0.3)
+        entry[1] += 1
+        if stage == 5:
+            self.entries.remove(entry)
+
+    def beat(self, us):
+        self.clock += us
+        while self.entries:
+            entry = min(self.entries, key=lambda item: item[0])
+            if entry[0] > self.clock:
+                break
+            self.take(entry)
 
     def drain(self):
-        while self.waiting or self.active:
-            self.beat(1)
+        while self.entries:
+            entry = min(self.entries, key=lambda item: item[0])
+            self.clock = max(self.clock, entry[0])
+            self.take(entry)
 
 
 def layer_kernel(plan, n, fast, cuts, sum_shapes, *refs):
@@ -901,9 +920,11 @@
             args = (row, col, cols, gss.at[at], grs, base)
             pieces.append(Piece(spot, shards[at], wholes[at], *args))
         formed = []
-        for j in range(HIDDEN_BLOCKS):
-            formed.append((rows_ref, sum_wr, j * unit, 0))
-            formed.append((cols_ref, sum_we, 0, j * tile_cols))
+        for ring, j in BLOCK_ORDER:
+            if ring == "rows":
+                formed.append((rows_ref, sum_wr, j * unit, 0))
+            else:
+                formed.append((cols_ref, sum_we, 0, j * tile_cols))
         formed.append((rows_ref, sum_wo, 0, 0))
         for j in range(3):
             formed.append((rows_ref, sum_wt, 0, j * width))
@@ -1181,49 +1202,46 @@
                 act_ref[j % 2, low:high, :] = value.astype(bf16)
                 slope_ref[j % 2, low:high, :] = slope.astype(bf16)
 
-            before(0)
-            for i in range(len(spans)):
-                activate(0, i)
-                step()
-            for j in range(HIDDEN_BLOCKS):
-                ahead = j + 1 < HIDDEN_BLOCKS
+            def first_part(j):
+                before(j)
+                for i in range(len(spans)):
+                    activate(j, i)
+                    step()
+                queue.beat(4.0)
+                push("rows", mm(act_ref[j % 2], dfeed_ref[...], TN), sum_wr, j * unit, 0)
+
+            def second_part(j):
                 gather_until(16 + 2 * (((j + 1) * unit - 1) // 96) + 1)
                 wr_load(j).start()
-                if ahead:
-                    before(j + 1)
-                d_feed = dfeed_ref[...]
-                act = act_ref[j % 2]
-                push("rows", mm(act, d_feed, TN), sum_wr, j * unit, 0)
-                if ahead:
-                    activate(j + 1, 0)
-                queue.beat()
-                step()
+                queue.beat(1.5)
                 wr_load(j).wait()
+                d_feed, act = dfeed_ref[...], act_ref[j % 2]
                 wr = wr_ref[j % 2].reshape(tile_cols, width)
-                feed = mm(act, wr)
-                feed_ref[...] = feed if j == 0 else feed_ref[...] + feed
-                if ahead:
-                    activate(j + 1, 1)
-                queue.beat()
-                step()
                 d_act = mm(d_feed, wr, NT)
                 d_pre = (d_act * slope_ref[j % 2].astype(f32)).astype(bf16)
                 dbe_ref[j : j + 1, :] = rows_sum(d_pre.astype(f32))
-                if ahead:
-                    activate(j + 1, 2)
-                queue.beat()
                 step()
+                queue.beat(1.5)
                 push("cols", mm(half_ref[...], d_pre, TN), sum_we, 0, j * tile_cols)
-                if ahead:
-                    activate(j + 1, 3)
-                queue.beat()
                 step()
+                queue.beat(1.5)
+                feed = mm(act, wr)
+                feed_ref[...] = feed if j == 0 else feed_ref[...] + feed
+                step()
+                queue.beat(1.5)
                 d_second = mm(d_pre, we_tile(j), NT)
                 dsec_ref[...] = d_second if j == 0 else dsec_ref[...] + d_second
                 if j + 2 < HIDDEN_BLOCKS:
                     for copy in we_loads(j + 2):
                         copy.start()
-                queue.beat()
+                step()
+                queue.beat(1.5)
+
+            first_part(0)
+            for j in range(HIDDEN_BLOCKS):
+                if j + 1 < HIDDEN_BLOCKS:
+                    first_part(j + 1)
+                second_part(j)
 
         pl.run_scoped(
             feed_forward,
@@ -1270,7 +1288,7 @@
             normal, inv = norm_stats(middle)
             d_middle = grad + norm_back(d_second, vec(vec_ref, SECOND_GAIN), normal, inv)
             d_branch = (vec(vec_ref, ATTEND_SCALE) * d_middle).astype(bf16)
-            queue.beat()
+            queue.beat(3.5)
             note(FEED_SCALE, rows_sum(grad * feed_out))
             note(SECOND_GAIN, rows_sum(d_second * normal))
             note(SECOND_SHIFT, rows_sum(d_second))
@@ -1283,7 +1301,7 @@
             push("rows", mm(mixed, d_branch, TN), sum_wo, 0, 0)
             normed_ref = dfeed_ref
             normed_copy = fetch(normed_out, normed_ref, late_sems.at[0])
-            queue.beat()
+            queue.beat(4.0)
 
             def ds_copy(p):
                 slot = p % 3
@@ -1335,15 +1353,15 @@
 
                     @pl.when(p == 2 * group)
                     def _():
-                        queue.beat()
-
-                queue.beat()
+                        queue.beat(2.3)
+
+                queue.beat(2.3)
                 if group == 0:
                     normed_copy.wait()
                 d_part = [dtri_ref[j, :, group * span : (group + 1) * span] for j in range(3)]
                 d_part = jnp.concatenate(d_part, axis=1)
                 push("rows", mm(normed_ref[...], d_part, TN), sum_wt, 0, group * width)
-                queue.beat()
+                queue.beat(1.6)
 
             out_copy.wait()
             tok_ref = half_ref
@@ -1356,12 +1374,12 @@
                     tiles[3].start()
                 if j != 1:
                     note(QUERY_BIAS if j == 0 else VALUE_BIAS, rows_sum(d_part.astype(f32)))
-                queue.beat()
+                queue.beat(1.3)
             tok_copy.wait()
             normal, inv = norm_stats(tok_ref[...].astype(f32))
             note(FIRST_GAIN, rows_sum(feed_ref[...] * normal))
             note(FIRST_SHIFT, rows_sum(feed_ref[...]))
-            queue.beat()
+            queue.beat(1.0)
 
             ds_copy(pairs - 2).wait()
             ds_copy(pairs - 1).wait()
@@ -1388,7 +1406,7 @@
 
                     @pl.when(p == i)
                     def _():
-                        queue.beat()
+                        queue.beat(1.9)
 
             lines_ref[...] = fold_lines(plan, large_ref, strip_ref, tail_ref, is_large)
 
@@ -1409,7 +1427,7 @@
             pltpu.VMEM((heads, 16, plan.strip_s), f32),
             pltpu.VMEM((heads, 1, 128), f32),
         )
-        queue.beat()
+        queue.beat(1.9)
         line_of = lambda chunk: lines_ref[:, 128 * chunk : 128 * (chunk + 1)]
         d_table = table_from_lines(plan, line_of, lab_ref, plan.buckets)
         wide = hidden // 8
@@ -1437,24 +1455,24 @@
                 axis=1,
             )
             bias = jnp.broadcast_to(bias_sum(f), (16, wide))
-            block[f] = jnp.where(iota((16, wide), 0) == heads, bias, value)
+            block[f] = jnp.where(iota((16, wide), 0) == heads, bias, value).astype(bf16)
         sums = []
         for k, peer in enumerate(peers):
             dst = (spot.f + k + 1) % n
             sums.append(send(block.at[dst], got.at[k], bss.at[k], brs.at[k], peer))
             sums[k].start()
         tok_copy = first_norm_back()
-        queue.beat()
-        value = block[spot.f]
+        queue.beat(4.0)
+        value = block[spot.f].astype(f32)
         for k, copy in enumerate(sums):
             copy.wait_recv()
-            value = value + got[k]
+            value = value + got[k].astype(f32)
         reps[spot.rep] = value
         for k, other in enumerate(others):
             mine = reps.at[spot.rep]
             sums.append(send(mine, mine, bss.at[n - 1 + k], brs.at[n - 1 + k], other))
             sums[-1].start()
-        queue.beat()
+        queue.beat(3.0)
         for copy in sums[n - 1 :]:
             copy.wait_recv()
         small_out[...] = (reps[0] + reps[1]) + (reps[2] + reps[3])
@@ -1497,8 +1515,10 @@
     unit = hidden // 8 // HIDDEN_BLOCKS
     eighth = width // 8
     cuts = piece_cuts([w.shape for w in shards]) if fast else []
-    sum_shapes = [(unit, width // 2)] * 2 + [(eighth, 4 * unit)] * 2
-    sum_shapes = sum_shapes * HIDDEN_BLOCKS + [(eighth, width // 2)] * 8
+    sum_shapes = []
+    for ring, _ in BLOCK_ORDER:
+        sum_shapes += [(unit, width // 2) if ring == "rows" else (eighth, 4 * unit)] * 2
+    sum_shapes += [(eighth, width // 2)] * 8
     colsel = jnp.asarray(plan.selector_arrays()[1], bf16)
     inputs = [kind, tokens, cot, large_index, pick_plan(plan), colsel, image_selectors(plan)]
     in_specs = [smem_spec] + [any_spec] * 3 + [vmem_spec] * 3
@@ -1552,8 +1572,8 @@
         scratch += [
             pltpu.VMEM((16, wide), bf16),
             pltpu.VMEM((n, 16, wide), bf16),
-            pltpu.VMEM((n, 16, wide), f32),
-            pltpu.VMEM((n - 1, 16, wide), f32),
+            pltpu.VMEM((n, 16, wide), bf16),
+            pltpu.VMEM((n - 1, 16, wide), bf16),
             pltpu.VMEM((4, 16, wide), f32),
             dma((4, 4)),
             dma((len(cuts) * Piece.sems,)),

time: 180 us -> 179 us (level)
  Pallas kernels: 176 us -> 174 us
where the time goes in v6:
time: 179 us; the launch traced here: 176 us
  Pallas kernels  174 us (97%)
    pallas_call x1, Pallas kernels, layer(): pl.pallas_call(functools.partial(layer_kernel, plan, n, fast, cuts, sum_s...  170 us
    pallas_call x1, Pallas kernels, wrap(): pl.pallas_call(functools.partial(wrap_kernel, share, heads), in_specs=[vm...  4.47 us

profile of v6, /device:TPU:0, one launch (start us, length us, event | category | flops | bytes accessed | tf_op | source)
XLA Modules:
  0.0 175.8 jit_solution(1648281579830156998)
XLA Ops:
  1.3 169.9 %layer.1 = (bf16[592,768]{1,0:T(8,128)(2,1)}, bf16[592,768]{1,0:T(8,128)(2,1)}, bf16[96,2304]{1,0:T(8,128)(2,1)}, bf16[96,768]{1,0:T(8,128)(2,1)}, bf16[96,3072]...) custom-call(s32[1]{0:T(128)S(6)} %copy.41.refs_0_, ...), custom_call_target="tpu_custom_call" | custom-call | tf_op jit(solution)/shard_map/layer/pallas_call | solution.py:1589
  171.2 4.5 %wrap.1 = (bf16[1,592,768]{2,1,0:T(8,128)(2,1)}, bf16[1,592,768]{2,1,0:T(8,128)(2,1)}, f32[1,96]{1,0:T(1,128)}, f32[1,96]{1,0:T(1,128)}, f32[1,96,2304]{2,1,0:T(...) custom-call(bf16[592,768]{1,0:T(8,128)(2,1)} %get-tuple-element.43.o, ...), custom_call_target="tpu_custom_call" | custom-call | tf_op jit(solution)/shard_map/wrap/pallas_call | solution.py:1733

commit v7 on v6

--- a/solution.py
+++ b/solution.py
@@ -803,7 +803,7 @@
         return [2 * levels * cls.outer, levels * kept, kept, part, (levels - 1) * kept]
 
 
-LATENCY_US, LINK_BYTES_PER_US = 2.2, 82e3
+LATENCY_US, LINK_BYTES_PER_US = 1.6, 85e3
 HIDDEN_BLOCKS = 3
 BLOCK_ORDER = [("rows", 0), ("rows", 1), ("cols", 0), ("rows", 2), ("cols", 1), ("cols", 2)]
 
@@ -1463,6 +1463,11 @@
             sums[k].start()
         tok_copy = first_norm_back()
         queue.beat(4.0)
+        for job in jobs:
+            job.free()
+        for at, whole in enumerate(wholes):
+            for copy in Piece.sent_waits(n // 2, whole, gss.at[at]):
+                copy.wait()
         value = block[spot.f].astype(f32)
         for k, copy in enumerate(sums):
             copy.wait_recv()
@@ -1480,8 +1485,6 @@
         tok_copy.wait()
         for copy in sums:
             copy.wait_send()
-        for job in jobs:
-            job.free()
         flat = normed_out
         for kind, shape in enumerate(sum_kinds):
             count = sum_shapes.count(shape)
@@ -1489,9 +1492,6 @@
                 total = count * out_rows * shape[1] // width
                 view = flat.at[pl.ds(0, total)]
                 pltpu.make_async_copy(view, view, rss.at[kind, idx + 1]).wait()
-        for at, whole in enumerate(wholes):
-            for copy in Piece.sent_waits(n // 2, whole, gss.at[at]):
-                copy.wait()
 
     pl.run_scoped(
         backward,

time: 179 us -> 177 us (0.989)
  no operation moved by 1% of the time
where the time goes in v7:
time: 177 us; the launch traced here: 174 us
  Pallas kernels  173 us (98%)
    pallas_call x1, Pallas kernels, layer(): pl.pallas_call(functools.partial(layer_kernel, plan, n, fast, cuts, sum_s...  168 us
    pallas_call x1, Pallas kernels, wrap(): pl.pallas_call(functools.partial(wrap_kernel, share, heads), in_specs=[vm...  4.47 us

profile of v7, /device:TPU:0, one launch (start us, length us, event | category | flops | bytes accessed | tf_op | source)
XLA Modules:
  0.0 174.2 jit_solution(10492634866153820189)
XLA Ops:
  1.3 168.2 %layer.1 = (bf16[592,768]{1,0:T(8,128)(2,1)}, bf16[592,768]{1,0:T(8,128)(2,1)}, bf16[96,2304]{1,0:T(8,128)(2,1)}, bf16[96,768]{1,0:T(8,128)(2,1)}, bf16[96,3072]...) custom-call(s32[1]{0:T(128)S(6)} %copy.41.refs_0_, ...), custom_call_target="tpu_custom_call" | custom-call | tf_op jit(solution)/shard_map/layer/pallas_call | solution.py:1589
  169.6 4.5 %wrap.1 = (bf16[1,592,768]{2,1,0:T(8,128)(2,1)}, bf16[1,592,768]{2,1,0:T(8,128)(2,1)}, f32[1,96]{1,0:T(1,128)}, f32[1,96]{1,0:T(1,128)}, f32[1,96,2304]{2,1,0:T(...) custom-call(bf16[592,768]{1,0:T(8,128)(2,1)} %get-tuple-element.43.o, ...), custom_call_target="tpu_custom_call" | custom-call | tf_op jit(solution)/shard_map/wrap/pallas_call | solution.py:1733
